TPU v7x, 32 devices: a whole 2x2x4 slice. The times are simulated.
32 devices in a mesh: pts: 16 (over z, x, core), rep: 2 (over y).
Axes of the slice: x: 2, y: 2, z: 4, core: 2. Of those that a mesh axis runs over, the one named last changes fastest.
Arguments:
- points: bfloat16 [65536, 512], P(('rep', 'pts')), parts along dimension 0, may hold values from -6 to 6
- point_row_index: int32 [65536], P(('rep', 'pts')), parts along dimension 0, may hold values from 0 to 32767, as said below
- neighbour_ball_list: int32 [256, 4], P(('rep', 'pts')), parts along dimension 0, may hold values from 0 to 127, as said below
- attention_norm_gain: float32 [512], replicated, may hold values from 0.1 to 1.9
- query_weight: bfloat16 [512, 512], replicated, may hold values from -0.25 to 0.25
- key_weight: bfloat16 [512, 512], replicated, may hold values from -0.25 to 0.25
- value_weight: bfloat16 [512, 512], replicated, may hold values from -0.25 to 0.25
- pooled_key_weight: bfloat16 [512, 512], replicated, may hold values from -0.75 to 0.75
- pooled_value_weight: bfloat16 [512, 512], replicated, may hold values from -0.75 to 0.75
- head_score_scale: float32 [16], replicated, may hold values from 4 to 16
- output_weight: bfloat16 [512, 512], replicated, may hold values from -0.25 to 0.25
- feedforward_norm_gain: float32 [512], replicated, may hold values from 0.1 to 1.9
- gate_weight: bfloat16 [512, 1024], replicated, may hold values from -0.25 to 0.25
- up_weight: bfloat16 [512, 1024], replicated, may hold values from -0.25 to 0.25
- down_weight: bfloat16 [1024, 512], replicated, may hold values from -0.1875 to 0.1875
Outputs:
- layer_out: bfloat16 [65536, 512], P(('rep', 'pts')), parts along dimension 0
There are 2 independent parts, one for each index of `rep`. A program takes and returns all parts, laid end to end along the dimension named above; an argument that names none is the same for every part. Nothing has to cross between parts.
Inputs may be any that keep to these rules, and one draw needn't show every extreme that they name: point_row_index holds every number of 0 to 32767 once; of the 2048 points of one device (rows d * 2048 to (d + 1) * 2048 - 1 of points) exactly 128 go to the rows of each device. `neighbour_ball_list`: row b starts with b itself; its other three entries are balls on three different devices among those 1 to 4 places away from ball b's device around the loop of devices, ball c lying on device c // 8.
All inputs are finite; a program needn't handle non-finite values.
Results may differ from a plain program's by a relative error of at most 0.012.
Values may be sent and summed in bfloat16 or wider, within the bound.
No kernel may reach another device: no remote copies, remote signals or barrier semaphores. Data moves between devices by JAX's collectives and lax.ppermute only.
A program may use at most 128 MiB of HBM per device.

v0:
```python
import jax
import jax.numpy as jnp
from jax import lax
from jax.sharding import PartitionSpec as P

BALL = 256
POOL = 8
OWNERS = 4
REACH = 4


def from_behind(block, axis, distance):
    devices = range(lax.axis_size(axis))
    route = [((i - distance) % len(devices), i) for i in devices]
    return lax.ppermute(block, axis, route)


def row_norm(values, scale_gain):
    mean_square = jnp.mean(values * values, axis=-1, keepdims=True)
    return values * lax.rsqrt(mean_square + 1e-05) * scale_gain


def column_head_norm(values):
    mean_square = jnp.mean(values * values, axis=1, keepdims=True)
    return values * lax.rsqrt(mean_square + 1e-06)


def project_columns(rows, weight):
    return jnp.einsum("nc,cx->xn", rows, weight, preferred_element_type=jnp.float32)


def fetch_blocks(payload):
    both_sides = []
    for step_sign in (1, -1):
        received = [payload]
        received.append(from_behind(payload, "pts", step_sign))
        for places in range(2, REACH + 1):
            received.append(from_behind(payload, "pts", step_sign * places))
        both_sides.append(received)
    upward = both_sides[0]
    downward = both_sides[1]
    ordered = (
        [upward[k] for k in range(REACH, 0, -1)]
        + [payload]
        + [downward[k] for k in range(1, REACH + 1)]
    )
    return jnp.stack(ordered)


def on_device(
    points,
    point_row_index,
    neighbour_ball_list,
    attention_norm_gain,
    query_weight,
    key_weight,
    value_weight,
    pooled_key_weight,
    pooled_value_weight,
    head_score_scale,
    output_weight,
    feedforward_norm_gain,
    gate_weight,
    up_weight,
    down_weight,
):
    rows_dev, model_width = points.shape
    head_total = head_score_scale.shape[0]
    head_size = model_width // head_total
    peer_count = lax.axis_size("pts")
    my_index = lax.axis_index("pts")
    send_each = rows_dev // peer_count
    blocks_dev = rows_dev // BALL
    comp_rows = BALL // POOL
    sort_order = jnp.argsort(point_row_index)
    outgoing = jnp.take(points, sort_order, axis=0).reshape(peer_count, send_each, model_width)
    outgoing_ids = jnp.take(point_row_index, sort_order, axis=0).reshape(peer_count, send_each)
    arrived, arrived_ids = (
        lax.all_to_all(outgoing, "pts", split_axis=0, concat_axis=0, tiled=True),
        lax.all_to_all(outgoing_ids, "pts", split_axis=0, concat_axis=0, tiled=True),
    )
    local_slots = arrived_ids.reshape(rows_dev) - my_index * rows_dev
    grouped = jnp.take(arrived.reshape(rows_dev, model_width), jnp.argsort(local_slots), axis=0)
    normed = row_norm(grouped.astype(jnp.float32), attention_norm_gain).astype(jnp.bfloat16)
    col_shape = (head_total, head_size, rows_dev)
    query_cols = column_head_norm(project_columns(normed, query_weight).reshape(col_shape)).astype(
        jnp.bfloat16
    )
    key_cols = column_head_norm(project_columns(normed, key_weight).reshape(col_shape)).astype(
        jnp.bfloat16
    )
    value_cols = project_columns(normed, value_weight).astype(jnp.bfloat16).reshape(col_shape)
    pooled = jnp.mean(
        normed.astype(jnp.float32).reshape(rows_dev // POOL, POOL, model_width), axis=1
    ).astype(jnp.bfloat16)
    payload_width = pooled.shape[1]
    candidates = fetch_blocks(pooled).reshape(
        (2 * REACH + 1) * blocks_dev, comp_rows, payload_width
    )
    owner_device = neighbour_ball_list // blocks_dev
    offsets = jnp.mod(owner_device - my_index + REACH, peer_count) - REACH
    chosen_rows = (offsets + REACH) * blocks_dev + neighbour_ball_list % blocks_dev
    chosen = jnp.take(candidates, chosen_rows.reshape(-1), axis=0).reshape(
        blocks_dev, OWNERS * comp_rows, payload_width
    )
    score_scale = (head_score_scale / head_size)[:, None, None]
    output_heads = output_weight.reshape(head_total, head_size, model_width)
    coarse_count = OWNERS * comp_rows

    def one_ball(ball_index):
        start = ball_index * BALL
        ball_query = lax.dynamic_slice_in_dim(query_cols, start, BALL, 2)
        ball_key = lax.dynamic_slice_in_dim(key_cols, start, BALL, 2)
        ball_value = lax.dynamic_slice_in_dim(value_cols, start, BALL, 2)
        coarse = lax.dynamic_index_in_dim(chosen, ball_index, 0, keepdims=False)
        coarse_key = column_head_norm(
            project_columns(coarse, pooled_key_weight).reshape(head_total, head_size, coarse_count)
        ).astype(jnp.bfloat16)
        coarse_value = (
            project_columns(coarse, pooled_value_weight)
            .astype(jnp.bfloat16)
            .reshape(head_total, head_size, coarse_count)
        )
        local_score = (
            jnp.einsum("hdq,hdk->hqk", ball_query, ball_key, preferred_element_type=jnp.float32)
            * score_scale
        )
        far_score = (
            jnp.einsum("hdq,hdk->hqk", ball_query, coarse_key, preferred_element_type=jnp.float32)
            * score_scale
        )
        local_exp = jnp.exp(local_score)
        far_exp = jnp.exp(far_score)
        denominator = jnp.sum(local_exp, axis=-1, keepdims=True) + jnp.sum(
            far_exp, axis=-1, keepdims=True
        )
        local_prob = (local_exp / denominator).astype(jnp.bfloat16)
        far_prob = (far_exp / denominator).astype(jnp.bfloat16)
        attended = jnp.einsum(
            "hqk,hdk->hdq", local_prob, ball_value, preferred_element_type=jnp.float32
        )
        attended = attended + jnp.einsum(
            "hqk,hdk->hdq", far_prob, coarse_value, preferred_element_type=jnp.float32
        )
        attended = attended.astype(jnp.bfloat16)
        return jnp.einsum("hdq,hde->qe", attended, output_heads, preferred_element_type=jnp.float32)

    projected_rows = lax.map(one_ball, jnp.arange(blocks_dev, dtype=jnp.int32)).reshape(
        rows_dev, model_width
    )
    residual = (grouped.astype(jnp.float32) + projected_rows).astype(jnp.bfloat16)
    ffn_normed = row_norm(residual.astype(jnp.float32), feedforward_norm_gain).astype(jnp.bfloat16)
    gate_proj = jnp.dot(ffn_normed, gate_weight, preferred_element_type=jnp.float32)
    up_proj = jnp.dot(ffn_normed, up_weight, preferred_element_type=jnp.float32)
    hidden = (jax.nn.silu(gate_proj) * up_proj).astype(jnp.bfloat16)
    ball_out = (
        residual.astype(jnp.float32)
        + jnp.dot(hidden, down_weight, preferred_element_type=jnp.float32)
    ).astype(jnp.bfloat16)
    returning = jnp.take(ball_out, local_slots, axis=0).reshape(peer_count, send_each, model_width)
    came_back = lax.all_to_all(returning, "pts", split_axis=0, concat_axis=0, tiled=True).reshape(
        rows_dev, model_width
    )
    return jnp.take(came_back, jnp.argsort(sort_order), axis=0)


def solution(mesh):
    return jax.shard_map(
        on_device,
        mesh=mesh,
        in_specs=(
            P(("rep", "pts"), None),
            P(("rep", "pts")),
            P(("rep", "pts"), None),
            P(),
            P(),
            P(),
            P(),
            P(),
            P(),
            P(),
            P(),
            P(),
            P(),
            P(),
            P(),
        ),
        out_specs=P(("rep", "pts"), None),
        check_vma=False,
    )
```

profile of v0, /device:TPU:1, one launch (start us, length us, event | category | flops | bytes accessed | tf_op | source)
XLA Modules:
  0.0 358.1 jit_solution(14439424945560573369)
XLA Ops:
  0.0 5.9 %sort.45 = (s32[2048]{0:T(1024)}, s32[2048]{0:T(1024)S(1)}) sort(s32[2048]{0:T(1024)} %param.20, s32[2048]{0:T(1024)S(1)} %iota.13), dimensions={0}, to_apply=%region_0.0 | sort | flops 22528 | bytes 32768 | tf_op jit(solution)/shard_map/jit(argsort)/sort | solution.py:75
  5.9 11.8 %gather_fusion = s32[2048]{0:T(1024)S(1)} fusion(s32[2048]{0:T(1024)S(1)} %copy-done.2, s32[2048]{0:T(1024)S(1)} %fusion.36), kind=kCustom, calls=%fused_computation.4 | custom fusion | bytes 24576 | tf_op jit(solution)/shard_map/jit(_take)/gather | solution.py:77
  18.3 7.3 %all-to-all-start.1 = ((s32[16,1,128]{2,1,0:T(1,128)}), s32[16,1,128]{2,1,0:T(1,128)S(1)}, u32[]{:S(2)}, u32[]{:S(2)}) async-start(s32[16,1,128]{2,1,0:T(1,128)} %bitcast.9), calls=%async_computation.1 | async-start | bytes 16384 | tf_op jit(solution)/shard_map/all_to_all | solution.py:80
  25.6 9.2 %gather_fusion.2 = bf16[2048,512]{1,0:T(8,128)(2,1)} fusion(bf16[2048,512]{1,0:T(8,128)(2,1)S(1)} %copy-done, s32[2048]{0:T(1024)S(1)} %fusion.36), kind=kCustom, calls=%fused_computation.clone | custom fusion | bytes 4202496 | tf_op jit(solution)/shard_map/jit(_take)/gather | solution.py:76
  34.8 2.7 broadcast_select_fusion.3
  37.6 6.2 %all-to-all-start = ((bf16[16,128,512]{2,1,0:T(8,128)(2,1)}), bf16[16,128,512]{2,1,0:T(8,128)(2,1)S(1)}, u32[]{:S(2)}, u32[]{:S(2)}) async-start(bf16[16,128,512]{2,1,0:T(8,128)(2,1)} %bitcast.113), calls=%async_computation | async-start | bytes 4194304 | tf_op jit(solution)/shard_map/all_to_all | solution.py:79
  44.3 5.0 %sort.46 = (s32[2048]{0:T(1024)}, s32[2048]{0:T(1024)S(1)}) sort(s32[2048]{0:T(1024)S(1)} %bitcast.117, s32[2048]{0:T(1024)S(1)} %iota.14), dimensions={0}, to_apply=%region_1.3 | sort | flops 22528 | bytes 32768 | tf_op jit(solution)/shard_map/jit(argsort)/sort | solution.py:83
  49.4 35.8 %all-to-all-done = bf16[16,128,512]{2,1,0:T(8,128)(2,1)S(1)} async-done(((bf16[16,128,512]{2,1,0:T(8,128)(2,1)}), bf16[16,128,512]{2,1,0:T(8,128)(2,1)S(1)}, u32[]{:S(2)}, u32[]{:S(2)}) %all-to-all-start) | async-done | bytes 2097184 | tf_op jit(solution)/shard_map/all_to_all | solution.py:79
  85.2 9.2 %gather_fusion.3 = bf16[2048,512]{1,0:T(8,128)(2,1)} fusion(bf16[2048,512]{1,0:T(8,128)(2,1)S(1)} %bitcast.111, s32[2048]{0:T(1024)S(1)} %fusion.37), kind=kCustom, calls=%fused_computation.1.clone | custom fusion | bytes 4202496 | tf_op jit(solution)/shard_map/jit(_take)/gather | solution.py:83
  94.4 2.4 fusion.24
  96.8 2.2 convert_reduce_fusion
  99.1 6.0 %collective-permute-start = (bf16[256,512]{1,0:T(8,128)(2,1)S(1)}, bf16[256,512]{1,0:T(8,128)(2,1)S(1)}, u32[]{:S(2)}, u32[]{:S(2)}) collective-permute-start(bf16[256,512]{1,0:T(8,128)(2,1)S(1)} %multiply_convert_fusion.5), channel_id=1, source_target_pairs={{24,0},{26,2},{28,4},{30,6},{0,8},{2,10},{4,12},{6,14},{8,16},{10,... | collective-permute-start | bytes 786440 | tf_op jit(solution)/shard_map/ppermute | solution.py:15
  105.1 3.4 collective-permute-start.1
  109.9 1.8 multiply_reduce_fusion.2
  111.8 1.8 multiply_reduce_fusion.1
  113.6 3.3 multiply_convert_fusion.3
  116.9 3.2 convolution_convert_fusion.1
  120.1 3.4 collective-permute-start.5
  127.2 2.4 collective-permute-done.3
  129.7 4.8 %collective-permute-done.5 = bf16[256,512]{1,0:T(8,128)(2,1)S(1)} collective-permute-done((bf16[256,512]{1,0:T(8,128)(2,1)S(1)}, bf16[256,512]{1,0:T(8,128)(2,1)S(1)}, u32[]{:S(2)}, u32[]{:S(2)}) %collective-permute-start.5) | collective-permute-done | bytes 262176 | tf_op jit(solution)/shard_map/ppermute | solution.py:15
  134.9 4.5 %collective-permute-done.7 = bf16[256,512]{1,0:T(8,128)(2,1)S(1)} collective-permute-done((bf16[256,512]{1,0:T(8,128)(2,1)S(1)}, bf16[256,512]{1,0:T(8,128)(2,1)S(1)}, u32[]{:S(2)}, u32[]{:S(2)}) %collective-permute-start.7) | collective-permute-done | bytes 262176 | tf_op jit(solution)/shard_map/ppermute | solution.py:15
  140.9 2.3 gather_fusion.1
  144.3 118.8 %while.10 = (s32[]{:T(128)}, f32[8,256,512]{2,1,0:T(8,128)}, s32[8]{0:T(128)S(1)}, bf16[16,32,2048]{2,1,0:T(8,128)(2,1)}, bf16[16,32,2048]{2,1,0:T(8,128)(2,1)},...) while((s32[]{:T(128)}, f32[8,256,512]{2,1,0:T(8,128)}, ...), condition=%wide.region_10.12_spmd, body=%wide.region_6.0_spmd.sunk | while | flops 478214144 | bytes 19023872 | solution.py:148
  148.8 1.5 fusion.85
  150.4 2.1 fusion.84
  152.5 2.6 fusion.86
  156.3 2.8 fusion.88
  163.6 1.5 fusion.85
  165.2 2.1 fusion.84
  167.3 2.6 fusion.86
  171.2 2.8 fusion.88
  178.5 1.5 fusion.85
  180.0 2.1 fusion.84
  182.1 2.6 fusion.86
  186.0 2.9 fusion.88
  193.4 1.5 fusion.85
  194.9 2.1 fusion.84
  197.0 2.6 fusion.86
  200.9 2.8 fusion.88
  208.2 1.5 fusion.85
  209.7 2.1 fusion.84
  211.8 2.6 fusion.86
  215.7 2.8 fusion.88
  223.0 1.5 fusion.85
  224.6 2.1 fusion.84
  226.7 2.6 fusion.86
  230.6 2.8 fusion.88
  237.9 1.5 fusion.85
  239.4 2.1 fusion.84
  241.5 2.6 fusion.86
  245.4 2.8 fusion.88
  254.3 2.1 fusion.84
  256.4 2.6 fusion.86
  260.2 2.8 fusion.88
  263.1 3.5 fusion.28
  268.0 5.6 %fusion.34 = f32[2048,1024]{1,0:T(8,128)} fusion(bf16[512,1024]{1,0:T(8,128)(2,1)S(1)} %copy-done.10, bf16[2048,512]{1,0:T(8,128)(2,1)S(1)} %get-tuple-element.93, f32[512]{0:T(512)S(1)} %copy-done.14, f32[2048]{0:T(1024)S(1)} %add_rsqrt_fusion.3), kind=kOutput, calls=%fused_computation.66 | convolution fusion | flops 2151677952 | bytes 11544576 | tf_op jit(solution)/shard_map/dot_general | solution.py:153
  273.6 9.5 %fusion.31 = bf16[2048,512]{1,0:T(8,128)(2,1)S(1)} fusion(bf16[2048,512]{1,0:T(8,128)(2,1)} %copy-done.6, bf16[1024,512]{1,0:T(8,128)(2,1)} %param.33, f32[2048,1024]{1,0:T(8,128)} %fusion.34, bf16[512,1024]{1,0:T(8,128)(2,1)} %param.32, f32[512]{0:T(512)S(1)} %copy-done.14, f32[2048]{0:T(1024)S(1)} %add_rsqrt_fusion.3), kind=kOutput, calls=%fused_computation.54 | convolution fusion | flops 4314890240 | bytes 14690304 | tf_op jit(solution)/shard_map/dot_general | solution.py:158
  283.1 9.2 %gather_fusion.4 = bf16[2048,512]{1,0:T(8,128)(2,1)} fusion(bf16[2048,512]{1,0:T(8,128)(2,1)S(1)} %fusion.31, s32[2048]{0:T(1024)S(1)} %fusion.38), kind=kCustom, calls=%fused_computation.2.clone | custom fusion | bytes 4202496 | tf_op jit(solution)/shard_map/jit(_take)/gather | solution.py:160
  292.3 2.7 broadcast_select_fusion.1
  295.1 7.4 %all-to-all-start.2 = ((bf16[16,128,512]{2,1,0:T(8,128)(2,1)}), bf16[16,128,512]{2,1,0:T(8,128)(2,1)}, u32[]{:S(2)}, u32[]{:S(2)}) async-start(bf16[16,128,512]{2,1,0:T(8,128)(2,1)} %bitcast.37), calls=%async_computation.2 | async-start | bytes 4194304 | tf_op jit(solution)/shard_map/all_to_all | solution.py:161
  302.5 5.0 %sort.47 = (s32[2048]{0:T(1024)}, s32[2048]{0:T(1024)S(1)}) sort(s32[2048]{0:T(1024)S(1)} %get-tuple-element.66, s32[2048]{0:T(1024)S(1)} %iota.16), dimensions={0}, to_apply=%region_12.14 | sort | flops 22528 | bytes 32768 | tf_op jit(solution)/shard_map/jit(argsort)/sort | solution.py:164
  307.6 36.5 %all-to-all-done.2 = bf16[16,128,512]{2,1,0:T(8,128)(2,1)} async-done(((bf16[16,128,512]{2,1,0:T(8,128)(2,1)}), bf16[16,128,512]{2,1,0:T(8,128)(2,1)}, u32[]{:S(2)}, u32[]{:S(2)}) %all-to-all-start.2) | async-done | bytes 2097184 | tf_op jit(solution)/shard_map/all_to_all | solution.py:161
  344.1 11.3 %gather_fusion.5 = bf16[2048,512]{1,0:T(8,128)(2,1)} fusion(bf16[2048,512]{1,0:T(8,128)(2,1)} %bitcast.38, s32[2048]{0:T(1024)S(1)} %fusion.39), kind=kCustom, calls=%fused_computation.3.clone | custom fusion | bytes 4202496 | tf_op jit(solution)/shard_map/jit(_take)/gather | solution.py:164
  355.4 2.7 broadcast_select_fusion
  (146 shorter events, 37.6 us)
Async XLA Ops:
  0.0 25.6 %copy-start = (bf16[2048,512]{1,0:T(8,128)(2,1)S(1)}, bf16[2048,512]{1,0:T(8,128)(2,1)}, u32[]{:S(2)}) copy-start(bf16[2048,512]{1,0:T(8,128)(2,1)} %param.19) | copy-start | bytes 6291460
  0.0 5.9 %copy-start.2 = (s32[2048]{0:T(1024)S(1)}, s32[2048]{0:T(1024)}, u32[]{:S(2)}) copy-start(s32[2048]{0:T(1024)} %param.20) | copy-start | bytes 24580
  18.3 19.3 %all-to-all-start.1 = ((s32[16,1,128]{2,1,0:T(1,128)}), s32[16,1,128]{2,1,0:T(1,128)S(1)}, u32[]{:S(2)}, u32[]{:S(2)}) async-start(s32[16,1,128]{2,1,0:T(1,128)} %bitcast.9), calls=%async_computation.1 | async-start | bytes 16384 | tf_op jit(solution)/shard_map/all_to_all | solution.py:80
  37.6 6.2 %copy-start.9 = (s32[8,4]{0,1:T(4,128)S(1)}, s32[8,4]{0,1:T(4,128)}, u32[]{:S(2)}) copy-start(s32[8,4]{0,1:T(4,128)} %param.21) | copy-start | bytes 388
  37.6 6.7 %copy-start.15 = (f32[16]{0:T(128)S(1)}, f32[16]{0:T(128)}, u32[]{:S(2)}) copy-start(f32[16]{0:T(128)} %param.28) | copy-start | bytes 196
  37.6 47.6 %all-to-all-start = ((bf16[16,128,512]{2,1,0:T(8,128)(2,1)}), bf16[16,128,512]{2,1,0:T(8,128)(2,1)S(1)}, u32[]{:S(2)}, u32[]{:S(2)}) async-start(bf16[16,128,512]{2,1,0:T(8,128)(2,1)} %bitcast.113), calls=%async_computation | async-start | bytes 4194304 | tf_op jit(solution)/shard_map/all_to_all | solution.py:79
  85.2 11.6 %copy-start.8 = (f32[512]{0:T(512)S(1)}, f32[512]{0:T(512)}, u32[]{:S(2)}) copy-start(f32[512]{0:T(512)} %param.22) | copy-start | bytes 6148
  94.4 2.4 copy-start.3
  94.4 15.5 %copy-start.11 = (bf16[512,512]{1,0:T(8,128)(2,1)S(1)}, bf16[512,512]{1,0:T(8,128)(2,1)}, u32[]{:S(2)}) copy-start(bf16[512,512]{1,0:T(8,128)(2,1)} %param.23) | copy-start | bytes 1572868
  99.1 12.7 %copy-start.12 = (bf16[512,512]{1,0:T(8,128)(2,1)S(1)}, bf16[512,512]{1,0:T(8,128)(2,1)}, u32[]{:S(2)}) copy-start(bf16[512,512]{1,0:T(8,128)(2,1)} %param.24) | copy-start | bytes 1572868
  99.1 21.0 %collective-permute-start = (bf16[256,512]{1,0:T(8,128)(2,1)S(1)}, bf16[256,512]{1,0:T(8,128)(2,1)S(1)}, u32[]{:S(2)}, u32[]{:S(2)}) collective-permute-start(bf16[256,512]{1,0:T(8,128)(2,1)S(1)} %multiply_convert_fusion.5), channel_id=1, source_target_pairs={{24,0},{26,2},{28,4},{30,6},{0,8},{2,10},{4,12},{6,14},{8,16},{10,... | collective-permute-start | bytes 786440 | tf_op jit(solution)/shard_map/ppermute | solution.py:15
  105.1 18.5 %collective-permute-start.1 = (bf16[256,512]{1,0:T(8,128)(2,1)S(1)}, bf16[256,512]{1,0:T(8,128)(2,1)S(1)}, u32[]{:S(2)}, u32[]{:S(2)}) collective-permute-start(bf16[256,512]{1,0:T(8,128)(2,1)S(1)} %multiply_convert_fusion.5), channel_id=1, source_target_pairs={{26,0},{28,2},{30,4},{0,6},{2,8},{4,10},{6,12},{8,14},{10,16},{12,... | collective-permute-start | bytes 786440 | tf_op jit(solution)/shard_map/ppermute | solution.py:15
  108.4 17.6 %collective-permute-start.2 = (bf16[256,512]{1,0:T(8,128)(2,1)S(1)}, bf16[256,512]{1,0:T(8,128)(2,1)S(1)}, u32[]{:S(2)}, u32[]{:S(2)}) collective-permute-start(bf16[256,512]{1,0:T(8,128)(2,1)S(1)} %multiply_convert_fusion.5), channel_id=1, source_target_pairs={{28,0},{30,2},{0,4},{2,6},{4,8},{6,10},{8,12},{10,14},{12,16},{14,... | collective-permute-start | bytes 786440 | tf_op jit(solution)/shard_map/ppermute | solution.py:15
  108.4 21.2 %collective-permute-start.3 = (bf16[256,512]{1,0:T(8,128)(2,1)S(1)}, bf16[256,512]{1,0:T(8,128)(2,1)S(1)}, u32[]{:S(2)}, u32[]{:S(2)}) collective-permute-start(bf16[256,512]{1,0:T(8,128)(2,1)S(1)} %multiply_convert_fusion.5), channel_id=1, source_target_pairs={{30,0},{0,2},{2,4},{4,6},{6,8},{8,10},{10,12},{12,14},{14,16},{16,... | collective-permute-start | bytes 786440 | tf_op jit(solution)/shard_map/ppermute | solution.py:15
  109.9 19.8 %collective-permute-start.4 = (bf16[256,512]{1,0:T(8,128)(2,1)S(1)}, bf16[256,512]{1,0:T(8,128)(2,1)S(1)}, u32[]{:S(2)}, u32[]{:S(2)}) collective-permute-start(bf16[256,512]{1,0:T(8,128)(2,1)S(1)} %multiply_convert_fusion.5), channel_id=1, source_target_pairs={{2,0},{4,2},{6,4},{8,6},{10,8},{12,10},{14,12},{16,14},{18,16},{20... | collective-permute-start | bytes 786440 | tf_op jit(solution)/shard_map/ppermute | solution.py:15
  113.6 3.3 copy-start.13
  120.1 14.4 %collective-permute-start.5 = (bf16[256,512]{1,0:T(8,128)(2,1)S(1)}, bf16[256,512]{1,0:T(8,128)(2,1)S(1)}, u32[]{:S(2)}, u32[]{:S(2)}) collective-permute-start(bf16[256,512]{1,0:T(8,128)(2,1)S(1)} %multiply_convert_fusion.5), channel_id=1, source_target_pairs={{4,0},{6,2},{8,4},{10,6},{12,8},{14,10},{16,12},{18,14},{20,16},{2... | collective-permute-start | bytes 786440 | tf_op jit(solution)/shard_map/ppermute | solution.py:15
  123.6 11.3 %collective-permute-start.6 = (bf16[256,512]{1,0:T(8,128)(2,1)S(1)}, bf16[256,512]{1,0:T(8,128)(2,1)S(1)}, u32[]{:S(2)}, u32[]{:S(2)}) collective-permute-start(bf16[256,512]{1,0:T(8,128)(2,1)S(1)} %multiply_convert_fusion.5), channel_id=1, source_target_pairs={{6,0},{8,2},{10,4},{12,6},{14,8},{16,10},{18,12},{20,14},{22,16},{... | collective-permute-start | bytes 786440 | tf_op jit(solution)/shard_map/ppermute | solution.py:15
  126.0 13.4 %collective-permute-start.7 = (bf16[256,512]{1,0:T(8,128)(2,1)S(1)}, bf16[256,512]{1,0:T(8,128)(2,1)S(1)}, u32[]{:S(2)}, u32[]{:S(2)}) collective-permute-start(bf16[256,512]{1,0:T(8,128)(2,1)S(1)} %multiply_convert_fusion.5), channel_id=1, source_target_pairs={{8,0},{10,2},{12,4},{14,6},{16,8},{18,10},{20,12},{22,14},{24,16},... | collective-permute-start | bytes 786440 | tf_op jit(solution)/shard_map/ppermute | solution.py:15
  134.9 9.4 %copy-start.4 = (bf16[512,512]{1,0:T(8,128)(2,1)S(1)}, bf16[512,512]{1,0:T(8,128)(2,1)}, u32[]{:S(2)}) copy-start(bf16[512,512]{1,0:T(8,128)(2,1)} %param.26) | copy-start | bytes 1572868
  134.9 9.4 %copy-start.5 = (bf16[512,512]{1,0:T(8,128)(2,1)S(1)}, bf16[512,512]{1,0:T(8,128)(2,1)}, u32[]{:S(2)}) copy-start(bf16[512,512]{1,0:T(8,128)(2,1)} %param.27) | copy-start | bytes 1572868
  139.4 1.4 copy-start.7
  263.1 4.9 %copy-start.10 = (bf16[512,1024]{1,0:T(8,128)(2,1)S(1)}, bf16[512,1024]{1,0:T(8,128)(2,1)}, u32[]{:S(2)}) copy-start(bf16[512,1024]{1,0:T(8,128)(2,1)} %param.31) | copy-start | bytes 3145732
  263.1 4.9 %copy-start.14 = (f32[512]{0:T(512)S(1)}, f32[512]{0:T(512)}, u32[]{:S(2)}) copy-start(f32[512]{0:T(512)} %param.30) | copy-start | bytes 6148
  266.6 1.3 copy-start.6
  295.1 49.0 %all-to-all-start.2 = ((bf16[16,128,512]{2,1,0:T(8,128)(2,1)}), bf16[16,128,512]{2,1,0:T(8,128)(2,1)}, u32[]{:S(2)}, u32[]{:S(2)}) async-start(bf16[16,128,512]{2,1,0:T(8,128)(2,1)} %bitcast.37), calls=%async_computation.2 | async-start | bytes 4194304 | tf_op jit(solution)/shard_map/all_to_all | solution.py:161
  344.1 14.0 %copy-start.1 = (bf16[2048,512]{1,0:T(8,128)(2,1)S(1)}, bf16[2048,512]{1,0:T(8,128)(2,1)}, u32[]{:S(2)}) copy-start(bf16[2048,512]{1,0:T(8,128)(2,1)} %param.19) | copy-start | bytes 6291460
where the time goes:
time: 365 us; the launch traced here: 358 us
  matrix products  113 us (31%)
  waiting for transfers between devices  85.9 us (24%)
  local copies, waits for them, and re-layouts  63.1 us (17%)
  other arithmetic  38 us (10%)
  starting transfers between devices  37.2 us (10%)
  loops' own time  20.9 us (6%)
    all_to_all x1, waiting for transfers between devices, on_device(): lax.all_to_all(returning, 'pts', split_axis=0, concat_axis=0, tiled=True)  36.5 us
    all_to_all x1, waiting for transfers between devices, on_device(): lax.all_to_all(outgoing, 'pts', split_axis=0, concat_axis=0, tiled=True)  35.8 us
    dot_general x19, matrix products, project_columns(): jnp.einsum('nc,cx->xn', rows, weight, preferred_element_type=jnp.float32)  24.9 us
    dot_general x8, matrix products, one_ball(): jnp.einsum('hdq,hde->qe', attended, output_heads, preferred_element_type=...  22.7 us
    dot_general x8, matrix products, one_ball(): jnp.einsum('hqk,hdk->hdq', local_prob, ball_value, preferred_element_type...  21.1 us
    another operation x1, loops' own time, on_device(): lax.map(one_ball, jnp.arange(blocks_dev, dtype=jnp.int32))  20.9 us
    dot_general x8, matrix products, one_ball(): jnp.einsum('hdq,hdk->hqk', ball_query, ball_key, preferred_element_type=j...  16.6 us
    ppermute x8, starting transfers between devices, from_behind(): return lax.ppermute(block, axis, route)  16.3 us
  transfers between devices with their start and end apart: 11, of which 7 were waited for; matrix products, arithmetic and copies ran while one was open for 9% of the time, Pallas kernels for 0%

commit v1 on v0

v1 whole, which is shorter than its diff:
```python
import functools
import math

import jax
import jax.numpy as jnp
from jax import lax
from jax.experimental import pallas as pl
from jax.experimental.pallas import tpu as pltpu
from jax.sharding import PartitionSpec as P

BALL = 256
POOL = 8
OWNERS = 4
REACH = 4
LANES = 128
TILE = 256
LOW = 64
LOG2E = math.log2(math.e)
F32 = jnp.float32
BF16 = jnp.bfloat16
VMEM_BYTES = 56 * 1024 * 1024


def params(**kwargs):
    return pltpu.CompilerParams(vmem_limit_bytes=VMEM_BYTES, **kwargs)


def dot(a, b):
    return jnp.dot(a, b, preferred_element_type=F32)


def dot_nt(a, b):
    return lax.dot_general(a, b, (((1,), (1,)), ((), ())), preferred_element_type=F32)


def whole(shape):
    return pl.BlockSpec(shape, lambda *_: (0,) * len(shape))


def column_of(row):
    return jnp.broadcast_to(row, (LANES, LANES)).T


def one_hot_by_lane_ids(ids_ref, first, rows):
    targets = (lax.broadcasted_iota(jnp.int32, (rows, LANES), 0) + first).astype(F32)
    tiles = [
        jnp.where(ids_ref[t : t + 1, :] == targets, 1.0, 0.0).astype(BF16)
        for t in range(ids_ref.shape[0])
    ]
    return jnp.concatenate(tiles, axis=1)


def send_kernel(rows_dev, index_ref, points_ref, out_ref, ids_ref, rank_ref, col, aux):
    tiles = rows_dev // LANES
    step = pl.program_id(0)

    @pl.when(step == 0)
    def _():
        for t in range(tiles):
            col[t * LANES : (t + 1) * LANES, :] = column_of(index_ref[t : t + 1, :].astype(F32))

        def rank_tile(t, carry):
            row = index_ref[pl.ds(t, 1), :].astype(F32)
            below = jnp.where(col[...] < row, 1.0, 0.0)
            rank_ref[pl.ds(t, 1), :] = jnp.sum(below, axis=0, keepdims=True)
            return carry

        lax.fori_loop(0, tiles, rank_tile, 0)
        local = lax.rem(col[...].astype(jnp.int32), rows_dev)
        lane = lax.broadcasted_iota(jnp.int32, (rows_dev, LANES), 1)
        high = lax.div(local, LOW)
        low = lax.rem(local, LOW)
        aux[...] = jnp.where(lane == 0, high, jnp.where(lane == 1, low, 0)).astype(F32).astype(BF16)

    pick = one_hot_by_lane_ids(rank_ref, step * TILE, TILE)
    out_ref[...] = dot(pick, points_ref[...]).astype(BF16)
    ids = dot(pick, aux[...])
    for u in range(TILE // LANES):
        part = ids[u * LANES : (u + 1) * LANES, :].T
        ids_ref[pl.ds(step * (TILE // LANES) + u, 1), :] = (
            part[0:1, :] * LOW + part[1:2, :]
        ).astype(jnp.int32)


def send_order(points, index_tiles):
    rows_dev, width = points.shape
    tiles = rows_dev // LANES
    return pl.pallas_call(
        functools.partial(send_kernel, rows_dev),
        grid=(rows_dev // TILE,),
        in_specs=[whole((tiles, LANES)), whole((rows_dev, width))],
        out_specs=[
            pl.BlockSpec((TILE, width), lambda i: (i, 0)),
            whole((tiles, LANES)),
            whole((tiles, LANES)),
        ],
        out_shape=[
            jax.ShapeDtypeStruct((rows_dev, width), BF16),
            jax.ShapeDtypeStruct((tiles, LANES), jnp.int32),
            jax.ShapeDtypeStruct((tiles, LANES), F32),
        ],
        scratch_shapes=[
            pltpu.VMEM((rows_dev, LANES), F32),
            pltpu.VMEM((rows_dev, LANES), BF16),
        ],
        compiler_params=params(),
        cost_estimate=pl.CostEstimate(
            flops=2 * rows_dev * rows_dev * (width + LANES), bytes_accessed=4 * rows_dev * width, transcendentals=0
        ),
        name="send_order",
    )(index_tiles, points)


def group_kernel(ids_ref, arrived_ref, gain_ref, grouped_ref, normed_ref, pooled_ref):
    pick = one_hot_by_lane_ids(ids_ref, pl.program_id(0) * BALL, BALL)
    grouped = dot(pick, arrived_ref[...])
    grouped_ref[...] = grouped.astype(BF16)
    mean_square = jnp.mean(grouped * grouped, axis=-1, keepdims=True)
    normed = (grouped * lax.rsqrt(mean_square + 1e-05) * gain_ref[...]).astype(BF16)
    normed_ref[...] = normed
    comp = BALL // POOL
    member = lax.broadcasted_iota(jnp.int32, (comp, BALL), 1) // POOL
    pool_of = lax.broadcasted_iota(jnp.int32, (comp, BALL), 0)
    mean_of = jnp.where(member == pool_of, 1.0 / POOL, 0.0).astype(BF16)
    pooled_ref[...] = dot(mean_of, normed).astype(BF16)


def group(ids, arrived, gain):
    rows_dev, width = arrived.shape
    tiles = rows_dev // LANES
    comp = BALL // POOL
    return pl.pallas_call(
        group_kernel,
        grid=(rows_dev // BALL,),
        in_specs=[whole((tiles, LANES)), whole((rows_dev, width)), whole((1, width))],
        out_specs=[
            pl.BlockSpec((BALL, width), lambda i: (i, 0)),
            pl.BlockSpec((BALL, width), lambda i: (i, 0)),
            pl.BlockSpec((comp, width), lambda i: (i, 0)),
        ],
        out_shape=[
            jax.ShapeDtypeStruct((rows_dev, width), BF16),
            jax.ShapeDtypeStruct((rows_dev, width), BF16),
            jax.ShapeDtypeStruct((rows_dev // POOL, width), BF16),
        ],
        compiler_params=params(),
        cost_estimate=pl.CostEstimate(
            flops=2 * rows_dev * rows_dev * width, bytes_accessed=6 * rows_dev * width, transcendentals=0
        ),
        name="group_balls",
    )(ids, arrived, gain)


def head_normed(columns, head_size, factors=None):
    heads = columns.shape[0] // head_size
    parts = []
    for h in range(heads):
        part = columns[h * head_size : (h + 1) * head_size, :]
        root = lax.rsqrt(jnp.mean(part * part, axis=0, keepdims=True) + 1e-06)
        if factors is not None:
            root = root * factors[h]
        parts.append((part * root).astype(BF16))
    return parts


def head_sums(query, key_rows, value, h, head_size):
    per_group = LANES // head_size
    group_at, at = h // per_group, h % per_group
    empty = jnp.zeros_like(query)
    spread = jnp.concatenate([query if j == at else empty for j in range(per_group)], axis=0)
    score = dot(key_rows[:, group_at * LANES : (group_at + 1) * LANES], spread)
    weight = jnp.exp2(score).astype(BF16)
    ones = jnp.ones((16, value.shape[1]), BF16)
    both = dot(jnp.concatenate([value, ones], axis=0), weight)
    return both[:head_size, :], both[head_size : head_size + 1, :]


def local_kernel(heads, scale_ref, normed_ref, wq_ref, wk_ref, wv_ref, query_ref, num_ref, den_ref):
    normed = normed_ref[...]
    head_size = wq_ref.shape[0] // heads
    factors = [scale_ref[h] for h in range(heads)]
    queries = head_normed(dot_nt(wq_ref[...], normed), head_size, factors)
    for h in range(heads):
        query_ref[h * head_size : (h + 1) * head_size, :] = queries[h]
    key_rows = jnp.concatenate(head_normed(dot_nt(wk_ref[...], normed), head_size), axis=0).T
    values = dot_nt(wv_ref[...], normed).astype(BF16)
    for h in range(heads):
        rows = slice(h * head_size, (h + 1) * head_size)
        num, den = head_sums(queries[h], key_rows, values[rows, :], h, head_size)
        num_ref[rows, :] = num
        den_ref[h : h + 1, :] = den


def local_attention(normed, wq, wk, wv, scale):
    rows_dev, width = normed.shape
    heads = scale.shape[0]
    square = whole((width, width))
    columns = lambda rows: pl.BlockSpec((rows, BALL), lambda i: (0, i))
    return pl.pallas_call(
        functools.partial(local_kernel, heads),
        grid=(rows_dev // BALL,),
        in_specs=[
            pl.BlockSpec(memory_space=pltpu.SMEM),
            pl.BlockSpec((BALL, width), lambda i: (i, 0)),
            square,
            square,
            square,
        ],
        out_specs=[columns(width), columns(width), columns(heads)],
        out_shape=[
            jax.ShapeDtypeStruct((width, rows_dev), BF16),
            jax.ShapeDtypeStruct((width, rows_dev), F32),
            jax.ShapeDtypeStruct((heads, rows_dev), F32),
        ],
        compiler_params=params(),
        cost_estimate=pl.CostEstimate(
            flops=20 * rows_dev * width * width, bytes_accessed=8 * rows_dev * width, transcendentals=heads * rows_dev * BALL
        ),
        name="local_attention",
    )(scale, normed, wq, wk, wv)


def finish_kernel(
    heads,
    chosen_ref,
    candidates_ref,
    query_ref,
    num_ref,
    den_ref,
    grouped_ref,
    wpk_ref,
    wpv_ref,
    wo_ref,
    gain_ref,
    wg_ref,
    wu_ref,
    wd_ref,
    out_ref,
    attended,
):
    ball = pl.program_id(0)
    width = wpk_ref.shape[0]
    head_size = width // heads
    coarse = jnp.concatenate(
        [candidates_ref[chosen_ref[ball * OWNERS + o]] for o in range(OWNERS)], axis=0
    )
    key_rows = jnp.concatenate(head_normed(dot_nt(wpk_ref[...], coarse), head_size), axis=0).T
    values = dot_nt(wpv_ref[...], coarse).astype(BF16)
    for h in range(heads):
        rows = slice(h * head_size, (h + 1) * head_size)
        num, den = head_sums(query_ref[rows, :], key_rows, values[rows, :], h, head_size)
        num = num + num_ref[rows, :]
        den = den + den_ref[h : h + 1, :]
        attended[rows, :] = (num / den).astype(BF16)
    projected = dot(attended[...].T, wo_ref[...])
    residual = (grouped_ref[...].astype(F32) + projected).astype(BF16)
    rows32 = residual.astype(F32)
    mean_square = jnp.mean(rows32 * rows32, axis=-1, keepdims=True)
    ffn = (rows32 * lax.rsqrt(mean_square + 1e-05) * gain_ref[...]).astype(BF16)
    gate = dot(ffn, wg_ref[...])
    up = dot(ffn, wu_ref[...])
    hidden = (gate / (1.0 + jnp.exp(-gate)) * up).astype(BF16)
    out_ref[...] = (rows32 + dot(hidden, wd_ref[...])).astype(BF16)


def finish(chosen, candidates, query, num, den, grouped, wpk, wpv, wo, gain, wg, wu, wd):
    rows_dev, width = grouped.shape
    heads = den.shape[0]
    hidden = wg.shape[1]
    columns = lambda rows: pl.BlockSpec((rows, BALL), lambda i, *_: (0, i))
    return pl.pallas_call(
        functools.partial(finish_kernel, heads),
        grid_spec=pltpu.PrefetchScalarGridSpec(
            num_scalar_prefetch=1,
            grid=(rows_dev // BALL,),
            in_specs=[
                whole(candidates.shape),
                columns(width),
                columns(width),
                columns(heads),
                pl.BlockSpec((BALL, width), lambda i, *_: (i, 0)),
                whole(wpk.shape),
                whole(wpv.shape),
                whole(wo.shape),
                whole(gain.shape),
                whole(wg.shape),
                whole(wu.shape),
                whole(wd.shape),
            ],
            out_specs=pl.BlockSpec((BALL, width), lambda i, *_: (i, 0)),
            scratch_shapes=[pltpu.VMEM((width, BALL), BF16)],
        ),
        out_shape=jax.ShapeDtypeStruct((rows_dev, width), BF16),
        compiler_params=params(),
        cost_estimate=pl.CostEstimate(
            flops=2 * rows_dev * width * (3 * hidden + 6 * width),
            bytes_accessed=12 * rows_dev * width,
            transcendentals=heads * rows_dev * BALL // 2,
        ),
        name="finish_balls",
    )(chosen, candidates, query, num, den, grouped, wpk, wpv, wo, gain, wg, wu, wd)


def rows_kernel(ids_ref, source_ref, out_ref):
    first = pl.program_id(0) * (TILE // LANES)
    count = source_ref.shape[0]
    lane = lax.broadcasted_iota(jnp.int32, (LANES, LANES), 1).astype(F32)
    for u in range(TILE // LANES):
        wanted = column_of(ids_ref[pl.ds(first + u, 1), :])
        pick = jnp.concatenate(
            [
                jnp.where(wanted - float(c) == lane, 1.0, 0.0).astype(BF16)
                for c in range(0, count, LANES)
            ],
            axis=1,
        )
        out_ref[u * LANES : (u + 1) * LANES, :] = dot(pick, source_ref[...]).astype(BF16)


def take_rows(ids, source):
    rows_dev, width = source.shape
    return pl.pallas_call(
        rows_kernel,
        grid=(rows_dev // TILE,),
        in_specs=[whole(ids.shape), whole(source.shape)],
        out_specs=pl.BlockSpec((TILE, width), lambda i: (i, 0)),
        out_shape=jax.ShapeDtypeStruct((rows_dev, width), BF16),
        compiler_params=params(),
        cost_estimate=pl.CostEstimate(
            flops=2 * rows_dev * rows_dev * width, bytes_accessed=4 * rows_dev * width, transcendentals=0
        ),
        name="take_rows",
    )(ids, source)


def from_behind(block, axis, distance):
    devices = range(lax.axis_size(axis))
    route = [((i - distance) % len(devices), i) for i in devices]
    return lax.ppermute(block, axis, route)


def fetch_blocks(payload):
    return jnp.stack(
        [payload if k == 0 else from_behind(payload, "pts", k) for k in range(REACH, -REACH - 1, -1)]
    )


def on_device(
    points,
    point_row_index,
    neighbour_ball_list,
    attention_norm_gain,
    query_weight,
    key_weight,
    value_weight,
    pooled_key_weight,
    pooled_value_weight,
    head_score_scale,
    output_weight,
    feedforward_norm_gain,
    gate_weight,
    up_weight,
    down_weight,
):
    rows_dev, width = points.shape
    heads = head_score_scale.shape[0]
    peers = lax.axis_size("pts")
    me = lax.axis_index("pts")
    send_each = rows_dev // peers
    blocks_dev = rows_dev // BALL
    comp = BALL // POOL
    tiles = (rows_dev // LANES, LANES)

    def swap(array):
        return lax.all_to_all(array, "pts", split_axis=0, concat_axis=0, tiled=True)

    outgoing, outgoing_ids, rank = send_order(points, point_row_index.reshape(tiles))
    ids = swap(outgoing_ids.reshape(peers, send_each)).reshape(tiles).astype(F32)
    arrived = swap(outgoing.reshape(peers, send_each, width)).reshape(rows_dev, width)
    grouped, normed, pooled = group(ids, arrived, attention_norm_gain[None])
    candidates = fetch_blocks(pooled).reshape((2 * REACH + 1) * blocks_dev, comp, width)
    owner = neighbour_ball_list // blocks_dev
    offset = jnp.mod(owner - me + REACH, peers)
    chosen = (offset * blocks_dev + neighbour_ball_list % blocks_dev).reshape(-1)
    scale = head_score_scale * (LOG2E * heads / width)
    query, num, den = local_attention(normed, query_weight.T, key_weight.T, value_weight.T, scale)
    ball_out = finish(
        chosen,
        candidates,
        query,
        num,
        den,
        grouped,
        pooled_key_weight.T,
        pooled_value_weight.T,
        output_weight,
        feedforward_norm_gain[None],
        gate_weight,
        up_weight,
        down_weight,
    )
    returning = take_rows(ids, ball_out).reshape(peers, send_each, width)
    came_back = swap(returning).reshape(rows_dev, width)
    return take_rows(rank, came_back)


def solution(mesh):
    rows = P(("rep", "pts"), None)
    return jax.shard_map(
        on_device,
        mesh=mesh,
        in_specs=(rows, P(("rep", "pts")), rows) + (P(),) * 12,
        out_specs=rows,
        check_vma=False,
    )
```

time: 365 us -> 266 us (0.73); the launches traced: 358 us -> 266 us
  Pallas kernels: 0 us -> 118 us
  matrix products: 113 us -> 0 us
  blocking collectives: 0 us -> 68.5 us
  local copies, waits for them, and re-layouts: 63.1 us -> 9.82 us
  waiting for transfers between devices: 85.9 us -> 47.6 us
  other arithmetic: 38 us -> 1.14 us
  loops' own time: 20.9 us -> 0 us
  starting transfers between devices: 37.2 us -> 20.1 us
    pallas_call x0 -> x6, Pallas kernels: none -> 118 us  [the longest x1 41.6 us: finish(): pl.pallas_call(functools.partial(finish_kernel, heads), grid_spec=pltpu.P...]
    dot_general x53 -> x0, matrix products: 113 us -> none  [the longest x19 24.9 us: project_columns(): jnp.einsum('nc,cx->xn', rows, weight, preferred_element_type=jnp.float32)]
    all_to_all x0 -> x2, blocking collectives: none -> 68.5 us  [swap(): return lax.all_to_all(array, 'pts', split_axis=0, concat_axis=0, tiled=True)]
    gather x6 -> x0, local copies, waits for them, and re-layouts: 52.9 us -> none  [the longest x1 11.8 us: on_device(): jnp.take(point_row_index, sort_order, axis=0).reshape(peer_count, send_each)]
    all_to_all x3 -> x1, waiting for transfers between devices: 72.4 us -> 33.5 us  [swap(): return lax.all_to_all(array, 'pts', split_axis=0, concat_axis=0, tiled=True)]
    another operation x1 -> x0, loops' own time: 20.9 us -> none  [on_device(): lax.map(one_ball, jnp.arange(blocks_dev, dtype=jnp.int32))]
    all_to_all x3 -> x1, starting transfers between devices: 20.9 us -> 4.36 us  [swap(): return lax.all_to_all(array, 'pts', split_axis=0, concat_axis=0, tiled=True)]
    sort x3 -> x0, other arithmetic: 16 us -> none  [the longest x1 5.89 us: on_device(): sort_order = jnp.argsort(point_row_index)]
  transfers between devices with their start and end apart: 11 -> 9, of which waited for: 7 -> 4; matrix products, arithmetic and copies ran while one was open for 9% -> 3% of each run, Pallas kernels for 0% -> 13%
where the time goes in v1:
time: 266 us
  Pallas kernels  118 us (44%)
  blocking collectives  68.5 us (26%)
  waiting for transfers between devices  47.6 us (18%)
  starting transfers between devices  20.1 us (8%)
  local copies, waits for them, and re-layouts  9.82 us (4%)
    all_to_all x2, blocking collectives, swap(): return lax.all_to_all(array, 'pts', split_axis=0, concat_axis=0, tiled=True)  68.5 us
    pallas_call x1, Pallas kernels, finish(): pl.pallas_call(functools.partial(finish_kernel, heads), grid_spec=pltpu.P...  41.6 us
    pallas_call x1, Pallas kernels, local_attention(): pl.pallas_call(functools.partial(local_kernel, heads), grid=(rows_dev //...  34.3 us
    all_to_all x1, waiting for transfers between devices, swap(): return lax.all_to_all(array, 'pts', split_axis=0, concat_axis=0, tiled=True)  33.5 us
    pallas_call x2, Pallas kernels, take_rows(): pl.pallas_call(rows_kernel, grid=(rows_dev // TILE,), in_specs=[whole(ids...  16.9 us
    pallas_call x1, Pallas kernels, send_order(): pl.pallas_call(functools.partial(send_kernel, rows_dev), grid=(rows_dev /...  15.9 us
    ppermute x8, starting transfers between devices, from_behind(): return lax.ppermute(block, axis, route)  15.7 us
    ppermute x8, waiting for transfers between devices, from_behind(): return lax.ppermute(block, axis, route)  14.1 us
  transfers between devices with their start and end apart: 9, of which 4 were waited for; matrix products, arithmetic and copies ran while one was open for 3% of the time, Pallas kernels for 13%

profile of v1, /device:TPU:1, one launch (start us, length us, event | category | flops | bytes accessed | tf_op | source)
XLA Modules:
  0.0 265.6 jit_solution(9424768441290562897)
XLA Ops:
  0.0 15.9 %send_order.1 = (bf16[2048,512]{1,0:T(8,128)(2,1)}, s32[16,128]{1,0:T(8,128)}, f32[16,128]{1,0:T(8,128)}) custom-call(s32[16,128]{1,0:T(8,128)} %bitcast.49, bf16[2048,512]{1,0:T(8,128)(2,1)} %points_ref.1), custom_call_target="tpu_custom_call" | custom-call | flops 5368709120 | bytes 4194304 | tf_op jit(solution)/shard_map/send_order/pallas_call | solution.py:88
  15.9 0.0 copy-start.1
  15.9 13.2 %all_to_all.19 = s32[16,1,128]{2,1,0:T(1,128)S(1)} all-to-all(s32[16,1,128]{2,1,0:T(1,128)} %bitcast.48), channel_id=1, replica_groups=mesh['pts'=16,'rep'=2] {'pts'}, dimensions={0} | all-to-all | bytes 16384 | tf_op jit(solution)/shard_map/all_to_all | solution.py:375
  29.1 0.0 copy-start.2
  29.1 4.4 %all-to-all-start.1 = ((bf16[16,128,512]{2,1,0:T(8,128)(2,1)}), bf16[16,128,512]{2,1,0:T(8,128)(2,1)S(1)}, u32[]{:S(2)}, u32[]{:S(2)}) async-start(bf16[16,128,512]{2,1,0:T(8,128)(2,1)} %bitcast.38), calls=%async_computation.1 | async-start | bytes 4194304 | tf_op jit(solution)/shard_map/all_to_all | solution.py:375
  33.5 0.0 copy-done.1
  33.5 1.0 copy.31
  34.6 0.0 copy-done.2
  34.6 0.0 copy-start.3
  34.6 0.0 copy-start.7
  34.6 0.0 copy-start.8
  34.6 1.0 copy.32
  35.6 0.0 copy-start.4
  35.6 2.1 copy.33
  37.7 0.0 copy-done.3
  37.7 1.0 copy.34
  38.7 0.0 copy-done.4
  38.7 1.0 copy.35
  39.7 0.0 copy-done.7
  39.7 0.1 copy.30
  39.8 0.7 reshape.25.chosen_ref
  40.4 0.0 copy-done.8
  40.4 0.5 broadcast_multiply_fusion.scale_ref
  40.9 0.6 convert_bitcast_fusion.ids_ref
  41.5 33.5 %all-to-all-done.1 = bf16[16,128,512]{2,1,0:T(8,128)(2,1)S(1)} async-done(((bf16[16,128,512]{2,1,0:T(8,128)(2,1)}), bf16[16,128,512]{2,1,0:T(8,128)(2,1)S(1)}, u32[]{:S(2)}, u32[]{:S(2)}) %all-to-all-start.1) | async-done | bytes 2097184 | tf_op jit(solution)/shard_map/all_to_all | solution.py:375
  75.0 0.0 copy-start
  75.0 1.3 copy-done
  76.3 9.7 %group_balls.1 = (bf16[2048,512]{1,0:T(8,128)(2,1)}, bf16[2048,512]{1,0:T(8,128)(2,1)}, bf16[256,512]{1,0:T(8,128)(2,1)}) custom-call(f32[16,128]{1,0:T(8,128)} %convert_bitcast_fusion.ids_ref, bf16[2048,512]{1,0:T(8,128)(2,1)} %bitcast.37, f32[1,512]{1,0:T(1,128)} %bitcast.50), custom_call_target="tpu_custom_call" | custom-call | flops 4294967296 | bytes 6291456 | tf_op jit(solution)/shard_map/group_balls/pallas_call | solution.py:132
  86.0 5.9 %collective-permute-start = (bf16[256,512]{1,0:T(8,128)(2,1)}, bf16[256,512]{1,0:T(8,128)(2,1)S(1)}, u32[]{:S(2)}, u32[]{:S(2)}) collective-permute-start(bf16[256,512]{1,0:T(8,128)(2,1)} %get-tuple-element.17), channel_id=1, source_target_pairs={{24,0},{26,2},{28,4},{30,6},{0,8},{2,10},{4,12},{6,14},{8,16},{10,... | collective-permute-start | bytes 786440 | tf_op jit(solution)/shard_map/ppermute | solution.py:339
  91.9 3.4 %collective-permute-start.1 = (bf16[256,512]{1,0:T(8,128)(2,1)}, bf16[256,512]{1,0:T(8,128)(2,1)S(1)}, u32[]{:S(2)}, u32[]{:S(2)}) collective-permute-start(bf16[256,512]{1,0:T(8,128)(2,1)} %get-tuple-element.17), channel_id=1, source_target_pairs={{26,0},{28,2},{30,4},{0,6},{2,8},{4,10},{6,12},{8,14},{10,16},{12,... | collective-permute-start | bytes 786440 | tf_op jit(solution)/shard_map/ppermute | solution.py:339
  95.3 0.0 collective-permute-start.2
  95.3 1.5 collective-permute-start.3
  96.7 0.0 collective-permute-start.4
  96.7 0.0 copy-start.5
  96.7 34.3 %local_attention.1 = (bf16[512,2048]{1,0:T(8,128)(2,1)}, f32[512,2048]{1,0:T(8,128)}, f32[16,2048]{1,0:T(8,128)}) custom-call(f32[16]{0:T(128)} %broadcast_multiply_fusion.scale_ref, bf16[2048,512]{1,0:T(8,128)(2,1)} %get-tuple-element.18.normed_ref, bf16[512,512]{1,0:T(8,128)(2,1)} %bitcast.43, bf16[512,512]{1,0:T(8,128)(2,1)} %bitcast.44, ...), custom_call_target="tpu_custom_call" | custom-call | flops 10737418240 | bytes 8388608 | tf_op jit(solution)/shard_map/local_attention/pallas_call | solution.py:199
  131.1 0.0 collective-permute-done
  131.1 0.0 copy-done.5
  131.1 3.4 %collective-permute-start.5 = (bf16[256,512]{1,0:T(8,128)(2,1)S(1)}, bf16[256,512]{1,0:T(8,128)(2,1)S(1)}, u32[]{:S(2)}, u32[]{:S(2)}) collective-permute-start(bf16[256,512]{1,0:T(8,128)(2,1)S(1)} %copy-done.5), channel_id=1, source_target_pairs={{4,0},{6,2},{8,4},{10,6},{12,8},{14,10},{16,12},{18,14},{20,16},{2... | collective-permute-start | bytes 786440 | tf_op jit(solution)/shard_map/ppermute | solution.py:339
  134.6 0.0 collective-permute-done.1
  134.6 1.0 collective-permute-start.6
  135.6 0.0 collective-permute-done.2
  135.6 0.6 collective-permute-start.7
  136.2 0.0 collective-permute-done.3
  136.2 0.0 collective-permute-done.4
  136.3 2.9 %collective-permute-done.5 = bf16[256,512]{1,0:T(8,128)(2,1)S(1)} collective-permute-done((bf16[256,512]{1,0:T(8,128)(2,1)S(1)}, bf16[256,512]{1,0:T(8,128)(2,1)S(1)}, u32[]{:S(2)}, u32[]{:S(2)}) %collective-permute-start.5) | collective-permute-done | bytes 262176 | tf_op jit(solution)/shard_map/ppermute | solution.py:339
  139.2 6.2 %collective-permute-done.6 = bf16[256,512]{1,0:T(8,128)(2,1)S(1)} collective-permute-done((bf16[256,512]{1,0:T(8,128)(2,1)S(1)}, bf16[256,512]{1,0:T(8,128)(2,1)S(1)}, u32[]{:S(2)}, u32[]{:S(2)}) %collective-permute-start.6) | collective-permute-done | bytes 262176 | tf_op jit(solution)/shard_map/ppermute | solution.py:339
  145.5 4.9 %collective-permute-done.7 = bf16[256,512]{1,0:T(8,128)(2,1)S(1)} collective-permute-done((bf16[256,512]{1,0:T(8,128)(2,1)S(1)}, bf16[256,512]{1,0:T(8,128)(2,1)S(1)}, u32[]{:S(2)}, u32[]{:S(2)}) %collective-permute-start.7) | collective-permute-done | bytes 262176 | tf_op jit(solution)/shard_map/ppermute | solution.py:339
  150.4 0.0 copy-start.6
  150.4 1.4 copy-done.6
  151.9 41.6 %finish_balls.1.source_ref = bf16[2048,512]{1,0:T(8,128)(2,1)} custom-call(s32[32]{0:T(128)} %reshape.25.chosen_ref, bf16[72,32,512]{2,1,0:T(8,128)(2,1)} %bitcast.47, bf16[512,2048]{1,0:T(8,128)(2,1)} %get-tuple-element.19.query_ref, f32[512,2048]{1,0:T(8,128)} %get-tuple-element.20.num_ref, f32[16,2048]{1,0:T(8,128)} %get-tuple-element.21.den_ref, ...), custom_call_target="tpu_custom_call" | custom-call | flops 12884901888 | bytes 12582912 | tf_op jit(solution)/shard_map/finish_balls/pallas_call | solution.py:271
  193.5 8.5 %take_rows.2 = bf16[2048,512]{1,0:T(8,128)(2,1)} custom-call(f32[16,128]{1,0:T(8,128)} %convert_bitcast_fusion.ids_ref, bf16[2048,512]{1,0:T(8,128)(2,1)} %finish_balls.1.source_ref), custom_call_target="tpu_custom_call" | custom-call | flops 4294967296 | bytes 4194304 | tf_op jit(solution)/shard_map/take_rows/pallas_call | solution.py:322
  201.9 55.2 %all_to_all.20 = bf16[16,128,512]{2,1,0:T(8,128)(2,1)} all-to-all(bf16[16,128,512]{2,1,0:T(8,128)(2,1)} %bitcast.40), channel_id=1, replica_groups=mesh['pts'=16,'rep'=2] {'pts'}, dimensions={0} | all-to-all | bytes 4194304 | tf_op jit(solution)/shard_map/all_to_all | solution.py:375
  257.2 8.5 %take_rows.3 = bf16[2048,512]{1,0:T(8,128)(2,1)} custom-call(f32[16,128]{1,0:T(8,128)} %get-tuple-element.14.ids_ref, bf16[2048,512]{1,0:T(8,128)(2,1)} %bitcast.39), custom_call_target="tpu_custom_call" | custom-call | flops 4294967296 | bytes 4194304 | tf_op jit(solution)/shard_map/take_rows/pallas_call | solution.py:322
  (10 shorter events, 0.2 us)
Async XLA Ops:
  15.9 17.6 %copy-start.1 = (bf16[512,512]{1,0:T(8,128)(2,1)S(1)}, bf16[512,512]{1,0:T(8,128)(2,1)}, u32[]{:S(2)}) copy-start(bf16[512,512]{1,0:T(8,128)(2,1)} %param.19) | copy-start | bytes 1572868
  29.1 5.4 %copy-start.2 = (bf16[512,512]{1,0:T(8,128)(2,1)S(1)}, bf16[512,512]{1,0:T(8,128)(2,1)}, u32[]{:S(2)}) copy-start(bf16[512,512]{1,0:T(8,128)(2,1)} %param.20) | copy-start | bytes 1572868
  29.1 45.9 %all-to-all-start.1 = ((bf16[16,128,512]{2,1,0:T(8,128)(2,1)}), bf16[16,128,512]{2,1,0:T(8,128)(2,1)S(1)}, u32[]{:S(2)}, u32[]{:S(2)}) async-start(bf16[16,128,512]{2,1,0:T(8,128)(2,1)} %bitcast.38), calls=%async_computation.1 | async-start | bytes 4194304 | tf_op jit(solution)/shard_map/all_to_all | solution.py:375
  34.6 3.1 %copy-start.3 = (bf16[512,512]{1,0:T(8,128)(2,1)S(1)}, bf16[512,512]{1,0:T(8,128)(2,1)}, u32[]{:S(2)}) copy-start(bf16[512,512]{1,0:T(8,128)(2,1)} %param.22) | copy-start | bytes 1572868
  34.6 5.1 %copy-start.7 = (s32[8,4]{0,1:T(4,128)S(1)}, s32[8,4]{0,1:T(4,128)}, u32[]{:S(2)}) copy-start(s32[8,4]{0,1:T(4,128)} %param.17) | copy-start | bytes 388
  34.6 5.9 %copy-start.8 = (f32[16]{0:T(128)S(1)}, f32[16]{0:T(128)}, u32[]{:S(2)}) copy-start(f32[16]{0:T(128)} %param.24) | copy-start | bytes 196
  35.6 3.1 %copy-start.4 = (bf16[512,512]{1,0:T(8,128)(2,1)S(1)}, bf16[512,512]{1,0:T(8,128)(2,1)}, u32[]{:S(2)}) copy-start(bf16[512,512]{1,0:T(8,128)(2,1)} %param.23) | copy-start | bytes 1572868
  75.0 1.3 copy-start
  86.0 45.1 %collective-permute-start = (bf16[256,512]{1,0:T(8,128)(2,1)}, bf16[256,512]{1,0:T(8,128)(2,1)S(1)}, u32[]{:S(2)}, u32[]{:S(2)}) collective-permute-start(bf16[256,512]{1,0:T(8,128)(2,1)} %get-tuple-element.17), channel_id=1, source_target_pairs={{24,0},{26,2},{28,4},{30,6},{0,8},{2,10},{4,12},{6,14},{8,16},{10,... | collective-permute-start | bytes 786440 | tf_op jit(solution)/shard_map/ppermute | solution.py:339
  91.9 42.7 %collective-permute-start.1 = (bf16[256,512]{1,0:T(8,128)(2,1)}, bf16[256,512]{1,0:T(8,128)(2,1)S(1)}, u32[]{:S(2)}, u32[]{:S(2)}) collective-permute-start(bf16[256,512]{1,0:T(8,128)(2,1)} %get-tuple-element.17), channel_id=1, source_target_pairs={{26,0},{28,2},{30,4},{0,6},{2,8},{4,10},{6,12},{8,14},{10,16},{12,... | collective-permute-start | bytes 786440 | tf_op jit(solution)/shard_map/ppermute | solution.py:339
  95.3 40.3 %collective-permute-start.2 = (bf16[256,512]{1,0:T(8,128)(2,1)}, bf16[256,512]{1,0:T(8,128)(2,1)S(1)}, u32[]{:S(2)}, u32[]{:S(2)}) collective-permute-start(bf16[256,512]{1,0:T(8,128)(2,1)} %get-tuple-element.17), channel_id=1, source_target_pairs={{28,0},{30,2},{0,4},{2,6},{4,8},{6,10},{8,12},{10,14},{12,16},{14,... | collective-permute-start | bytes 786440 | tf_op jit(solution)/shard_map/ppermute | solution.py:339
  95.3 40.9 %collective-permute-start.3 = (bf16[256,512]{1,0:T(8,128)(2,1)}, bf16[256,512]{1,0:T(8,128)(2,1)S(1)}, u32[]{:S(2)}, u32[]{:S(2)}) collective-permute-start(bf16[256,512]{1,0:T(8,128)(2,1)} %get-tuple-element.17), channel_id=1, source_target_pairs={{30,0},{0,2},{2,4},{4,6},{6,8},{8,10},{10,12},{12,14},{14,16},{16,... | collective-permute-start | bytes 786440 | tf_op jit(solution)/shard_map/ppermute | solution.py:339
  96.7 39.5 %collective-permute-start.4 = (bf16[256,512]{1,0:T(8,128)(2,1)}, bf16[256,512]{1,0:T(8,128)(2,1)S(1)}, u32[]{:S(2)}, u32[]{:S(2)}) collective-permute-start(bf16[256,512]{1,0:T(8,128)(2,1)} %get-tuple-element.17), channel_id=1, source_target_pairs={{2,0},{4,2},{6,4},{8,6},{10,8},{12,10},{14,12},{16,14},{18,16},{20... | collective-permute-start | bytes 786440 | tf_op jit(solution)/shard_map/ppermute | solution.py:339
  96.7 34.4 %copy-start.5 = (bf16[256,512]{1,0:T(8,128)(2,1)S(1)}, bf16[256,512]{1,0:T(8,128)(2,1)}, u32[]{:S(2)}) copy-start(bf16[256,512]{1,0:T(8,128)(2,1)} %get-tuple-element.17) | copy-start | bytes 786436
  131.1 8.1 %collective-permute-start.5 = (bf16[256,512]{1,0:T(8,128)(2,1)S(1)}, bf16[256,512]{1,0:T(8,128)(2,1)S(1)}, u32[]{:S(2)}, u32[]{:S(2)}) collective-permute-start(bf16[256,512]{1,0:T(8,128)(2,1)S(1)} %copy-done.5), channel_id=1, source_target_pairs={{4,0},{6,2},{8,4},{10,6},{12,8},{14,10},{16,12},{18,14},{20,16},{2... | collective-permute-start | bytes 786440 | tf_op jit(solution)/shard_map/ppermute | solution.py:339
  134.6 10.9 %collective-permute-start.6 = (bf16[256,512]{1,0:T(8,128)(2,1)S(1)}, bf16[256,512]{1,0:T(8,128)(2,1)S(1)}, u32[]{:S(2)}, u32[]{:S(2)}) collective-permute-start(bf16[256,512]{1,0:T(8,128)(2,1)S(1)} %copy-done.5), channel_id=1, source_target_pairs={{6,0},{8,2},{10,4},{12,6},{14,8},{16,10},{18,12},{20,14},{22,16},{... | collective-permute-start | bytes 786440 | tf_op jit(solution)/shard_map/ppermute | solution.py:339
  135.6 14.8 %collective-permute-start.7 = (bf16[256,512]{1,0:T(8,128)(2,1)S(1)}, bf16[256,512]{1,0:T(8,128)(2,1)S(1)}, u32[]{:S(2)}, u32[]{:S(2)}) collective-permute-start(bf16[256,512]{1,0:T(8,128)(2,1)S(1)} %copy-done.5), channel_id=1, source_target_pairs={{8,0},{10,2},{12,4},{14,6},{16,8},{18,10},{20,12},{22,14},{24,16},... | collective-permute-start | bytes 786440 | tf_op jit(solution)/shard_map/ppermute | solution.py:339
  150.4 1.5 copy-start.6

commit v2 on v1

v2 whole, which is shorter than its diff:
```python
import functools
import math

import jax
import jax.numpy as jnp
from jax import lax
from jax.experimental import pallas as pl
from jax.experimental.pallas import tpu as pltpu
from jax.sharding import PartitionSpec as P

BALL = 256
POOL = 8
OWNERS = 4
REACH = 4
LANES = 128
TILE = 512
DEPTH = 512
BALLS_STEP = 2
LOW = 64
LOG2E = math.log2(math.e)
F32 = jnp.float32
BF16 = jnp.bfloat16
VMEM_BYTES = 40 * 1024 * 1024


def params(**kwargs):
    return pltpu.CompilerParams(vmem_limit_bytes=VMEM_BYTES, **kwargs)


def dot(a, b):
    return jnp.dot(a, b, preferred_element_type=F32)


def dot_nt(a, b):
    return lax.dot_general(a, b, (((1,), (1,)), ((), ())), preferred_element_type=F32)


def whole(shape):
    return pl.BlockSpec(shape, lambda *_: (0,) * len(shape))


def row_blocks(rows, width):
    return pl.BlockSpec((rows, width), lambda i, *_: (i, 0))


def column_of(row):
    return jnp.broadcast_to(row, (LANES, LANES)).T


def picked_rows(pick_tile, rows, source_ref):
    count = source_ref.shape[0]
    total = None
    for start in range(0, count, DEPTH):
        pick = jnp.concatenate(
            [pick_tile(t) for t in range(start // LANES, (start + DEPTH) // LANES)], axis=1
        )
        part = dot(pick, source_ref[start : start + DEPTH, :])
        total = part if total is None else total + part
    return total


def by_lane_ids(ids_ref, first, rows):
    targets = (lax.broadcasted_iota(jnp.int32, (rows, LANES), 0) + first).astype(F32)
    return lambda t: jnp.where(ids_ref[t : t + 1, :] == targets, 1.0, 0.0).astype(BF16)


def by_row_ids(ids_ref, first, rows):
    wanted = jnp.concatenate(
        [column_of(ids_ref[pl.ds(first + u, 1), :]) for u in range(rows // LANES)], axis=0
    )
    lane = lax.broadcasted_iota(jnp.int32, (rows, LANES), 1).astype(F32)
    return lambda t: jnp.where(wanted - float(t * LANES) == lane, 1.0, 0.0).astype(BF16)


def send_kernel(send_each, me_ref, index_ref, points_ref, out_ref, rank_ref, col, aux):
    rows_dev, width = points_ref.shape
    tiles = rows_dev // LANES
    chunks = width // LANES
    per_tile = LANES // send_each
    step = pl.program_id(0)

    @pl.when(step == 0)
    def _():
        for t in range(tiles):
            col[t * LANES : (t + 1) * LANES, :] = column_of(index_ref[t : t + 1, :].astype(F32))

        def rank_tile(t, carry):
            row = index_ref[pl.ds(t, 1), :].astype(F32)
            below = jnp.where(col[...] < row, 1.0, 0.0)
            rank_ref[pl.ds(t, 1), :] = jnp.sum(below, axis=0, keepdims=True)
            return carry

        lax.fori_loop(0, tiles, rank_tile, 0)
        local = lax.rem(col[...].astype(jnp.int32), rows_dev)
        lane = lax.broadcasted_iota(jnp.int32, (rows_dev, LANES), 1)
        high = lax.div(local, LOW)
        low = lax.rem(local, LOW)
        aux[...] = jnp.where(lane == 0, high, jnp.where(lane == 1, low, 0)).astype(F32).astype(BF16)

    tile = by_lane_ids(rank_ref, step * TILE, TILE)
    rows = picked_rows(tile, TILE, points_ref).astype(BF16)
    ids = picked_rows(tile, TILE, aux)
    for u in range(TILE // LANES):
        both = ids[u * LANES : (u + 1) * LANES, :].T[0:16, :]
        for v in range(per_tile):
            peer = u * per_tile + v
            mine = both
            if per_tile > 1:
                lane = lax.broadcasted_iota(jnp.int32, both.shape, 1)
                mine = jnp.where(lane // send_each == v, both, 0.0)
                mine = pltpu.roll(mine, (me_ref[0] - v + per_tile) % per_tile * send_each, 1)
            out_ref[peer, chunks * send_each :, :] = mine.astype(BF16)
            first = peer * send_each
            for c in range(chunks):
                out_ref[peer, c * send_each : (c + 1) * send_each, :] = rows[
                    first : first + send_each, c * LANES : (c + 1) * LANES
                ]


def send_order(points, index_tiles, me, peers):
    rows_dev, width = points.shape
    tiles = rows_dev // LANES
    send_each = rows_dev // peers
    payload = width // LANES * send_each + 16
    return pl.pallas_call(
        functools.partial(send_kernel, send_each),
        grid_spec=pltpu.PrefetchScalarGridSpec(
            num_scalar_prefetch=1,
            grid=(rows_dev // TILE,),
            in_specs=[whole((tiles, LANES)), whole((rows_dev, width))],
            out_specs=[
                pl.BlockSpec((TILE // send_each, payload, LANES), lambda i, *_: (i, 0, 0)),
                whole((tiles, LANES)),
            ],
            scratch_shapes=[
                pltpu.VMEM((rows_dev, LANES), F32),
                pltpu.VMEM((rows_dev, LANES), BF16),
            ],
        ),
        out_shape=[
            jax.ShapeDtypeStruct((peers, payload, LANES), BF16),
            jax.ShapeDtypeStruct((tiles, LANES), F32),
        ],
        compiler_params=params(),
        cost_estimate=pl.CostEstimate(
            flops=2 * rows_dev * rows_dev * (width + LANES), bytes_accessed=4 * rows_dev * width, transcendentals=0
        ),
        name="send_order",
    )(me.reshape(1), index_tiles, points)


def group_kernel(arrived_ref, gain_ref, grouped_ref, normed_ref, pooled_ref, ids_ref, source):
    peers = arrived_ref.shape[0]
    rows_dev, width = source.shape
    chunks = width // LANES
    send_each = rows_dev // peers
    per_tile = LANES // send_each

    @pl.when(pl.program_id(0) == 0)
    def _():
        for t in range(rows_dev // LANES):
            row = jnp.zeros((1, LANES), F32)
            for p in range(t * per_tile, (t + 1) * per_tile):
                both = arrived_ref[p, chunks * send_each :, :].astype(F32)
                row = row + both[0:1, :] * LOW + both[1:2, :]
            ids_ref[t : t + 1, :] = row
        for p in range(peers):
            for c in range(chunks):
                source[p * send_each : (p + 1) * send_each, c * LANES : (c + 1) * LANES] = arrived_ref[
                    p, c * send_each : (c + 1) * send_each, :
                ]

    tile = by_lane_ids(ids_ref, pl.program_id(0) * TILE, TILE)
    grouped = picked_rows(tile, TILE, source)
    grouped_ref[...] = grouped.astype(BF16)
    mean_square = jnp.mean(grouped * grouped, axis=-1, keepdims=True)
    normed = (grouped * lax.rsqrt(mean_square + 1e-05) * gain_ref[...]).astype(BF16)
    normed_ref[...] = normed
    mean_of = block_matrix(TILE // POOL, 1, TILE, POOL, 1.0 / POOL)
    pooled_ref[...] = dot(mean_of, normed).astype(BF16)


def group(arrived, gain, rows_dev):
    width = gain.shape[1]
    tiles = rows_dev // LANES
    return pl.pallas_call(
        group_kernel,
        grid=(rows_dev // TILE,),
        in_specs=[whole(arrived.shape), whole((1, width))],
        out_specs=[
            row_blocks(TILE, width),
            row_blocks(TILE, width),
            row_blocks(TILE // POOL, width),
            whole((tiles, LANES)),
        ],
        out_shape=[
            jax.ShapeDtypeStruct((rows_dev, width), BF16),
            jax.ShapeDtypeStruct((rows_dev, width), BF16),
            jax.ShapeDtypeStruct((rows_dev // POOL, width), BF16),
            jax.ShapeDtypeStruct((tiles, LANES), F32),
        ],
        scratch_shapes=[pltpu.VMEM((rows_dev, width), BF16)],
        compiler_params=params(),
        cost_estimate=pl.CostEstimate(
            flops=2 * rows_dev * rows_dev * width, bytes_accessed=6 * rows_dev * width, transcendentals=0
        ),
        name="group_balls",
    )(arrived, gain)


def block_matrix(rows, row_step, cols, col_step, value):
    row = lax.broadcasted_iota(jnp.int32, (rows, cols), 0) // row_step
    col = lax.broadcasted_iota(jnp.int32, (rows, cols), 1) // col_step
    return jnp.where(row == col, value, 0.0).astype(BF16)


def clear_spread(head_size, keys_ref, values_ref):
    keys_ref[...] = jnp.zeros_like(keys_ref)
    ones = block_matrix(values_ref.shape[1], values_ref.shape[1] * head_size // LANES, LANES, head_size, 1.0)
    for g in range(values_ref.shape[0]):
        values_ref[g, :, LANES:] = ones


def spread_keys(head_size, columns, ref):
    count = columns.shape[1]
    per_group = LANES // head_size
    for h in range(columns.shape[0] // head_size):
        g, j = h // per_group, h % per_group
        part = columns[h * head_size : (h + 1) * head_size, :]
        root = lax.rsqrt(jnp.mean(part * part, axis=0, keepdims=True) + 1e-06)
        ref[g, j * head_size : (j + 1) * head_size, j * count : (j + 1) * count] = (part * root).astype(BF16)


def spread_values(head_size, values, ref):
    count, width = values.shape
    head = lax.broadcasted_iota(jnp.int32, (count, LANES), 1) // head_size
    for g in range(width // LANES):
        lanes = values[:, g * LANES : (g + 1) * LANES]
        for j in range(LANES // head_size):
            ref[g, j * count : (j + 1) * count, :LANES] = jnp.where(head == j, lanes, jnp.zeros((), BF16))


def local_kernel(head_size, scale_ref, normed_ref, wq_ref, wk_ref, wv_ref, query_ref, num_ref, den_ref, mean_of, keys, values, weights):
    width = normed_ref.shape[1]
    half = mean_of.shape[0]

    @pl.when(pl.program_id(0) == 0)
    def _():
        mean_of[...] = block_matrix(half, head_size, half, head_size, 1.0 / head_size)
        clear_spread(head_size, keys, values)

    normed = normed_ref[...]
    query = dot(normed, wq_ref[...])
    square = query * query
    high = square.astype(BF16)
    low = (square - high.astype(F32)).astype(BF16)
    mean_square = jnp.concatenate(
        [
            dot(high[:, c : c + half], mean_of[...]) + dot(low[:, c : c + half], mean_of[...])
            for c in range(0, width, half)
        ],
        axis=1,
    )
    query = (query * lax.rsqrt(mean_square + 1e-06) * scale_ref[...]).astype(BF16)
    query_ref[...] = query
    spread_keys(head_size, dot_nt(wk_ref[...], normed), keys)
    spread_values(head_size, dot(normed, wv_ref[...]).astype(BF16), values)
    groups = width // LANES
    for g in range(groups):
        weights[g] = jnp.exp2(dot(query[:, g * LANES : (g + 1) * LANES], keys[g])).astype(BF16)
    for g in range(groups):
        both = dot(weights[g], values[g])
        num_ref[:, g * LANES : (g + 1) * LANES] = both[:, :LANES]
        den_ref[:, g * LANES : (g + 1) * LANES] = both[:, LANES:]


def local_attention(normed, wq, wk, wv, scale, head_size):
    rows_dev, width = normed.shape
    square = whole((width, width))
    groups = width // LANES
    spread = LANES // head_size * BALL
    return pl.pallas_call(
        functools.partial(local_kernel, head_size),
        grid=(rows_dev // BALL,),
        in_specs=[whole((1, width)), row_blocks(BALL, width), square, square, square],
        out_specs=[row_blocks(BALL, width)] * 3,
        out_shape=[
            jax.ShapeDtypeStruct((rows_dev, width), BF16),
            jax.ShapeDtypeStruct((rows_dev, width), F32),
            jax.ShapeDtypeStruct((rows_dev, width), F32),
        ],
        scratch_shapes=[
            pltpu.VMEM((2 * LANES, 2 * LANES), BF16),
            pltpu.VMEM((groups, LANES, spread), BF16),
            pltpu.VMEM((groups, spread, 2 * LANES), BF16),
            pltpu.VMEM((groups, BALL, spread), BF16),
        ],
        compiler_params=params(),
        cost_estimate=pl.CostEstimate(
            flops=20 * rows_dev * width * width, bytes_accessed=12 * rows_dev * width, transcendentals=0
        ),
        name="local_attention",
    )(scale, normed, wq, wk, wv)


def finish_kernel(
    head_size,
    chosen_ref,
    candidates_ref,
    query_ref,
    num_ref,
    den_ref,
    grouped_ref,
    wpk_ref,
    wpv_ref,
    wo_ref,
    gain_ref,
    wg_ref,
    wu_ref,
    wd_ref,
    out_ref,
    keys,
    values,
    weights,
    attended,
):
    step = pl.program_id(0)
    groups = wo_ref.shape[0] // LANES
    far = OWNERS * BALL // POOL

    @pl.when(step == 0)
    def _():
        for b in range(BALLS_STEP):
            clear_spread(head_size, keys.at[b], values.at[b])

    first = step * BALLS_STEP * OWNERS
    coarse = jnp.concatenate(
        [candidates_ref[chosen_ref[first + o]] for o in range(BALLS_STEP * OWNERS)], axis=0
    )
    key_columns = dot_nt(wpk_ref[...], coarse)
    value_rows = dot(coarse, wpv_ref[...]).astype(BF16)
    for b in range(BALLS_STEP):
        spread_keys(head_size, key_columns[:, b * far : (b + 1) * far], keys.at[b])
        spread_values(head_size, value_rows[b * far : (b + 1) * far, :], values.at[b])
    for b in range(BALLS_STEP):
        rows = slice(b * BALL, (b + 1) * BALL)
        for g in range(groups):
            score = dot(query_ref[rows, g * LANES : (g + 1) * LANES], keys[b, g])
            weights[b, g] = jnp.exp2(score).astype(BF16)
    for b in range(BALLS_STEP):
        rows = slice(b * BALL, (b + 1) * BALL)
        for g in range(groups):
            lanes = slice(g * LANES, (g + 1) * LANES)
            both = dot(weights[b, g], values[b, g])
            num = both[:, :LANES] + num_ref[rows, lanes]
            den = both[:, LANES:] + den_ref[rows, lanes]
            attended[rows, lanes] = (num / den).astype(BF16)
    projected = dot(attended[...], wo_ref[...])
    residual = (grouped_ref[...].astype(F32) + projected).astype(BF16)
    rows32 = residual.astype(F32)
    mean_square = jnp.mean(rows32 * rows32, axis=-1, keepdims=True)
    ffn = (rows32 * lax.rsqrt(mean_square + 1e-05) * gain_ref[...]).astype(BF16)
    gate = dot(ffn, wg_ref[...])
    up = dot(ffn, wu_ref[...])
    hidden = (0.5 * gate * (1.0 + jnp.tanh(0.5 * gate)) * up).astype(BF16)
    out_ref[...] = (rows32 + dot(hidden, wd_ref[...])).astype(BF16)


def finish(chosen, candidates, query, num, den, grouped, wpk, wpv, wo, gain, wg, wu, wd, head_size):
    rows_dev, width = grouped.shape
    hidden = wg.shape[1]
    groups = width // LANES
    step_rows = BALLS_STEP * BALL
    spread = LANES // head_size * OWNERS * BALL // POOL
    rows = row_blocks(step_rows, width)
    fixed = [wpk, wpv, wo, gain, wg, wu, wd]
    return pl.pallas_call(
        functools.partial(finish_kernel, head_size),
        grid_spec=pltpu.PrefetchScalarGridSpec(
            num_scalar_prefetch=1,
            grid=(rows_dev // step_rows,),
            in_specs=[whole(candidates.shape), rows, rows, rows, rows] + [whole(a.shape) for a in fixed],
            out_specs=rows,
            scratch_shapes=[
                pltpu.VMEM((BALLS_STEP, groups, LANES, spread), BF16),
                pltpu.VMEM((BALLS_STEP, groups, spread, 2 * LANES), BF16),
                pltpu.VMEM((BALLS_STEP, groups, BALL, spread), BF16),
                pltpu.VMEM((step_rows, width), BF16),
            ],
        ),
        out_shape=jax.ShapeDtypeStruct((rows_dev, width), BF16),
        compiler_params=params(),
        cost_estimate=pl.CostEstimate(
            flops=2 * rows_dev * width * (3 * hidden + 6 * width),
            bytes_accessed=12 * rows_dev * width,
            transcendentals=0,
        ),
        name="finish_balls",
    )(chosen, candidates, query, num, den, grouped, *fixed)


def rows_kernel(ids_ref, source_ref, out_ref):
    tile = by_row_ids(ids_ref, pl.program_id(0) * (TILE // LANES), TILE)
    out_ref[...] = picked_rows(tile, TILE, source_ref).astype(BF16)


def take_rows(ids, source):
    rows_dev, width = source.shape
    return pl.pallas_call(
        rows_kernel,
        grid=(rows_dev // TILE,),
        in_specs=[whole(ids.shape), whole(source.shape)],
        out_specs=row_blocks(TILE, width),
        out_shape=jax.ShapeDtypeStruct((rows_dev, width), BF16),
        compiler_params=params(),
        cost_estimate=pl.CostEstimate(
            flops=2 * rows_dev * rows_dev * width, bytes_accessed=4 * rows_dev * width, transcendentals=0
        ),
        name="take_rows",
    )(ids, source)


def from_behind(block, axis, distance):
    devices = range(lax.axis_size(axis))
    route = [((i - distance) % len(devices), i) for i in devices]
    return lax.ppermute(block, axis, route)


def fetch_blocks(payload):
    return jnp.stack(
        [payload if k == 0 else from_behind(payload, "pts", k) for k in range(REACH, -REACH - 1, -1)]
    )


def on_device(
    points,
    point_row_index,
    neighbour_ball_list,
    attention_norm_gain,
    query_weight,
    key_weight,
    value_weight,
    pooled_key_weight,
    pooled_value_weight,
    head_score_scale,
    output_weight,
    feedforward_norm_gain,
    gate_weight,
    up_weight,
    down_weight,
):
    rows_dev, width = points.shape
    head_size = width // head_score_scale.shape[0]
    peers = lax.axis_size("pts")
    me = lax.axis_index("pts")
    send_each = rows_dev // peers
    blocks_dev = rows_dev // BALL
    comp = BALL // POOL

    def swap(array):
        return lax.all_to_all(array, "pts", split_axis=0, concat_axis=0, tiled=True)

    outgoing, rank = send_order(points, point_row_index.reshape(rows_dev // LANES, LANES), me, peers)
    grouped, normed, pooled, ids = group(swap(outgoing), attention_norm_gain[None], rows_dev)
    candidates = fetch_blocks(pooled).reshape((2 * REACH + 1) * blocks_dev, comp, width)
    owner = neighbour_ball_list // blocks_dev
    offset = jnp.mod(owner - me + REACH, peers)
    chosen = (offset * blocks_dev + neighbour_ball_list % blocks_dev).reshape(-1)
    scale = jnp.repeat(head_score_scale * (LOG2E / head_size), head_size)[None]
    query, num, den = local_attention(normed, query_weight, key_weight.T, value_weight, scale, head_size)
    ball_out = finish(
        chosen,
        candidates,
        query,
        num,
        den,
        grouped,
        pooled_key_weight.T,
        pooled_value_weight,
        output_weight,
        feedforward_norm_gain[None],
        gate_weight,
        up_weight,
        down_weight,
        head_size,
    )
    returning = take_rows(ids, ball_out).reshape(peers, send_each, width)
    came_back = swap(returning).reshape(rows_dev, width)
    return take_rows(rank, came_back)


def solution(mesh):
    rows = P(("rep", "pts"), None)
    return jax.shard_map(
        on_device,
        mesh=mesh,
        in_specs=(rows, P(("rep", "pts")), rows) + (P(),) * 12,
        out_specs=rows,
        check_vma=False,
    )
```

time: 266 us -> 206 us (0.77)
  Pallas kernels: 118 us -> 64.7 us
  blocking collectives: 68.5 us -> 54.9 us
  waiting for transfers between devices: 47.6 us -> 54.7 us
  starting transfers between devices: 20.1 us -> 23.7 us
    pallas_call x4, Pallas kernels: 101 us -> 53.5 us  [the longest x1 18.4 us: finish(): pl.pallas_call(functools.partial(finish_kernel, head_size), grid_spec=plt...]
    all_to_all x2 -> x1, blocking collectives: 68.5 us -> 54.9 us  [swap(): return lax.all_to_all(array, 'pts', split_axis=0, concat_axis=0, tiled=True)]
    all_to_all x1, waiting for transfers between devices: 33.5 us -> 40.8 us  [swap(): return lax.all_to_all(array, 'pts', split_axis=0, concat_axis=0, tiled=True)]
    pallas_call x2, Pallas kernels: 16.9 us -> 11.2 us  [take_rows(): pl.pallas_call(rows_kernel, grid=(rows_dev // TILE,), in_specs=[whole(ids...]
    all_to_all x1, starting transfers between devices: 4.36 us -> 7.47 us  [swap(): return lax.all_to_all(array, 'pts', split_axis=0, concat_axis=0, tiled=True)]
    unnamed x31 -> x44, local copies, waits for them, and re-layouts: 9.06 us -> 7.36 us
  transfers between devices with their start and end apart: 9 -> 9, of which waited for: 4 -> 4; matrix products, arithmetic and copies ran while one was open for 3% -> 1% of each run, Pallas kernels for 13% -> 8%
where the time goes in v2:
time: 206 us
  Pallas kernels  64.7 us (31%)
  blocking collectives  54.9 us (27%)
  waiting for transfers between devices  54.7 us (27%)
  starting transfers between devices  23.7 us (12%)
  local copies, waits for them, and re-layouts  7.7 us (4%)
    all_to_all x1, blocking collectives, swap(): return lax.all_to_all(array, 'pts', split_axis=0, concat_axis=0, tiled=True)  54.9 us
    all_to_all x1, waiting for transfers between devices, swap(): return lax.all_to_all(array, 'pts', split_axis=0, concat_axis=0, tiled=True)  40.8 us
    pallas_call x1, Pallas kernels, finish(): pl.pallas_call(functools.partial(finish_kernel, head_size), grid_spec=plt...  18.4 us
    ppermute x8, starting transfers between devices, from_behind(): return lax.ppermute(block, axis, route)  16.2 us
    pallas_call x1, Pallas kernels, local_attention(): pl.pallas_call(functools.partial(local_kernel, head_size), grid=(rows_dev...  15.7 us
    ppermute x8, waiting for transfers between devices, from_behind(): return lax.ppermute(block, axis, route)  14 us
    pallas_call x1, Pallas kernels, send_order(): pl.pallas_call(functools.partial(send_kernel, send_each), grid_spec=pltpu...  12.9 us
    pallas_call x2, Pallas kernels, take_rows(): pl.pallas_call(rows_kernel, grid=(rows_dev // TILE,), in_specs=[whole(ids...  11.2 us
  transfers between devices with their start and end apart: 9, of which 4 were waited for; matrix products, arithmetic and copies ran while one was open for 1% of the time, Pallas kernels for 8%

profile of v2, /device:TPU:1, one launch (start us, length us, event | category | flops | bytes accessed | tf_op | source)
XLA Modules:
  0.0 206.0 jit_solution(1566835168603841581)
XLA Ops:
  0.0 0.0 copy-start.1
  0.0 1.6 copy-done.1
  1.6 0.0 copy-start.9
  1.6 0.7 copy-done.9
  2.3 12.9 %send_order.1 = (bf16[16,528,128]{2,1,0:T(8,128)(2,1)S(1)}, f32[16,128]{1,0:T(8,128)S(1)}) custom-call(s32[1]{0:T(128)} %bitcast.me_ref, s32[16,128]{1,0:T(8,128)S(1)} %bitcast.32, bf16[2048,512]{1,0:T(8,128)(2,1)S(1)} %copy-done.1), custom_call_target="tpu_custom_call" | custom-call | flops 5368709120 | bytes 4194304 | tf_op jit(solution)/shard_map/send_order/pallas_call | solution.py:125
  15.2 0.0 copy-start
  15.2 1.4 copy-done
  16.6 0.0 copy-start.15
  16.6 0.0 copy-start.16
  16.6 0.0 copy-start.14
  16.6 0.0 copy-start.10
  16.6 7.5 %all-to-all-start = ((bf16[16,528,128]{2,1,0:T(8,128)(2,1)}), bf16[16,528,128]{2,1,0:T(8,128)(2,1)S(1)}, u32[]{:S(2)}, u32[]{:S(2)}) async-start(bf16[16,528,128]{2,1,0:T(8,128)(2,1)} %copy-done), calls=%async_computation | async-start | bytes 4325376 | tf_op jit(solution)/shard_map/all_to_all | solution.py:461
  24.1 0.0 copy-done.15
  24.1 0.1 copy.19
  24.2 0.1 reshape.20.chosen_ref
  24.3 0.0 copy-done.16
  24.3 0.1 broadcast_in_dim.10
  24.3 0.1 broadcast_in_dim_reshape.3.scale_ref
  24.4 0.0 copy-done.14
  24.4 0.2 copy.20
  24.7 1.3 copy.21
  25.9 40.8 %all-to-all-done.arrived_ref = bf16[16,528,128]{2,1,0:T(8,128)(2,1)S(1)} async-done(((bf16[16,528,128]{2,1,0:T(8,128)(2,1)}), bf16[16,528,128]{2,1,0:T(8,128)(2,1)S(1)}, u32[]{:S(2)}, u32[]{:S(2)}) %all-to-all-start) | async-done | bytes 2162720 | tf_op jit(solution)/shard_map/all_to_all | solution.py:461
  66.7 0.0 copy-done.10
  66.7 0.0 copy-start.5
  66.7 6.4 %group_balls.1 = (bf16[2048,512]{1,0:T(8,128)(2,1)S(1)}, bf16[2048,512]{1,0:T(8,128)(2,1)S(1)}, bf16[256,512]{1,0:T(8,128)(2,1)S(1)}, f32[16,128]{1,0:T(8,128)S(1)}) custom-call(bf16[16,528,128]{2,1,0:T(8,128)(2,1)S(1)} %all-to-all-done.arrived_ref, f32[1,512]{1,0:T(1,128)S(1)} %bitcast.33), custom_call_target="tpu_custom_call" | custom-call | flops 4294967296 | bytes 6291456 | tf_op jit(solution)/shard_map/group_balls/pallas_call | solution.py:186
  73.1 6.1 %collective-permute-start = (bf16[256,512]{1,0:T(8,128)(2,1)S(1)}, bf16[256,512]{1,0:T(8,128)(2,1)S(1)}, u32[]{:S(2)}, u32[]{:S(2)}) collective-permute-start(bf16[256,512]{1,0:T(8,128)(2,1)S(1)} %get-tuple-element.17), channel_id=1, source_target_pairs={{24,0},{26,2},{28,4},{30,6},{0,8},{2,10},{4,12},{6,14},{8,16},{10,... | collective-permute-start | bytes 786440 | tf_op jit(solution)/shard_map/ppermute | solution.py:426
  79.2 3.5 %collective-permute-start.1 = (bf16[256,512]{1,0:T(8,128)(2,1)S(1)}, bf16[256,512]{1,0:T(8,128)(2,1)S(1)}, u32[]{:S(2)}, u32[]{:S(2)}) collective-permute-start(bf16[256,512]{1,0:T(8,128)(2,1)S(1)} %get-tuple-element.17), channel_id=1, source_target_pairs={{26,0},{28,2},{30,4},{0,6},{2,8},{4,10},{6,12},{8,14},{10,16},{12,... | collective-permute-start | bytes 786440 | tf_op jit(solution)/shard_map/ppermute | solution.py:426
  82.7 0.0 collective-permute-start.2
  82.7 1.5 collective-permute-start.3
  84.2 0.0 collective-permute-start.4
  84.2 0.0 copy-done.5
  84.2 0.0 copy-done.6
  84.2 15.7 %local_attention.1 = (bf16[2048,512]{1,0:T(8,128)(2,1)S(1)}, f32[2048,512]{1,0:T(8,128)S(1)}, f32[2048,512]{1,0:T(8,128)S(1)}) custom-call(f32[1,512]{1,0:T(1,128)S(1)} %broadcast_in_dim_reshape.3.scale_ref, bf16[2048,512]{1,0:T(8,128)(2,1)S(1)} %get-tuple-element.18.normed_ref, bf16[512,512]{1,0:T(8,128)(2,1)S(1)} %copy-done.5, ...), custom_call_target="tpu_custom_call" | custom-call | flops 10737418240 | bytes 12582912 | tf_op jit(solution)/shard_map/local_attention/pallas_call | solution.py:282
  99.9 0.0 copy-start.13
  99.9 2.0 copy-done.13
  102.0 0.0 copy-start.12
  102.0 0.0 copy-start.2
  102.0 0.0 copy-start.3
  102.0 0.0 copy-start.4
  102.0 0.0 copy-start.7
  102.0 0.0 copy-start.8
  102.0 0.0 copy-start.11
  102.0 0.0 collective-permute-done
  102.0 3.5 %collective-permute-start.5 = (bf16[256,512]{1,0:T(8,128)(2,1)S(1)}, bf16[256,512]{1,0:T(8,128)(2,1)S(1)}, u32[]{:S(2)}, u32[]{:S(2)}) collective-permute-start(bf16[256,512]{1,0:T(8,128)(2,1)S(1)} %get-tuple-element.17), channel_id=1, source_target_pairs={{4,0},{6,2},{8,4},{10,6},{12,8},{14,10},{16,12},{18,14},{20,16},{2... | collective-permute-start | bytes 786440 | tf_op jit(solution)/shard_map/ppermute | solution.py:426
  105.5 0.0 collective-permute-done.1
  105.5 0.9 collective-permute-start.6
  106.4 0.0 collective-permute-done.2
  106.4 0.8 collective-permute-start.7
  107.3 0.0 collective-permute-done.3
  107.3 0.0 collective-permute-done.4
  107.4 2.8 %collective-permute-done.5 = bf16[256,512]{1,0:T(8,128)(2,1)S(1)} collective-permute-done((bf16[256,512]{1,0:T(8,128)(2,1)S(1)}, bf16[256,512]{1,0:T(8,128)(2,1)S(1)}, u32[]{:S(2)}, u32[]{:S(2)}) %collective-permute-start.5) | collective-permute-done | bytes 262176 | tf_op jit(solution)/shard_map/ppermute | solution.py:426
  110.2 6.3 %collective-permute-done.6 = bf16[256,512]{1,0:T(8,128)(2,1)S(1)} collective-permute-done((bf16[256,512]{1,0:T(8,128)(2,1)S(1)}, bf16[256,512]{1,0:T(8,128)(2,1)S(1)}, u32[]{:S(2)}, u32[]{:S(2)}) %collective-permute-start.6) | collective-permute-done | bytes 262176 | tf_op jit(solution)/shard_map/ppermute | solution.py:426
  116.5 4.9 %collective-permute-done.7 = bf16[256,512]{1,0:T(8,128)(2,1)S(1)} collective-permute-done((bf16[256,512]{1,0:T(8,128)(2,1)S(1)}, bf16[256,512]{1,0:T(8,128)(2,1)S(1)}, u32[]{:S(2)}, u32[]{:S(2)}) %collective-permute-start.7) | collective-permute-done | bytes 262176 | tf_op jit(solution)/shard_map/ppermute | solution.py:426
  121.4 0.0 copy-done.12
  121.4 0.0 copy-done.2
  121.4 0.0 copy-done.3
  121.4 0.0 copy-done.4
  121.4 0.0 copy-done.7
  121.4 0.0 copy-done.8
  121.4 0.0 copy-done.11
  121.5 18.4 %finish_balls.1.source_ref = bf16[2048,512]{1,0:T(8,128)(2,1)S(1)} custom-call(s32[32]{0:T(128)S(1)} %reshape.20.chosen_ref, bf16[72,32,512]{2,1,0:T(8,128)(2,1)S(1)} %bitcast.31, bf16[2048,512]{1,0:T(8,128)(2,1)S(1)} %get-tuple-element.19.query_ref, f32[2048,512]{1,0:T(8,128)} %copy-done.12, f32[2048,512]{1,0:T(8,128)} %copy-done.13, ...), custom_call_target="tpu_custom_call" | custom-call | flops 12884901888 | bytes 12582912 | tf_op jit(solution)/shard_map/finish_balls/pallas_call | solution.py:377
  139.8 5.2 %take_rows.2 = bf16[2048,512]{1,0:T(8,128)(2,1)S(1)} custom-call(f32[16,128]{1,0:T(8,128)S(1)} %get-tuple-element.16.ids_ref, bf16[2048,512]{1,0:T(8,128)(2,1)S(1)} %finish_balls.1.source_ref), custom_call_target="tpu_custom_call" | custom-call | flops 4294967296 | bytes 4194304 | tf_op jit(solution)/shard_map/take_rows/pallas_call | solution.py:409
  145.1 54.9 %all_to_all.10 = bf16[16,128,512]{2,1,0:T(8,128)(2,1)S(1)} all-to-all(bf16[16,128,512]{2,1,0:T(8,128)(2,1)S(1)} %bitcast.28), channel_id=1, replica_groups=mesh['pts'=16,'rep'=2] {'pts'}, dimensions={0} | all-to-all | bytes 4194304 | tf_op jit(solution)/shard_map/all_to_all | solution.py:461
  200.0 6.0 %take_rows.3 = bf16[2048,512]{1,0:T(8,128)(2,1)} custom-call(f32[16,128]{1,0:T(8,128)S(1)} %get-tuple-element.14.ids_ref, bf16[2048,512]{1,0:T(8,128)(2,1)S(1)} %bitcast.27), custom_call_target="tpu_custom_call" | custom-call | flops 4294967296 | bytes 4194304 | tf_op jit(solution)/shard_map/take_rows/pallas_call | solution.py:409
  (12 shorter events, 0.2 us)
Async XLA Ops:
  0.0 1.6 copy-start.1
  1.6 0.7 copy-start.9
  15.2 1.4 copy-start
  16.6 7.5 %copy-start.15 = (s32[8,4]{0,1:T(4,128)S(1)}, s32[8,4]{0,1:T(4,128)}, u32[]{:S(2)}) copy-start(s32[8,4]{0,1:T(4,128)} %param.17) | copy-start | bytes 388
  16.6 7.7 %copy-start.16 = (f32[16]{0:T(128)S(1)}, f32[16]{0:T(128)}, u32[]{:S(2)}) copy-start(f32[16]{0:T(128)} %param.24) | copy-start | bytes 196
  16.6 7.8 %copy-start.14 = (bf16[512,512]{1,0:T(8,128)(2,1)S(1)}, bf16[512,512]{1,0:T(8,128)(2,1)}, u32[]{:S(2)}) copy-start(bf16[512,512]{1,0:T(8,128)(2,1)} %param.20) | copy-start | bytes 1572868
  16.6 50.1 %copy-start.10 = (f32[512]{0:T(512)S(1)}, f32[512]{0:T(512)}, u32[]{:S(2)}) copy-start(f32[512]{0:T(512)} %param.18) | copy-start | bytes 6148
  16.6 50.1 %all-to-all-start = ((bf16[16,528,128]{2,1,0:T(8,128)(2,1)}), bf16[16,528,128]{2,1,0:T(8,128)(2,1)S(1)}, u32[]{:S(2)}, u32[]{:S(2)}) async-start(bf16[16,528,128]{2,1,0:T(8,128)(2,1)} %copy-done), calls=%async_computation | async-start | bytes 4325376 | tf_op jit(solution)/shard_map/all_to_all | solution.py:461
  66.7 17.5 %copy-start.5 = (bf16[512,512]{1,0:T(8,128)(2,1)S(1)}, bf16[512,512]{1,0:T(8,128)(2,1)}, u32[]{:S(2)}) copy-start(bf16[512,512]{1,0:T(8,128)(2,1)} %wq_ref.1) | copy-start | bytes 1572868
  66.7 17.5 %copy-start.6 = (bf16[512,512]{1,0:T(8,128)(2,1)S(1)}, bf16[512,512]{1,0:T(8,128)(2,1)}, u32[]{:S(2)}) copy-start(bf16[512,512]{1,0:T(8,128)(2,1)} %wv_ref.1) | copy-start | bytes 1572868
  73.1 28.9 %collective-permute-start = (bf16[256,512]{1,0:T(8,128)(2,1)S(1)}, bf16[256,512]{1,0:T(8,128)(2,1)S(1)}, u32[]{:S(2)}, u32[]{:S(2)}) collective-permute-start(bf16[256,512]{1,0:T(8,128)(2,1)S(1)} %get-tuple-element.17), channel_id=1, source_target_pairs={{24,0},{26,2},{28,4},{30,6},{0,8},{2,10},{4,12},{6,14},{8,16},{10,... | collective-permute-start | bytes 786440 | tf_op jit(solution)/shard_map/ppermute | solution.py:426
  79.2 26.2 %collective-permute-start.1 = (bf16[256,512]{1,0:T(8,128)(2,1)S(1)}, bf16[256,512]{1,0:T(8,128)(2,1)S(1)}, u32[]{:S(2)}, u32[]{:S(2)}) collective-permute-start(bf16[256,512]{1,0:T(8,128)(2,1)S(1)} %get-tuple-element.17), channel_id=1, source_target_pairs={{26,0},{28,2},{30,4},{0,6},{2,8},{4,10},{6,12},{8,14},{10,16},{12,... | collective-permute-start | bytes 786440 | tf_op jit(solution)/shard_map/ppermute | solution.py:426
  82.7 23.7 %collective-permute-start.2 = (bf16[256,512]{1,0:T(8,128)(2,1)S(1)}, bf16[256,512]{1,0:T(8,128)(2,1)S(1)}, u32[]{:S(2)}, u32[]{:S(2)}) collective-permute-start(bf16[256,512]{1,0:T(8,128)(2,1)S(1)} %get-tuple-element.17), channel_id=1, source_target_pairs={{28,0},{30,2},{0,4},{2,6},{4,8},{6,10},{8,12},{10,14},{12,16},{14,... | collective-permute-start | bytes 786440 | tf_op jit(solution)/shard_map/ppermute | solution.py:426
  82.7 24.6 %collective-permute-start.3 = (bf16[256,512]{1,0:T(8,128)(2,1)S(1)}, bf16[256,512]{1,0:T(8,128)(2,1)S(1)}, u32[]{:S(2)}, u32[]{:S(2)}) collective-permute-start(bf16[256,512]{1,0:T(8,128)(2,1)S(1)} %get-tuple-element.17), channel_id=1, source_target_pairs={{30,0},{0,2},{2,4},{4,6},{6,8},{8,10},{10,12},{12,14},{14,16},{16,... | collective-permute-start | bytes 786440 | tf_op jit(solution)/shard_map/ppermute | solution.py:426
  84.2 23.2 %collective-permute-start.4 = (bf16[256,512]{1,0:T(8,128)(2,1)S(1)}, bf16[256,512]{1,0:T(8,128)(2,1)S(1)}, u32[]{:S(2)}, u32[]{:S(2)}) collective-permute-start(bf16[256,512]{1,0:T(8,128)(2,1)S(1)} %get-tuple-element.17), channel_id=1, source_target_pairs={{2,0},{4,2},{6,4},{8,6},{10,8},{12,10},{14,12},{16,14},{18,16},{20... | collective-permute-start | bytes 786440 | tf_op jit(solution)/shard_map/ppermute | solution.py:426
  99.9 2.0 copy-start.13
  102.0 19.4 %copy-start.12 = (f32[2048,512]{1,0:T(8,128)}, f32[2048,512]{1,0:T(8,128)S(1)}, u32[]{:S(2)}) copy-start(f32[2048,512]{1,0:T(8,128)S(1)} %get-tuple-element.20.num_ref) | copy-start | bytes 12582916
  102.0 19.4 %copy-start.2 = (bf16[512,1024]{1,0:T(8,128)(2,1)S(1)}, bf16[512,1024]{1,0:T(8,128)(2,1)}, u32[]{:S(2)}) copy-start(bf16[512,1024]{1,0:T(8,128)(2,1)} %wg_ref.1) | copy-start | bytes 3145732
  102.0 19.5 %copy-start.3 = (bf16[512,1024]{1,0:T(8,128)(2,1)S(1)}, bf16[512,1024]{1,0:T(8,128)(2,1)}, u32[]{:S(2)}) copy-start(bf16[512,1024]{1,0:T(8,128)(2,1)} %wu_ref.1) | copy-start | bytes 3145732
  102.0 19.5 %copy-start.4 = (bf16[1024,512]{1,0:T(8,128)(2,1)S(1)}, bf16[1024,512]{1,0:T(8,128)(2,1)}, u32[]{:S(2)}) copy-start(bf16[1024,512]{1,0:T(8,128)(2,1)} %wd_ref.1) | copy-start | bytes 3145732
  102.0 19.5 %copy-start.7 = (bf16[512,512]{1,0:T(8,128)(2,1)S(1)}, bf16[512,512]{1,0:T(8,128)(2,1)}, u32[]{:S(2)}) copy-start(bf16[512,512]{1,0:T(8,128)(2,1)} %wpv_ref.1) | copy-start | bytes 1572868
  102.0 19.5 %copy-start.8 = (bf16[512,512]{1,0:T(8,128)(2,1)S(1)}, bf16[512,512]{1,0:T(8,128)(2,1)}, u32[]{:S(2)}) copy-start(bf16[512,512]{1,0:T(8,128)(2,1)} %wo_ref.1) | copy-start | bytes 1572868
  102.0 19.5 %copy-start.11 = (f32[512]{0:T(512)S(1)}, f32[512]{0:T(512)}, u32[]{:S(2)}) copy-start(f32[512]{0:T(512)} %param.26) | copy-start | bytes 6148
  102.0 8.1 %collective-permute-start.5 = (bf16[256,512]{1,0:T(8,128)(2,1)S(1)}, bf16[256,512]{1,0:T(8,128)(2,1)S(1)}, u32[]{:S(2)}, u32[]{:S(2)}) collective-permute-start(bf16[256,512]{1,0:T(8,128)(2,1)S(1)} %get-tuple-element.17), channel_id=1, source_target_pairs={{4,0},{6,2},{8,4},{10,6},{12,8},{14,10},{16,12},{18,14},{20,16},{2... | collective-permute-start | bytes 786440 | tf_op jit(solution)/shard_map/ppermute | solution.py:426
  105.5 11.0 %collective-permute-start.6 = (bf16[256,512]{1,0:T(8,128)(2,1)S(1)}, bf16[256,512]{1,0:T(8,128)(2,1)S(1)}, u32[]{:S(2)}, u32[]{:S(2)}) collective-permute-start(bf16[256,512]{1,0:T(8,128)(2,1)S(1)} %get-tuple-element.17), channel_id=1, source_target_pairs={{6,0},{8,2},{10,4},{12,6},{14,8},{16,10},{18,12},{20,14},{22,16},{... | collective-permute-start | bytes 786440 | tf_op jit(solution)/shard_map/ppermute | solution.py:426
  106.4 14.9 %collective-permute-start.7 = (bf16[256,512]{1,0:T(8,128)(2,1)S(1)}, bf16[256,512]{1,0:T(8,128)(2,1)S(1)}, u32[]{:S(2)}, u32[]{:S(2)}) collective-permute-start(bf16[256,512]{1,0:T(8,128)(2,1)S(1)} %get-tuple-element.17), channel_id=1, source_target_pairs={{8,0},{10,2},{12,4},{14,6},{16,8},{18,10},{20,12},{22,14},{24,16},... | collective-permute-start | bytes 786440 | tf_op jit(solution)/shard_map/ppermute | solution.py:426

commit v3 on v2

--- a/solution.py
+++ b/solution.py
@@ -11,7 +11,7 @@
 BALL = 256
 POOL = 8
 OWNERS = 4
-REACH = 4
+GROUP = 4
 LANES = 128
 TILE = 512
 DEPTH = 512
@@ -20,11 +20,10 @@
 LOG2E = math.log2(math.e)
 F32 = jnp.float32
 BF16 = jnp.bfloat16
-VMEM_BYTES = 40 * 1024 * 1024
-
-
-def params(**kwargs):
-    return pltpu.CompilerParams(vmem_limit_bytes=VMEM_BYTES, **kwargs)
+
+
+def params(mebibytes=40):
+    return pltpu.CompilerParams(vmem_limit_bytes=mebibytes * 1024 * 1024)
 
 
 def dot(a, b):
@@ -72,33 +71,46 @@
     return lambda t: jnp.where(wanted - float(t * LANES) == lane, 1.0, 0.0).astype(BF16)
 
 
-def send_kernel(send_each, me_ref, index_ref, points_ref, out_ref, rank_ref, col, aux):
-    rows_dev, width = points_ref.shape
+def send_kernel(send_each, me_ref, index_ref, points_ref, out_ref, slot_ref, held, aux, arrivals):
+    rows_dev, width = held.shape
     tiles = rows_dev // LANES
     chunks = width // LANES
     per_tile = LANES // send_each
+    peers = rows_dev // send_each
     step = pl.program_id(0)
+    pieces = [
+        pltpu.make_async_copy(points_ref.at[pl.ds(k, DEPTH)], held.at[pl.ds(k, DEPTH)], arrivals.at[k // DEPTH])
+        for k in range(0, rows_dev, DEPTH)
+    ]
 
     @pl.when(step == 0)
     def _():
+        for piece in pieces:
+            piece.start()
+        index = index_ref[...].astype(F32)
+        dest = jnp.floor(index * (1.0 / rows_dev))
+        local = index - dest * rows_dev
+        high = jnp.floor(local * (1.0 / LOW))
+        low = local - high * LOW
+        row = lax.broadcasted_iota(jnp.int32, (LANES, LANES), 0)
         for t in range(tiles):
-            col[t * LANES : (t + 1) * LANES, :] = column_of(index_ref[t : t + 1, :].astype(F32))
-
-        def rank_tile(t, carry):
-            row = index_ref[pl.ds(t, 1), :].astype(F32)
-            below = jnp.where(col[...] < row, 1.0, 0.0)
-            rank_ref[pl.ds(t, 1), :] = jnp.sum(below, axis=0, keepdims=True)
-            return carry
-
-        lax.fori_loop(0, tiles, rank_tile, 0)
-        local = lax.rem(col[...].astype(jnp.int32), rows_dev)
-        lane = lax.broadcasted_iota(jnp.int32, (rows_dev, LANES), 1)
-        high = lax.div(local, LOW)
-        low = lax.rem(local, LOW)
-        aux[...] = jnp.where(lane == 0, high, jnp.where(lane == 1, low, 0)).astype(F32).astype(BF16)
-
-    tile = by_lane_ids(rank_ref, step * TILE, TILE)
-    rows = picked_rows(tile, TILE, points_ref).astype(BF16)
+            pair = jnp.where(row == 0, high[t : t + 1, :], jnp.where(row == 1, low[t : t + 1, :], 0.0))
+            aux[t * LANES : (t + 1) * LANES, :] = pair.T.astype(BF16)
+        peer = lax.broadcasted_iota(jnp.int32, (peers, LANES), 0).astype(F32)
+        member = [jnp.where(dest[t : t + 1, :] == peer, 1.0, 0.0) for t in range(tiles)]
+        lane = lax.broadcasted_iota(jnp.int32, (LANES, LANES), 1)
+        up_to = jnp.where(row <= lane, 1.0, 0.0).astype(BF16)
+        counts = dot(jnp.concatenate(member, axis=0).astype(BF16), up_to)
+        before = peer[:, 0:1] * send_each - 1.0
+        for t in range(tiles):
+            count = counts[t * peers : (t + 1) * peers, :]
+            slot_ref[t : t + 1, :] = jnp.sum(member[t] * (count + before), axis=0, keepdims=True)
+            before = before + count[:, LANES - 1 :]
+        for piece in pieces:
+            piece.wait()
+
+    tile = by_lane_ids(slot_ref, step * TILE, TILE)
+    rows = picked_rows(tile, TILE, held).astype(BF16)
     ids = picked_rows(tile, TILE, aux)
     for u in range(TILE // LANES):
         both = ids[u * LANES : (u + 1) * LANES, :].T[0:16, :]
@@ -127,85 +139,125 @@
         grid_spec=pltpu.PrefetchScalarGridSpec(
             num_scalar_prefetch=1,
             grid=(rows_dev // TILE,),
-            in_specs=[whole((tiles, LANES)), whole((rows_dev, width))],
+            in_specs=[whole((tiles, LANES)), pl.BlockSpec(memory_space=pl.ANY)],
             out_specs=[
                 pl.BlockSpec((TILE // send_each, payload, LANES), lambda i, *_: (i, 0, 0)),
                 whole((tiles, LANES)),
             ],
             scratch_shapes=[
-                pltpu.VMEM((rows_dev, LANES), F32),
+                pltpu.VMEM((rows_dev, width), BF16),
                 pltpu.VMEM((rows_dev, LANES), BF16),
+                pltpu.SemaphoreType.DMA((rows_dev // DEPTH,)),
             ],
         ),
         out_shape=[
             jax.ShapeDtypeStruct((peers, payload, LANES), BF16),
             jax.ShapeDtypeStruct((tiles, LANES), F32),
         ],
+        compiler_params=params(60),
+        cost_estimate=pl.CostEstimate(
+            flops=2 * rows_dev * rows_dev * (width + LANES), bytes_accessed=4 * rows_dev * width, transcendentals=0
+        ),
+        name="send_order",
+    )(me.reshape(1), index_tiles, points)
+
+
+def normed_rows(rows32, gain):
+    mean_square = jnp.mean(rows32 * rows32, axis=-1, keepdims=True)
+    return (rows32 * lax.rsqrt(mean_square + 1e-05) * gain).astype(BF16)
+
+
+def pool_kernel(arrived_ref, gain_ref, source_ref, ids_ref, pooled_ref, ids, total):
+    peers = arrived_ref.shape[0]
+    rows, width = source_ref.shape
+    chunks = width // LANES
+    send_each = rows // peers
+    per_tile = LANES // send_each
+    step = pl.program_id(0)
+
+    @pl.when(step == 0)
+    def _():
+        total[...] = jnp.zeros_like(total)
+
+    for t in range(rows // LANES):
+        row = jnp.zeros((1, LANES), F32)
+        for p in range(t * per_tile, (t + 1) * per_tile):
+            both = arrived_ref[p, chunks * send_each :, :].astype(F32)
+            row = row + both[0:1, :] * LOW + both[1:2, :]
+        ids[t : t + 1, :] = row
+        ids_ref[pl.ds(step * (rows // LANES) + t, 1), :] = row
+    for p in range(peers):
+        for c in range(chunks):
+            source_ref[p * send_each : (p + 1) * send_each, c * LANES : (c + 1) * LANES] = arrived_ref[
+                p, c * send_each : (c + 1) * send_each, :
+            ]
+    normed = normed_rows(source_ref[...].astype(F32), gain_ref[...])
+    pools = total.shape[0]
+    pool = lax.broadcasted_iota(jnp.int32, (pools, LANES), 0).astype(F32)
+    pick = jnp.concatenate(
+        [
+            jnp.where(jnp.floor(ids[t : t + 1, :] * (1.0 / POOL)) == pool, 1.0 / POOL, 0.0).astype(BF16)
+            for t in range(rows // LANES)
+        ],
+        axis=1,
+    )
+    total[...] += dot(pick, normed)
+
+    @pl.when(step == pl.num_programs(0) - 1)
+    def _():
+        pooled_ref[...] = total[...].astype(BF16)
+
+
+def pool(arrived, gain, rows_dev):
+    width = gain.shape[1]
+    tiles = rows_dev // LANES
+    peers, payload, _ = arrived.shape
+    steps = rows_dev // TILE
+    pooled = (rows_dev // POOL, width)
+    return pl.pallas_call(
+        pool_kernel,
+        grid=(steps,),
+        in_specs=[
+            pl.BlockSpec((peers // steps, payload, LANES), lambda i: (i, 0, 0)),
+            whole((1, width)),
+        ],
+        out_specs=[row_blocks(TILE, width), whole((tiles, LANES)), whole(pooled)],
+        out_shape=[
+            jax.ShapeDtypeStruct((rows_dev, width), BF16),
+            jax.ShapeDtypeStruct((tiles, LANES), F32),
+            jax.ShapeDtypeStruct(pooled, BF16),
+        ],
+        scratch_shapes=[pltpu.VMEM((TILE // LANES, LANES), F32), pltpu.VMEM(pooled, F32)],
         compiler_params=params(),
         cost_estimate=pl.CostEstimate(
-            flops=2 * rows_dev * rows_dev * (width + LANES), bytes_accessed=4 * rows_dev * width, transcendentals=0
-        ),
-        name="send_order",
-    )(me.reshape(1), index_tiles, points)
-
-
-def group_kernel(arrived_ref, gain_ref, grouped_ref, normed_ref, pooled_ref, ids_ref, source):
-    peers = arrived_ref.shape[0]
+            flops=rows_dev * rows_dev * width // 4, bytes_accessed=4 * rows_dev * width, transcendentals=0
+        ),
+        name="pool_arrived",
+    )(arrived, gain)
+
+
+def group_kernel(ids_ref, source_ref, gain_ref, grouped_ref, normed_ref):
+    tile = by_lane_ids(ids_ref, pl.program_id(0) * TILE, TILE)
+    grouped = picked_rows(tile, TILE, source_ref)
+    grouped_ref[...] = grouped.astype(BF16)
+    normed_ref[...] = normed_rows(grouped, gain_ref[...])
+
+
+def group(ids, source, gain):
     rows_dev, width = source.shape
-    chunks = width // LANES
-    send_each = rows_dev // peers
-    per_tile = LANES // send_each
-
-    @pl.when(pl.program_id(0) == 0)
-    def _():
-        for t in range(rows_dev // LANES):
-            row = jnp.zeros((1, LANES), F32)
-            for p in range(t * per_tile, (t + 1) * per_tile):
-                both = arrived_ref[p, chunks * send_each :, :].astype(F32)
-                row = row + both[0:1, :] * LOW + both[1:2, :]
-            ids_ref[t : t + 1, :] = row
-        for p in range(peers):
-            for c in range(chunks):
-                source[p * send_each : (p + 1) * send_each, c * LANES : (c + 1) * LANES] = arrived_ref[
-                    p, c * send_each : (c + 1) * send_each, :
-                ]
-
-    tile = by_lane_ids(ids_ref, pl.program_id(0) * TILE, TILE)
-    grouped = picked_rows(tile, TILE, source)
-    grouped_ref[...] = grouped.astype(BF16)
-    mean_square = jnp.mean(grouped * grouped, axis=-1, keepdims=True)
-    normed = (grouped * lax.rsqrt(mean_square + 1e-05) * gain_ref[...]).astype(BF16)
-    normed_ref[...] = normed
-    mean_of = block_matrix(TILE // POOL, 1, TILE, POOL, 1.0 / POOL)
-    pooled_ref[...] = dot(mean_of, normed).astype(BF16)
-
-
-def group(arrived, gain, rows_dev):
-    width = gain.shape[1]
-    tiles = rows_dev // LANES
+    rows = row_blocks(TILE, width)
     return pl.pallas_call(
         group_kernel,
         grid=(rows_dev // TILE,),
-        in_specs=[whole(arrived.shape), whole((1, width))],
-        out_specs=[
-            row_blocks(TILE, width),
-            row_blocks(TILE, width),
-            row_blocks(TILE // POOL, width),
-            whole((tiles, LANES)),
-        ],
-        out_shape=[
-            jax.ShapeDtypeStruct((rows_dev, width), BF16),
-            jax.ShapeDtypeStruct((rows_dev, width), BF16),
-            jax.ShapeDtypeStruct((rows_dev // POOL, width), BF16),
-            jax.ShapeDtypeStruct((tiles, LANES), F32),
-        ],
-        scratch_shapes=[pltpu.VMEM((rows_dev, width), BF16)],
+        in_specs=[whole(ids.shape), whole(source.shape), whole((1, width))],
+        out_specs=[rows, rows],
+        out_shape=[jax.ShapeDtypeStruct((rows_dev, width), BF16)] * 2,
         compiler_params=params(),
         cost_estimate=pl.CostEstimate(
             flops=2 * rows_dev * rows_dev * width, bytes_accessed=6 * rows_dev * width, transcendentals=0
         ),
         name="group_balls",
-    )(arrived, gain)
+    )(ids, source, gain)
 
 
 def block_matrix(rows, row_step, cols, col_step, value):
@@ -240,7 +292,8 @@
             ref[g, j * count : (j + 1) * count, :LANES] = jnp.where(head == j, lanes, jnp.zeros((), BF16))
 
 
-def local_kernel(head_size, scale_ref, normed_ref, wq_ref, wk_ref, wv_ref, query_ref, num_ref, den_ref, mean_of, keys, values, weights):
+def local_kernel(head_size, scale_ref, normed_ref, wq_ref, wk_ref, wv_ref, *rest):
+    query_ref, num_ref, den_ref, mean_of, keys, values, weights = rest[-7:]
     width = normed_ref.shape[1]
     half = mean_of.shape[0]
 
@@ -274,16 +327,19 @@
         den_ref[:, g * LANES : (g + 1) * LANES] = both[:, LANES:]
 
 
-def local_attention(normed, wq, wk, wv, scale, head_size):
+def local_attention(part, parts, normed, wq, wk, wv, scale, head_size, earlier=()):
     rows_dev, width = normed.shape
     square = whole((width, width))
     groups = width // LANES
     spread = LANES // head_size * BALL
+    steps = rows_dev // BALL // parts
+    rows = pl.BlockSpec((BALL, width), lambda i: (part * steps + i, 0))
     return pl.pallas_call(
         functools.partial(local_kernel, head_size),
-        grid=(rows_dev // BALL,),
-        in_specs=[whole((1, width)), row_blocks(BALL, width), square, square, square],
-        out_specs=[row_blocks(BALL, width)] * 3,
+        grid=(steps,),
+        in_specs=[whole((1, width)), rows, square, square, square]
+        + [pl.BlockSpec(memory_space=pl.ANY)] * len(earlier),
+        out_specs=[rows] * 3,
         out_shape=[
             jax.ShapeDtypeStruct((rows_dev, width), BF16),
             jax.ShapeDtypeStruct((rows_dev, width), F32),
@@ -295,12 +351,13 @@
             pltpu.VMEM((groups, spread, 2 * LANES), BF16),
             pltpu.VMEM((groups, BALL, spread), BF16),
         ],
+        input_output_aliases={5 + k: k for k in range(len(earlier))},
         compiler_params=params(),
         cost_estimate=pl.CostEstimate(
-            flops=20 * rows_dev * width * width, bytes_accessed=12 * rows_dev * width, transcendentals=0
+            flops=20 * rows_dev * width * width // parts, bytes_accessed=12 * rows_dev * width // parts, transcendentals=0
         ),
         name="local_attention",
-    )(scale, normed, wq, wk, wv)
+    )(scale, normed, wq, wk, wv, *earlier)
 
 
 def finish_kernel(
@@ -358,8 +415,7 @@
     projected = dot(attended[...], wo_ref[...])
     residual = (grouped_ref[...].astype(F32) + projected).astype(BF16)
     rows32 = residual.astype(F32)
-    mean_square = jnp.mean(rows32 * rows32, axis=-1, keepdims=True)
-    ffn = (rows32 * lax.rsqrt(mean_square + 1e-05) * gain_ref[...]).astype(BF16)
+    ffn = normed_rows(rows32, gain_ref[...])
     gate = dot(ffn, wg_ref[...])
     up = dot(ffn, wu_ref[...])
     hidden = (0.5 * gate * (1.0 + jnp.tanh(0.5 * gate)) * up).astype(BF16)
@@ -420,16 +476,32 @@
     )(ids, source)
 
 
-def from_behind(block, axis, distance):
-    devices = range(lax.axis_size(axis))
-    route = [((i - distance) % len(devices), i) for i in devices]
-    return lax.ppermute(block, axis, route)
-
-
-def fetch_blocks(payload):
-    return jnp.stack(
-        [payload if k == 0 else from_behind(payload, "pts", k) for k in range(REACH, -REACH - 1, -1)]
-    )
+def route(block, target):
+    devices = range(lax.axis_size("pts"))
+    return lax.ppermute(block, "pts", [(i, target(i) % len(devices)) for i in devices])
+
+
+def to_mate(block, mate):
+    return route(block, lambda i: i ^ mate)
+
+
+def first_stage(pooled):
+    below = route(pooled, lambda i: i + GROUP)
+    above = route(pooled, lambda i: i - GROUP)
+    return below, above, [to_mate(pooled, mate) for mate in range(1, GROUP)]
+
+
+def second_stage(below, above, place):
+    return [
+        to_mate(jnp.where(place > (place ^ mate), below, above), mate) for mate in range(1, GROUP)
+    ]
+
+
+def block_slots(owner, me, peers):
+    mate = (owner % GROUP) ^ (me % GROUP)
+    ahead = jnp.mod(owner // GROUP - me // GROUP, peers // GROUP)
+    outside = jnp.where(mate == 0, jnp.where(ahead == 1, GROUP + 1, GROUP), GROUP + 1 + mate)
+    return jnp.where(ahead == 0, mate, outside)
 
 
 def on_device(
@@ -460,14 +532,28 @@
     def swap(array):
         return lax.all_to_all(array, "pts", split_axis=0, concat_axis=0, tiled=True)
 
-    outgoing, rank = send_order(points, point_row_index.reshape(rows_dev // LANES, LANES), me, peers)
-    grouped, normed, pooled, ids = group(swap(outgoing), attention_norm_gain[None], rows_dev)
-    candidates = fetch_blocks(pooled).reshape((2 * REACH + 1) * blocks_dev, comp, width)
-    owner = neighbour_ball_list // blocks_dev
-    offset = jnp.mod(owner - me + REACH, peers)
-    chosen = (offset * blocks_dev + neighbour_ball_list % blocks_dev).reshape(-1)
+    outgoing, slot = send_order(points, point_row_index.reshape(rows_dev // LANES, LANES), me, peers)
+    source, ids, pooled = pool(swap(outgoing), attention_norm_gain[None], rows_dev)
+    below, above, mates = first_stage(pooled)
+    grouped, normed = group(ids, source, attention_norm_gain[None])
     scale = jnp.repeat(head_score_scale * (LOG2E / head_size), head_size)[None]
-    query, num, den = local_attention(normed, query_weight, key_weight.T, value_weight, scale, head_size)
+    attend = functools.partial(
+        local_attention,
+        normed=normed,
+        wq=query_weight,
+        wk=key_weight.T,
+        wv=value_weight,
+        scale=scale,
+        head_size=head_size,
+    )
+    part = attend(0, 2)
+    below, above, part = lax.optimization_barrier((below, above, part))
+    more = second_stage(below, above, me % GROUP)
+    query, num, den = attend(1, 2, earlier=part)
+    candidates = jnp.stack([pooled, *mates, below, above, *more])
+    candidates = candidates.reshape(candidates.shape[0] * blocks_dev, comp, width)
+    slots = block_slots(neighbour_ball_list // blocks_dev, me, peers)
+    chosen = (slots * blocks_dev + neighbour_ball_list % blocks_dev).reshape(-1)
     ball_out = finish(
         chosen,
         candidates,
@@ -486,7 +572,7 @@
     )
     returning = take_rows(ids, ball_out).reshape(peers, send_each, width)
     came_back = swap(returning).reshape(rows_dev, width)
-    return take_rows(rank, came_back)
+    return take_rows(slot, came_back)
 
 
 def solution(mesh):

time: 206 us -> 193 us (0.937)
  waiting for transfers between devices: 54.7 us -> 49 us
  blocking collectives: 54.9 us -> 51.3 us
  starting transfers between devices: 23.7 us -> 20.2 us
    ppermute x8, waiting for transfers between devices: 14 us -> 8.2 us  [route(): lax.ppermute(block, 'pts', [(i, target(i) % len(devices)) for i in devices])]
    all_to_all x1, blocking collectives: 54.9 us -> 51.3 us  [swap(): return lax.all_to_all(array, 'pts', split_axis=0, concat_axis=0, tiled=True)]
    ppermute x8, starting transfers between devices: 16.2 us -> 12.7 us  [route(): lax.ppermute(block, 'pts', [(i, target(i) % len(devices)) for i in devices])]
    pallas_call x1, Pallas kernels: 12.9 us -> 10.4 us  [send_order(): pl.pallas_call(functools.partial(send_kernel, send_each), grid_spec=pltpu...]
    pallas_call x2 -> x4, Pallas kernels: 22.2 us -> 23.6 us  [the longest x2 16 us: local_attention(): pl.pallas_call(functools.partial(local_kernel, head_size), grid=(steps,),...]
    unnamed x44 -> x48, local copies, waits for them, and re-layouts: 7.36 us -> 7.98 us
  transfers between devices with their start and end apart: 9 -> 9, of which waited for: 4 -> 2; matrix products, arithmetic and copies ran while one was open for 1% -> 1% of each run, Pallas kernels for 8% -> 11%
where the time goes in v3:
time: 193 us
  Pallas kernels  63.3 us (33%)
  blocking collectives  51.3 us (27%)
  waiting for transfers between devices  49 us (25%)
  starting transfers between devices  20.2 us (10%)
  local copies, waits for them, and re-layouts  8.31 us (4%)
    all_to_all x1, blocking collectives, swap(): return lax.all_to_all(array, 'pts', split_axis=0, concat_axis=0, tiled=True)  51.3 us
    all_to_all x1, waiting for transfers between devices, swap(): return lax.all_to_all(array, 'pts', split_axis=0, concat_axis=0, tiled=True)  40.7 us
    pallas_call x1, Pallas kernels, finish(): pl.pallas_call(functools.partial(finish_kernel, head_size), grid_spec=plt...  18.1 us
    pallas_call x2, Pallas kernels, local_attention(): pl.pallas_call(functools.partial(local_kernel, head_size), grid=(steps,),...  16 us
    ppermute x8, starting transfers between devices, route(): lax.ppermute(block, 'pts', [(i, target(i) % len(devices)) for i in devices])  12.7 us
    pallas_call x2, Pallas kernels, take_rows(): pl.pallas_call(rows_kernel, grid=(rows_dev // TILE,), in_specs=[whole(ids...  11.2 us
    pallas_call x1, Pallas kernels, send_order(): pl.pallas_call(functools.partial(send_kernel, send_each), grid_spec=pltpu...  10.4 us
    ppermute x8, waiting for transfers between devices, route(): lax.ppermute(block, 'pts', [(i, target(i) % len(devices)) for i in devices])  8.2 us
  transfers between devices with their start and end apart: 9, of which 2 were waited for; matrix products, arithmetic and copies ran while one was open for 1% of the time, Pallas kernels for 11%

profile of v3, /device:TPU:1, one launch (start us, length us, event | category | flops | bytes accessed | tf_op | source)
XLA Modules:
  0.0 192.5 jit_solution(10526978105404605360)
XLA Ops:
  0.0 10.4 %send_order.1 = (bf16[16,528,128]{2,1,0:T(8,128)(2,1)}, f32[16,128]{1,0:T(8,128)}) custom-call(s32[1]{0:T(128)} %bitcast.me_ref, s32[16,128]{1,0:T(8,128)} %bitcast.36, bf16[2048,512]{1,0:T(8,128)(2,1)} %points_ref.1), custom_call_target="tpu_custom_call" | custom-call | flops 5368709120 | bytes 4194304 | tf_op jit(solution)/shard_map/send_order/pallas_call | solution.py:137
  10.4 0.0 copy-start.16
  10.4 0.0 copy-start.18
  10.5 0.0 copy-start.17
  10.5 0.0 copy-start
  10.5 7.5 %all-to-all-start = ((bf16[16,528,128]{2,1,0:T(8,128)(2,1)}), bf16[16,528,128]{2,1,0:T(8,128)(2,1)S(1)}, u32[]{:S(2)}, u32[]{:S(2)}) async-start(bf16[16,528,128]{2,1,0:T(8,128)(2,1)} %get-tuple-element.24), calls=%async_computation | async-start | bytes 4325376 | tf_op jit(solution)/shard_map/all_to_all | solution.py:533
  18.0 0.0 copy-done.16
  18.0 0.2 copy.23
  18.2 0.0 copy-done.18
  18.2 0.1 broadcast_in_dim.18
  18.3 0.1 broadcast_in_dim_reshape.3.scale_ref
  18.3 0.0 copy-done.17
  18.4 0.1 copy.22
  18.5 0.1 reshape.20.chosen_ref
  18.5 1.3 copy.24
  19.8 40.7 %all-to-all-done.arrived_ref = bf16[16,528,128]{2,1,0:T(8,128)(2,1)S(1)} async-done(((bf16[16,528,128]{2,1,0:T(8,128)(2,1)}), bf16[16,528,128]{2,1,0:T(8,128)(2,1)S(1)}, u32[]{:S(2)}, u32[]{:S(2)}) %all-to-all-start) | async-done | bytes 2162720 | tf_op jit(solution)/shard_map/all_to_all | solution.py:533
  60.6 0.0 copy-done
  60.6 2.1 %pool_arrived.1 = (bf16[2048,512]{1,0:T(8,128)(2,1)S(1)}, f32[16,128]{1,0:T(8,128)S(1)}, bf16[256,512]{1,0:T(8,128)(2,1)S(1)}) custom-call(bf16[16,528,128]{2,1,0:T(8,128)(2,1)S(1)} %all-to-all-done.arrived_ref, f32[1,512]{1,0:T(1,128)S(1)} %bitcast.33), custom_call_target="tpu_custom_call" | custom-call | flops 536870912 | bytes 4194304 | tf_op jit(solution)/shard_map/pool_arrived/pallas_call | solution.py:217
  62.7 6.1 %collective-permute-start.3 = (bf16[256,512]{1,0:T(8,128)(2,1)S(1)}, bf16[256,512]{1,0:T(8,128)(2,1)S(1)}, u32[]{:S(2)}, u32[]{:S(2)}) collective-permute-start(bf16[256,512]{1,0:T(8,128)(2,1)S(1)} %get-tuple-element.26), channel_id=1, source_target_pairs={{0,8},{2,10},{4,12},{6,14},{8,16},{10,18},{12,20},{14,22},{16,24},... | collective-permute-start | bytes 786440 | tf_op jit(solution)/shard_map/ppermute | solution.py:481
  68.8 0.2 collective-permute-start.4
  69.0 0.4 collective-permute-start
  69.4 3.7 %collective-permute-start.1 = (bf16[256,512]{1,0:T(8,128)(2,1)S(1)}, bf16[256,512]{1,0:T(8,128)(2,1)S(1)}, u32[]{:S(2)}, u32[]{:S(2)}) collective-permute-start(bf16[256,512]{1,0:T(8,128)(2,1)S(1)} %get-tuple-element.26), channel_id=1, source_target_pairs={{0,4},{2,6},{4,0},{6,2},{8,12},{10,14},{12,8},{14,10},{16,20},{18,... | collective-permute-start | bytes 786440 | tf_op jit(solution)/shard_map/ppermute | solution.py:481
  73.1 0.0 collective-permute-start.2
  73.1 5.5 %group_balls.1 = (bf16[2048,512]{1,0:T(8,128)(2,1)S(1)}, bf16[2048,512]{1,0:T(8,128)(2,1)S(1)}) custom-call(f32[16,128]{1,0:T(8,128)S(1)} %get-tuple-element.25.ids_ref, bf16[2048,512]{1,0:T(8,128)(2,1)S(1)} %get-tuple-element.27.source_ref, f32[1,512]{1,0:T(1,128)S(1)} %bitcast.34), custom_call_target="tpu_custom_call" | custom-call | flops 4294967296 | bytes 6291456 | tf_op jit(solution)/shard_map/group_balls/pallas_call | solution.py:249
  78.6 0.0 copy-start.13
  78.6 1.4 copy-done.13
  80.0 0.0 copy-done.4
  80.0 0.0 copy-done.5
  80.0 8.0 %local_attention.2 = (bf16[2048,512]{1,0:T(8,128)(2,1)S(1)}, f32[2048,512]{1,0:T(8,128)S(1)}, f32[2048,512]{1,0:T(8,128)S(1)}) custom-call(f32[1,512]{1,0:T(1,128)S(1)} %broadcast_in_dim_reshape.3.scale_ref, bf16[2048,512]{1,0:T(8,128)(2,1)S(1)} %get-tuple-element.28.normed_ref, bf16[512,512]{1,0:T(8,128)(2,1)S(1)} %copy-done.4, ...), custom_call_target="tpu_custom_call" | custom-call | flops 5368709120 | bytes 6291456 | tf_op jit(solution)/shard_map/local_attention/pallas_call | solution.py:337
  88.0 0.0 collective-permute-done.3
  88.0 0.0 collective-permute-done.4
  88.0 0.1 broadcast_select_fusion
  88.1 0.5 collective-permute-start.5
  88.6 1.4 collective-permute-start.6
  90.0 8.0 %local_attention.3 = (bf16[2048,512]{1,0:T(8,128)(2,1)S(1)}, f32[2048,512]{1,0:T(8,128)S(1)}, f32[2048,512]{1,0:T(8,128)S(1)}) custom-call(f32[1,512]{1,0:T(1,128)S(1)} %broadcast_in_dim_reshape.3.scale_ref, bf16[2048,512]{1,0:T(8,128)(2,1)S(1)} %get-tuple-element.28.normed_ref, ...), custom_call_target="tpu_custom_call", output_to_operand_aliasing={{0}: (5, {}), {1}: (6, {}), {2}: (7, {})} | custom-call | flops 5368709120 | bytes 6291456 | tf_op jit(solution)/shard_map/local_attention/pallas_call | solution.py:337
  98.0 0.0 copy-start.10
  98.0 2.0 %copy-done.10 = f32[2048,512]{1,0:T(8,128)} copy-done((f32[2048,512]{1,0:T(8,128)}, f32[2048,512]{1,0:T(8,128)S(1)}, u32[]{:S(2)}) %copy-start.10) | copy-done | bytes 4194328
  100.0 1.3 copy-done.11
  101.4 0.0 copy-start.6
  101.4 0.0 copy-start.7
  101.4 0.0 copy-start.8
  101.4 0.0 collective-permute-done
  101.4 0.3 collective-permute-start.7
  101.8 0.0 collective-permute-done.1
  101.8 0.0 collective-permute-done.2
  101.9 0.0 collective-permute-done.5
  101.9 0.0 collective-permute-done.6
  102.0 8.2 %collective-permute-done.7 = bf16[256,512]{1,0:T(8,128)(2,1)S(1)} collective-permute-done((bf16[256,512]{1,0:T(8,128)(2,1)S(1)}, bf16[256,512]{1,0:T(8,128)(2,1)S(1)}, u32[]{:S(2)}, u32[]{:S(2)}) %collective-permute-start.7) | collective-permute-done | bytes 262176 | tf_op jit(solution)/shard_map/ppermute | solution.py:481
  110.2 0.0 copy-done.9
  110.2 0.0 copy-done.14
  110.2 0.0 copy-done.1
  110.2 0.0 copy-done.2
  110.2 0.0 copy-done.3
  110.2 0.0 copy-done.6
  110.2 0.0 copy-done.7
  110.3 0.0 copy-done.8
  110.3 0.0 copy-start.12
  110.3 1.6 copy-done.12
  111.9 18.1 %finish_balls.1.source_ref = bf16[2048,512]{1,0:T(8,128)(2,1)S(1)} custom-call(s32[32]{0:T(128)S(1)} %reshape.20.chosen_ref, bf16[72,32,512]{2,1,0:T(8,128)(2,1)S(1)} %bitcast.32, bf16[2048,512]{1,0:T(8,128)(2,1)S(1)} %copy-done.12, f32[2048,512]{1,0:T(8,128)} %copy-done.9, f32[2048,512]{1,0:T(8,128)} %copy-done.10, bf16[2048,512]{1,0:T(8,128)(2,1)S(1)} %copy-done.14, ...), custom_call_target="tpu_custom_call" | custom-call | flops 12884901888 | bytes 12582912 | tf_op jit(solution)/shard_map/finish_balls/pallas_call | solution.py:433
  130.0 5.2 %take_rows.2 = bf16[2048,512]{1,0:T(8,128)(2,1)S(1)} custom-call(f32[16,128]{1,0:T(8,128)S(1)} %get-tuple-element.25.ids_ref, bf16[2048,512]{1,0:T(8,128)(2,1)S(1)} %finish_balls.1.source_ref), custom_call_target="tpu_custom_call" | custom-call | flops 4294967296 | bytes 4194304 | tf_op jit(solution)/shard_map/take_rows/pallas_call | solution.py:465
  135.2 0.0 copy-start.15
  135.2 51.3 %all_to_all.10 = bf16[16,128,512]{2,1,0:T(8,128)(2,1)S(1)} all-to-all(bf16[16,128,512]{2,1,0:T(8,128)(2,1)S(1)} %bitcast.28), channel_id=1, replica_groups=mesh['pts'=16,'rep'=2] {'pts'}, dimensions={0} | all-to-all | bytes 4194304 | tf_op jit(solution)/shard_map/all_to_all | solution.py:533
  186.5 0.0 copy-done.15
  186.5 6.0 %take_rows.3 = bf16[2048,512]{1,0:T(8,128)(2,1)} custom-call(f32[16,128]{1,0:T(8,128)S(1)} %copy-done.15, bf16[2048,512]{1,0:T(8,128)(2,1)S(1)} %bitcast.27), custom_call_target="tpu_custom_call" | custom-call | flops 4294967296 | bytes 4194304 | tf_op jit(solution)/shard_map/take_rows/pallas_call | solution.py:465
  (19 shorter events, 0.2 us)
Async XLA Ops:
  10.4 7.5 %copy-start.16 = (bf16[512,512]{1,0:T(8,128)(2,1)S(1)}, bf16[512,512]{1,0:T(8,128)(2,1)}, u32[]{:S(2)}) copy-start(bf16[512,512]{1,0:T(8,128)(2,1)} %param.20) | copy-start | bytes 1572868
  10.4 7.7 %copy-start.18 = (f32[16]{0:T(128)S(1)}, f32[16]{0:T(128)}, u32[]{:S(2)}) copy-start(f32[16]{0:T(128)} %param.24) | copy-start | bytes 196
  10.5 7.9 %copy-start.17 = (s32[8,4]{0,1:T(4,128)S(1)}, s32[8,4]{0,1:T(4,128)}, u32[]{:S(2)}) copy-start(s32[8,4]{0,1:T(4,128)} %param.17) | copy-start | bytes 388
  10.5 50.1 %copy-start = (f32[512]{0:T(512)S(1)}, f32[512]{0:T(512)}, u32[]{:S(2)}) copy-start(f32[512]{0:T(512)} %param.18) | copy-start | bytes 6148
  10.5 50.1 %all-to-all-start = ((bf16[16,528,128]{2,1,0:T(8,128)(2,1)}), bf16[16,528,128]{2,1,0:T(8,128)(2,1)S(1)}, u32[]{:S(2)}, u32[]{:S(2)}) async-start(bf16[16,528,128]{2,1,0:T(8,128)(2,1)} %get-tuple-element.24), calls=%async_computation | async-start | bytes 4325376 | tf_op jit(solution)/shard_map/all_to_all | solution.py:533
  62.7 25.3 %collective-permute-start.3 = (bf16[256,512]{1,0:T(8,128)(2,1)S(1)}, bf16[256,512]{1,0:T(8,128)(2,1)S(1)}, u32[]{:S(2)}, u32[]{:S(2)}) collective-permute-start(bf16[256,512]{1,0:T(8,128)(2,1)S(1)} %get-tuple-element.26), channel_id=1, source_target_pairs={{0,8},{2,10},{4,12},{6,14},{8,16},{10,18},{12,20},{14,22},{16,24},... | collective-permute-start | bytes 786440 | tf_op jit(solution)/shard_map/ppermute | solution.py:481
  68.8 19.2 %collective-permute-start.4 = (bf16[256,512]{1,0:T(8,128)(2,1)S(1)}, bf16[256,512]{1,0:T(8,128)(2,1)S(1)}, u32[]{:S(2)}, u32[]{:S(2)}) collective-permute-start(bf16[256,512]{1,0:T(8,128)(2,1)S(1)} %get-tuple-element.26), channel_id=1, source_target_pairs={{0,24},{2,26},{4,28},{6,30},{8,0},{10,2},{12,4},{14,6},{16,8},{18,... | collective-permute-start | bytes 786440 | tf_op jit(solution)/shard_map/ppermute | solution.py:481
  69.0 32.4 %collective-permute-start = (bf16[256,512]{1,0:T(8,128)(2,1)S(1)}, bf16[256,512]{1,0:T(8,128)(2,1)S(1)}, u32[]{:S(2)}, u32[]{:S(2)}) collective-permute-start(bf16[256,512]{1,0:T(8,128)(2,1)S(1)} %get-tuple-element.26), channel_id=1, source_target_pairs={{0,2},{2,0},{4,6},{6,4},{8,10},{10,8},{12,14},{14,12},{16,18},{18,... | collective-permute-start | bytes 786440 | tf_op jit(solution)/shard_map/ppermute | solution.py:481
  69.4 32.3 %collective-permute-start.1 = (bf16[256,512]{1,0:T(8,128)(2,1)S(1)}, bf16[256,512]{1,0:T(8,128)(2,1)S(1)}, u32[]{:S(2)}, u32[]{:S(2)}) collective-permute-start(bf16[256,512]{1,0:T(8,128)(2,1)S(1)} %get-tuple-element.26), channel_id=1, source_target_pairs={{0,4},{2,6},{4,0},{6,2},{8,12},{10,14},{12,8},{14,10},{16,20},{18,... | collective-permute-start | bytes 786440 | tf_op jit(solution)/shard_map/ppermute | solution.py:481
  73.1 28.7 %collective-permute-start.2 = (bf16[256,512]{1,0:T(8,128)(2,1)S(1)}, bf16[256,512]{1,0:T(8,128)(2,1)S(1)}, u32[]{:S(2)}, u32[]{:S(2)}) collective-permute-start(bf16[256,512]{1,0:T(8,128)(2,1)S(1)} %get-tuple-element.26), channel_id=1, source_target_pairs={{0,6},{2,4},{4,2},{6,0},{8,14},{10,12},{12,10},{14,8},{16,22},{18,... | collective-permute-start | bytes 786440 | tf_op jit(solution)/shard_map/ppermute | solution.py:481
  73.1 6.9 %copy-start.4 = (bf16[512,512]{1,0:T(8,128)(2,1)S(1)}, bf16[512,512]{1,0:T(8,128)(2,1)}, u32[]{:S(2)}) copy-start(bf16[512,512]{1,0:T(8,128)(2,1)} %wq_ref.3) | copy-start | bytes 1572868
  73.1 6.9 %copy-start.5 = (bf16[512,512]{1,0:T(8,128)(2,1)S(1)}, bf16[512,512]{1,0:T(8,128)(2,1)}, u32[]{:S(2)}) copy-start(bf16[512,512]{1,0:T(8,128)(2,1)} %wv_ref.3) | copy-start | bytes 1572868
  78.6 1.4 copy-start.13
  88.1 13.8 %collective-permute-start.5 = (bf16[256,512]{1,0:T(8,128)(2,1)S(1)}, bf16[256,512]{1,0:T(8,128)(2,1)S(1)}, u32[]{:S(2)}, u32[]{:S(2)}) collective-permute-start(bf16[256,512]{1,0:T(8,128)(2,1)S(1)} %get-tuple-element.43), channel_id=1, source_target_pairs={{0,2},{2,0},{4,6},{6,4},{8,10},{10,8},{12,14},{14,12},{16,18},{18,... | collective-permute-start | bytes 786440 | tf_op jit(solution)/shard_map/ppermute | solution.py:481
  88.6 13.4 %collective-permute-start.6 = (bf16[256,512]{1,0:T(8,128)(2,1)S(1)}, bf16[256,512]{1,0:T(8,128)(2,1)S(1)}, u32[]{:S(2)}, u32[]{:S(2)}) collective-permute-start(bf16[256,512]{1,0:T(8,128)(2,1)S(1)} %get-tuple-element.42), channel_id=1, source_target_pairs={{0,4},{2,6},{4,0},{6,2},{8,12},{10,14},{12,8},{14,10},{16,20},{18,... | collective-permute-start | bytes 786440 | tf_op jit(solution)/shard_map/ppermute | solution.py:481
  90.0 20.2 %copy-start.14 = (bf16[2048,512]{1,0:T(8,128)(2,1)S(1)}, bf16[2048,512]{1,0:T(8,128)(2,1)}, u32[]{:S(2)}) copy-start(bf16[2048,512]{1,0:T(8,128)(2,1)} %copy-done.13) | copy-start | bytes 6291460
  98.0 2.0 %copy-start.10 = (f32[2048,512]{1,0:T(8,128)}, f32[2048,512]{1,0:T(8,128)S(1)}, u32[]{:S(2)}) copy-start(f32[2048,512]{1,0:T(8,128)S(1)} %get-tuple-element.39.den_ref) | copy-start | bytes 12582916
  100.0 1.3 copy-start.11
  101.3 8.8 %copy-start.9 = (f32[2048,512]{1,0:T(8,128)}, f32[2048,512]{1,0:T(8,128)S(1)}, u32[]{:S(2)}) copy-start(f32[2048,512]{1,0:T(8,128)S(1)} %get-tuple-element.38.num_ref) | copy-start | bytes 12582916
  101.3 8.9 %copy-start.1 = (bf16[512,1024]{1,0:T(8,128)(2,1)S(1)}, bf16[512,1024]{1,0:T(8,128)(2,1)}, u32[]{:S(2)}) copy-start(bf16[512,1024]{1,0:T(8,128)(2,1)} %wg_ref.1) | copy-start | bytes 3145732
  101.4 8.9 %copy-start.2 = (bf16[512,1024]{1,0:T(8,128)(2,1)S(1)}, bf16[512,1024]{1,0:T(8,128)(2,1)}, u32[]{:S(2)}) copy-start(bf16[512,1024]{1,0:T(8,128)(2,1)} %wu_ref.1) | copy-start | bytes 3145732
  101.4 8.9 %copy-start.3 = (bf16[1024,512]{1,0:T(8,128)(2,1)S(1)}, bf16[1024,512]{1,0:T(8,128)(2,1)}, u32[]{:S(2)}) copy-start(bf16[1024,512]{1,0:T(8,128)(2,1)} %wd_ref.1) | copy-start | bytes 3145732
  101.4 8.9 %copy-start.6 = (bf16[512,512]{1,0:T(8,128)(2,1)S(1)}, bf16[512,512]{1,0:T(8,128)(2,1)}, u32[]{:S(2)}) copy-start(bf16[512,512]{1,0:T(8,128)(2,1)} %wpv_ref.1) | copy-start | bytes 1572868
  101.4 8.9 %copy-start.7 = (bf16[512,512]{1,0:T(8,128)(2,1)S(1)}, bf16[512,512]{1,0:T(8,128)(2,1)}, u32[]{:S(2)}) copy-start(bf16[512,512]{1,0:T(8,128)(2,1)} %wo_ref.1) | copy-start | bytes 1572868
  101.4 8.9 %copy-start.8 = (f32[512]{0:T(512)S(1)}, f32[512]{0:T(512)}, u32[]{:S(2)}) copy-start(f32[512]{0:T(512)} %param.26) | copy-start | bytes 6148
  101.4 8.8 %collective-permute-start.7 = (bf16[256,512]{1,0:T(8,128)(2,1)S(1)}, bf16[256,512]{1,0:T(8,128)(2,1)S(1)}, u32[]{:S(2)}, u32[]{:S(2)}) collective-permute-start(bf16[256,512]{1,0:T(8,128)(2,1)S(1)} %get-tuple-element.41), channel_id=1, source_target_pairs={{0,6},{2,4},{4,2},{6,0},{8,14},{10,12},{12,10},{14,8},{16,22},{18,... | collective-permute-start | bytes 786440 | tf_op jit(solution)/shard_map/ppermute | solution.py:481
  110.3 1.6 copy-start.12
  135.2 51.4 %copy-start.15 = (f32[16,128]{1,0:T(8,128)S(1)}, f32[16,128]{1,0:T(8,128)}, u32[]{:S(2)}) copy-start(f32[16,128]{1,0:T(8,128)} %get-tuple-element.23.ids_ref) | copy-start | bytes 24580

commit v4 on v3

--- a/solution.py
+++ b/solution.py
@@ -22,7 +22,7 @@
 BF16 = jnp.bfloat16
 
 
-def params(mebibytes=40):
+def params(mebibytes=28):
     return pltpu.CompilerParams(vmem_limit_bytes=mebibytes * 1024 * 1024)
 
 
@@ -35,6 +35,10 @@
 
 
 def whole(shape):
+    return pl.BlockSpec(shape, lambda *_: (0,) * len(shape), pipeline_mode=pl.Buffered(1))
+
+
+def kept(shape):
     return pl.BlockSpec(shape, lambda *_: (0,) * len(shape))
 
 
@@ -142,7 +146,7 @@
             in_specs=[whole((tiles, LANES)), pl.BlockSpec(memory_space=pl.ANY)],
             out_specs=[
                 pl.BlockSpec((TILE // send_each, payload, LANES), lambda i, *_: (i, 0, 0)),
-                whole((tiles, LANES)),
+                kept((tiles, LANES)),
             ],
             scratch_shapes=[
                 pltpu.VMEM((rows_dev, width), BF16),
@@ -221,7 +225,7 @@
             pl.BlockSpec((peers // steps, payload, LANES), lambda i: (i, 0, 0)),
             whole((1, width)),
         ],
-        out_specs=[row_blocks(TILE, width), whole((tiles, LANES)), whole(pooled)],
+        out_specs=[row_blocks(TILE, width), kept((tiles, LANES)), kept(pooled)],
         out_shape=[
             jax.ShapeDtypeStruct((rows_dev, width), BF16),
             jax.ShapeDtypeStruct((tiles, LANES), F32),
@@ -323,8 +327,8 @@
         weights[g] = jnp.exp2(dot(query[:, g * LANES : (g + 1) * LANES], keys[g])).astype(BF16)
     for g in range(groups):
         both = dot(weights[g], values[g])
-        num_ref[:, g * LANES : (g + 1) * LANES] = both[:, :LANES]
-        den_ref[:, g * LANES : (g + 1) * LANES] = both[:, LANES:]
+        num_ref[:, g * LANES : (g + 1) * LANES] = both[:, :LANES].astype(BF16)
+        den_ref[:, g * LANES : (g + 1) * LANES] = both[:, LANES:].astype(BF16)
 
 
 def local_attention(part, parts, normed, wq, wk, wv, scale, head_size, earlier=()):
@@ -342,8 +346,8 @@
         out_specs=[rows] * 3,
         out_shape=[
             jax.ShapeDtypeStruct((rows_dev, width), BF16),
-            jax.ShapeDtypeStruct((rows_dev, width), F32),
-            jax.ShapeDtypeStruct((rows_dev, width), F32),
+            jax.ShapeDtypeStruct((rows_dev, width), BF16),
+            jax.ShapeDtypeStruct((rows_dev, width), BF16),
         ],
         scratch_shapes=[
             pltpu.VMEM((2 * LANES, 2 * LANES), BF16),
@@ -409,8 +413,8 @@
         for g in range(groups):
             lanes = slice(g * LANES, (g + 1) * LANES)
             both = dot(weights[b, g], values[b, g])
-            num = both[:, :LANES] + num_ref[rows, lanes]
-            den = both[:, LANES:] + den_ref[rows, lanes]
+            num = both[:, :LANES] + num_ref[rows, lanes].astype(F32)
+            den = both[:, LANES:] + den_ref[rows, lanes].astype(F32)
             attended[rows, lanes] = (num / den).astype(BF16)
     projected = dot(attended[...], wo_ref[...])
     residual = (grouped_ref[...].astype(F32) + projected).astype(BF16)
@@ -485,23 +489,20 @@
     return route(block, lambda i: i ^ mate)
 
 
-def first_stage(pooled):
-    below = route(pooled, lambda i: i + GROUP)
-    above = route(pooled, lambda i: i - GROUP)
-    return below, above, [to_mate(pooled, mate) for mate in range(1, GROUP)]
-
-
-def second_stage(below, above, place):
-    return [
-        to_mate(jnp.where(place > (place ^ mate), below, above), mate) for mate in range(1, GROUP)
-    ]
+def wanted(below, above, place, mate):
+    return jnp.where(place > (place ^ mate), below, above)
+
+
+SLOT_INSIDE = (0, 5, 1, 6)
+SLOT_BELOW = (2, 7, 4, 8)
 
 
 def block_slots(owner, me, peers):
     mate = (owner % GROUP) ^ (me % GROUP)
     ahead = jnp.mod(owner // GROUP - me // GROUP, peers // GROUP)
-    outside = jnp.where(mate == 0, jnp.where(ahead == 1, GROUP + 1, GROUP), GROUP + 1 + mate)
-    return jnp.where(ahead == 0, mate, outside)
+    pick = lambda table: sum(jnp.where(mate == m, table[m], 0) for m in range(GROUP))
+    outside = pick(SLOT_BELOW) + jnp.where((mate == 0) & (ahead == 1), 1, 0)
+    return jnp.where(ahead == 0, pick(SLOT_INSIDE), outside)
 
 
 def on_device(
@@ -534,7 +535,9 @@
 
     outgoing, slot = send_order(points, point_row_index.reshape(rows_dev // LANES, LANES), me, peers)
     source, ids, pooled = pool(swap(outgoing), attention_norm_gain[None], rows_dev)
-    below, above, mates = first_stage(pooled)
+    below = route(pooled, lambda i: i + GROUP)
+    above = route(pooled, lambda i: i - GROUP)
+    beside = to_mate(pooled, 2)
     grouped, normed = group(ids, source, attention_norm_gain[None])
     scale = jnp.repeat(head_score_scale * (LOG2E / head_size), head_size)[None]
     attend = functools.partial(
@@ -547,10 +550,14 @@
         head_size=head_size,
     )
     part = attend(0, 2)
-    below, above, part = lax.optimization_barrier((below, above, part))
-    more = second_stage(below, above, me % GROUP)
+    below, above, beside, part = lax.optimization_barrier((below, above, beside, part))
+    place = me % GROUP
+    second = to_mate(wanted(below, above, place, 2), 2)
+    near = to_mate(jnp.stack([pooled, beside, wanted(below, above, place, 1)]), 1)
     query, num, den = attend(1, 2, earlier=part)
-    candidates = jnp.stack([pooled, *mates, below, above, *more])
+    second, query = lax.optimization_barrier((second, query))
+    last = to_mate(second, 1)
+    candidates = jnp.concatenate([jnp.stack([pooled, beside, below, above, second]), near, last[None]])
     candidates = candidates.reshape(candidates.shape[0] * blocks_dev, comp, width)
     slots = block_slots(neighbour_ball_list // blocks_dev, me, peers)
     chosen = (slots * blocks_dev + neighbour_ball_list % blocks_dev).reshape(-1)

time: 193 us -> 178 us (0.922)
  waiting for transfers between devices: 49 us -> 41.8 us
  local copies, waits for them, and re-layouts: 8.31 us -> 2.26 us
    ppermute x8 -> x6, waiting for transfers between devices: 8.2 us -> 1.08 us  [route(): lax.ppermute(block, 'pts', [(i, target(i) % len(devices)) for i in devices])]
    unnamed x48 -> x34, local copies, waits for them, and re-layouts: 7.98 us -> 1.92 us
    ppermute x8 -> x6, starting transfers between devices: 12.7 us -> 11.3 us  [route(): lax.ppermute(block, 'pts', [(i, target(i) % len(devices)) for i in devices])]
  transfers between devices with their start and end apart: 9 -> 7, of which waited for: 2 -> 2; matrix products, arithmetic and copies ran while one was open for 1% -> 1% of each run, Pallas kernels for 11% -> 12%
where the time goes in v4:
time: 178 us; the launch traced here: 177 us
  Pallas kernels  61.9 us (35%)
  blocking collectives  52.1 us (29%)
  waiting for transfers between devices  41.8 us (23%)
  starting transfers between devices  18.8 us (11%)
  local copies, waits for them, and re-layouts  2.26 us (1%)
    all_to_all x1, blocking collectives, swap(): return lax.all_to_all(array, 'pts', split_axis=0, concat_axis=0, tiled=True)  52.1 us
    all_to_all x1, waiting for transfers between devices, swap(): return lax.all_to_all(array, 'pts', split_axis=0, concat_axis=0, tiled=True)  40.7 us
    pallas_call x1, Pallas kernels, finish(): pl.pallas_call(functools.partial(finish_kernel, head_size), grid_spec=plt...  16.6 us
    pallas_call x2, Pallas kernels, local_attention(): pl.pallas_call(functools.partial(local_kernel, head_size), grid=(steps,),...  16.1 us
    ppermute x6, starting transfers between devices, route(): lax.ppermute(block, 'pts', [(i, target(i) % len(devices)) for i in devices])  11.3 us
    pallas_call x2, Pallas kernels, take_rows(): pl.pallas_call(rows_kernel, grid=(rows_dev // TILE,), in_specs=[whole(ids...  11.2 us
    pallas_call x1, Pallas kernels, send_order(): pl.pallas_call(functools.partial(send_kernel, send_each), grid_spec=pltpu...  10.4 us
    all_to_all x1, starting transfers between devices, swap(): return lax.all_to_all(array, 'pts', split_axis=0, concat_axis=0, tiled=True)  7.47 us
  transfers between devices with their start and end apart: 7, of which 2 were waited for; matrix products, arithmetic and copies ran while one was open for 1% of the time, Pallas kernels for 12%

profile of v4, /device:TPU:1, one launch (start us, length us, event | category | flops | bytes accessed | tf_op | source)
XLA Modules:
  0.0 177.3 jit_solution(11132262782657441217)
XLA Ops:
  0.0 10.4 %send_order.1 = (bf16[16,528,128]{2,1,0:T(8,128)(2,1)}, f32[16,128]{1,0:T(8,128)}) custom-call(s32[1]{0:T(128)} %bitcast.me_ref, s32[16,128]{1,0:T(8,128)} %bitcast.34, bf16[2048,512]{1,0:T(8,128)(2,1)} %points_ref.1), custom_call_target="tpu_custom_call" | custom-call | flops 5368709120 | bytes 4194304 | tf_op jit(solution)/shard_map/send_order/pallas_call | solution.py:141
  10.4 0.0 copy-start.10
  10.4 0.0 copy-start.12
  10.4 0.0 copy-start.11
  10.5 0.0 copy-start
  10.5 7.5 %all-to-all-start = ((bf16[16,528,128]{2,1,0:T(8,128)(2,1)}), bf16[16,528,128]{2,1,0:T(8,128)(2,1)S(1)}, u32[]{:S(2)}, u32[]{:S(2)}) async-start(bf16[16,528,128]{2,1,0:T(8,128)(2,1)} %get-tuple-element.27), calls=%async_computation | async-start | bytes 4325376 | tf_op jit(solution)/shard_map/all_to_all | solution.py:534
  17.9 0.0 copy-done.10
  17.9 0.2 copy.23
  18.2 0.0 copy-done.12
  18.2 0.1 broadcast_in_dim.40
  18.3 0.1 broadcast_in_dim_reshape.3.scale_ref
  18.3 0.0 copy-done.11
  18.4 0.1 copy.22
  18.5 0.1 reshape.20.chosen_ref
  18.5 1.3 copy.24
  19.8 40.7 %all-to-all-done.arrived_ref = bf16[16,528,128]{2,1,0:T(8,128)(2,1)S(1)} async-done(((bf16[16,528,128]{2,1,0:T(8,128)(2,1)}), bf16[16,528,128]{2,1,0:T(8,128)(2,1)S(1)}, u32[]{:S(2)}, u32[]{:S(2)}) %all-to-all-start) | async-done | bytes 2162720 | tf_op jit(solution)/shard_map/all_to_all | solution.py:534
  60.5 0.0 copy-done
  60.5 2.1 %pool_arrived.1 = (bf16[2048,512]{1,0:T(8,128)(2,1)S(1)}, f32[16,128]{1,0:T(8,128)S(1)}, bf16[256,512]{1,0:T(8,128)(2,1)S(1)}) custom-call(bf16[16,528,128]{2,1,0:T(8,128)(2,1)S(1)} %all-to-all-done.arrived_ref, f32[1,512]{1,0:T(1,128)S(1)} %bitcast.30), custom_call_target="tpu_custom_call" | custom-call | flops 536870912 | bytes 4194304 | tf_op jit(solution)/shard_map/pool_arrived/pallas_call | solution.py:221
  62.7 6.1 %collective-permute-start = (bf16[256,512]{1,0:T(8,128)(2,1)S(1)}, bf16[256,512]{1,0:T(8,128)(2,1)S(1)}, u32[]{:S(2)}, u32[]{:S(2)}) collective-permute-start(bf16[256,512]{1,0:T(8,128)(2,1)S(1)} %get-tuple-element.29), channel_id=1, source_target_pairs={{0,8},{2,10},{4,12},{6,14},{8,16},{10,18},{12,20},{14,22},{16,24},... | collective-permute-start | bytes 786440 | tf_op jit(solution)/shard_map/ppermute | solution.py:485
  68.8 0.2 collective-permute-start.1
  69.0 3.6 %collective-permute-start.2 = (bf16[256,512]{1,0:T(8,128)(2,1)S(1)}, bf16[256,512]{1,0:T(8,128)(2,1)S(1)}, u32[]{:S(2)}, u32[]{:S(2)}) collective-permute-start(bf16[256,512]{1,0:T(8,128)(2,1)S(1)} %get-tuple-element.29), channel_id=1, source_target_pairs={{0,4},{2,6},{4,0},{6,2},{8,12},{10,14},{12,8},{14,10},{16,20},{18,... | collective-permute-start | bytes 786440 | tf_op jit(solution)/shard_map/ppermute | solution.py:485
  72.6 0.0 copy-start.4
  72.6 0.0 copy-start.5
  72.6 5.5 %group_balls.1 = (bf16[2048,512]{1,0:T(8,128)(2,1)S(1)}, bf16[2048,512]{1,0:T(8,128)(2,1)S(1)}) custom-call(f32[16,128]{1,0:T(8,128)S(1)} %get-tuple-element.28.ids_ref, bf16[2048,512]{1,0:T(8,128)(2,1)S(1)} %get-tuple-element.30.source_ref, f32[1,512]{1,0:T(1,128)S(1)} %bitcast.31), custom_call_target="tpu_custom_call" | custom-call | flops 4294967296 | bytes 6291456 | tf_op jit(solution)/shard_map/group_balls/pallas_call | solution.py:253
  78.1 0.0 copy-done.4
  78.1 0.0 copy-done.5
  78.1 8.0 %local_attention.2 = (bf16[2048,512]{1,0:T(8,128)(2,1)S(1)}, bf16[2048,512]{1,0:T(8,128)(2,1)S(1)}, bf16[2048,512]{1,0:T(8,128)(2,1)S(1)}) custom-call(f32[1,512]{1,0:T(1,128)S(1)} %broadcast_in_dim_reshape.3.scale_ref, bf16[2048,512]{1,0:T(8,128)(2,1)S(1)} %get-tuple-element.31.normed_ref, bf16[512,512]{1,0:T(8,128)(2,1)S(1)} %copy-done.4, ...), custom_call_target="tpu_custom_call" | custom-call | flops 5368709120 | bytes 6291456 | tf_op jit(solution)/shard_map/local_attention/pallas_call | solution.py:341
  86.2 0.0 collective-permute-done
  86.2 0.0 collective-permute-done.1
  86.2 0.0 collective-permute-done.2
  86.3 0.1 pad_maximum_fusion
  86.4 0.8 collective-permute-start.4
  87.2 0.0 collective-permute-start.3
  87.2 8.0 %local_attention.3 = (bf16[2048,512]{1,0:T(8,128)(2,1)S(1)}, bf16[2048,512]{1,0:T(8,128)(2,1)S(1)}, bf16[2048,512]{1,0:T(8,128)(2,1)S(1)}) custom-call(f32[1,512]{1,0:T(1,128)S(1)} %broadcast_in_dim_reshape.3.scale_ref, bf16[2048,512]{1,0:T(8,128)(2,1)S(1)} %get-tuple-element.31.normed_ref, ...), custom_call_target="tpu_custom_call", output_to_operand_aliasing={{0}: (5, {}), {1}: (6, {}), {2}: (7, {})} | custom-call | flops 5368709120 | bytes 6291456 | tf_op jit(solution)/shard_map/local_attention/pallas_call | solution.py:341
  95.2 0.0 copy-start.1
  95.2 0.0 copy-start.2
  95.3 0.0 copy-start.3
  95.3 0.0 copy-start.6
  95.3 0.0 copy-start.7
  95.3 0.0 copy-start.8
  95.4 0.0 collective-permute-done.3
  95.4 0.5 collective-permute-start.5
  96.0 0.0 collective-permute-done.4
  96.0 0.1 constant_dynamic-update-slice_fusion
  96.0 1.1 collective-permute-done.5
  97.1 0.0 copy-done.1
  97.1 0.0 copy-done.2
  97.1 0.0 copy-done.3
  97.2 0.1 copy-done.6
  97.2 0.2 copy-done.7
  97.4 0.0 copy-done.8
  97.4 16.6 %finish_balls.1.source_ref = bf16[2048,512]{1,0:T(8,128)(2,1)S(1)} custom-call(s32[32]{0:T(128)S(1)} %reshape.20.chosen_ref, bf16[72,32,512]{2,1,0:T(8,128)(2,1)S(1)} %bitcast.29, bf16[2048,512]{1,0:T(8,128)(2,1)S(1)} %get-tuple-element.43.query_ref, bf16[2048,512]{1,0:T(8,128)(2,1)S(1)} %get-tuple-element.44.num_ref, ...), custom_call_target="tpu_custom_call" | custom-call | flops 12884901888 | bytes 12582912 | tf_op jit(solution)/shard_map/finish_balls/pallas_call | solution.py:437
  114.0 5.2 %take_rows.2 = bf16[2048,512]{1,0:T(8,128)(2,1)S(1)} custom-call(f32[16,128]{1,0:T(8,128)S(1)} %get-tuple-element.28.ids_ref, bf16[2048,512]{1,0:T(8,128)(2,1)S(1)} %finish_balls.1.source_ref), custom_call_target="tpu_custom_call" | custom-call | flops 4294967296 | bytes 4194304 | tf_op jit(solution)/shard_map/take_rows/pallas_call | solution.py:469
  119.2 0.0 copy-start.9
  119.2 52.1 %all_to_all.10 = bf16[16,128,512]{2,1,0:T(8,128)(2,1)S(1)} all-to-all(bf16[16,128,512]{2,1,0:T(8,128)(2,1)S(1)} %bitcast.24), channel_id=1, replica_groups=mesh['pts'=16,'rep'=2] {'pts'}, dimensions={0} | all-to-all | bytes 4194304 | tf_op jit(solution)/shard_map/all_to_all | solution.py:534
  171.3 0.0 copy-done.9
  171.3 6.0 %take_rows.3 = bf16[2048,512]{1,0:T(8,128)(2,1)} custom-call(f32[16,128]{1,0:T(8,128)S(1)} %copy-done.9, bf16[2048,512]{1,0:T(8,128)(2,1)S(1)} %bitcast.23), custom_call_target="tpu_custom_call" | custom-call | flops 4294967296 | bytes 4194304 | tf_op jit(solution)/shard_map/take_rows/pallas_call | solution.py:469
  (9 shorter events, 0.2 us)
Async XLA Ops:
  10.4 7.5 %copy-start.10 = (bf16[512,512]{1,0:T(8,128)(2,1)S(1)}, bf16[512,512]{1,0:T(8,128)(2,1)}, u32[]{:S(2)}) copy-start(bf16[512,512]{1,0:T(8,128)(2,1)} %param.20) | copy-start | bytes 1572868
  10.4 7.7 %copy-start.12 = (f32[16]{0:T(128)S(1)}, f32[16]{0:T(128)}, u32[]{:S(2)}) copy-start(f32[16]{0:T(128)} %param.24) | copy-start | bytes 196
  10.4 7.9 %copy-start.11 = (s32[8,4]{0,1:T(4,128)S(1)}, s32[8,4]{0,1:T(4,128)}, u32[]{:S(2)}) copy-start(s32[8,4]{0,1:T(4,128)} %param.17) | copy-start | bytes 388
  10.5 50.1 %copy-start = (f32[512]{0:T(512)S(1)}, f32[512]{0:T(512)}, u32[]{:S(2)}) copy-start(f32[512]{0:T(512)} %param.18) | copy-start | bytes 6148
  10.5 50.1 %all-to-all-start = ((bf16[16,528,128]{2,1,0:T(8,128)(2,1)}), bf16[16,528,128]{2,1,0:T(8,128)(2,1)S(1)}, u32[]{:S(2)}, u32[]{:S(2)}) async-start(bf16[16,528,128]{2,1,0:T(8,128)(2,1)} %get-tuple-element.27), calls=%async_computation | async-start | bytes 4325376 | tf_op jit(solution)/shard_map/all_to_all | solution.py:534
  62.7 23.5 %collective-permute-start = (bf16[256,512]{1,0:T(8,128)(2,1)S(1)}, bf16[256,512]{1,0:T(8,128)(2,1)S(1)}, u32[]{:S(2)}, u32[]{:S(2)}) collective-permute-start(bf16[256,512]{1,0:T(8,128)(2,1)S(1)} %get-tuple-element.29), channel_id=1, source_target_pairs={{0,8},{2,10},{4,12},{6,14},{8,16},{10,18},{12,20},{14,22},{16,24},... | collective-permute-start | bytes 786440 | tf_op jit(solution)/shard_map/ppermute | solution.py:485
  68.8 17.4 %collective-permute-start.1 = (bf16[256,512]{1,0:T(8,128)(2,1)S(1)}, bf16[256,512]{1,0:T(8,128)(2,1)S(1)}, u32[]{:S(2)}, u32[]{:S(2)}) collective-permute-start(bf16[256,512]{1,0:T(8,128)(2,1)S(1)} %get-tuple-element.29), channel_id=1, source_target_pairs={{0,24},{2,26},{4,28},{6,30},{8,0},{10,2},{12,4},{14,6},{16,8},{18,... | collective-permute-start | bytes 786440 | tf_op jit(solution)/shard_map/ppermute | solution.py:485
  69.0 17.2 %collective-permute-start.2 = (bf16[256,512]{1,0:T(8,128)(2,1)S(1)}, bf16[256,512]{1,0:T(8,128)(2,1)S(1)}, u32[]{:S(2)}, u32[]{:S(2)}) collective-permute-start(bf16[256,512]{1,0:T(8,128)(2,1)S(1)} %get-tuple-element.29), channel_id=1, source_target_pairs={{0,4},{2,6},{4,0},{6,2},{8,12},{10,14},{12,8},{14,10},{16,20},{18,... | collective-permute-start | bytes 786440 | tf_op jit(solution)/shard_map/ppermute | solution.py:485
  72.6 5.5 %copy-start.4 = (bf16[512,512]{1,0:T(8,128)(2,1)S(1)}, bf16[512,512]{1,0:T(8,128)(2,1)}, u32[]{:S(2)}) copy-start(bf16[512,512]{1,0:T(8,128)(2,1)} %wq_ref.3) | copy-start | bytes 1572868
  72.6 5.5 %copy-start.5 = (bf16[512,512]{1,0:T(8,128)(2,1)S(1)}, bf16[512,512]{1,0:T(8,128)(2,1)}, u32[]{:S(2)}) copy-start(bf16[512,512]{1,0:T(8,128)(2,1)} %wv_ref.3) | copy-start | bytes 1572868
  86.4 9.6 %collective-permute-start.4 = (bf16[3,256,512]{2,1,0:T(8,128)(2,1)S(1)}, bf16[3,256,512]{2,1,0:T(8,128)(2,1)S(1)}, u32[]{:S(2)}, u32[]{:S(2)}) collective-permute-start(bf16[3,256,512]{2,1,0:T(8,128)(2,1)S(1)} %pad_maximum_fusion), channel_id=1, source_target_pairs={{0,2},{2,0},{4,6},{6,4},{8,10},{10,8},{12,14},{14,12},{16,18},{18,... | collective-permute-start | bytes 2359304 | tf_op jit(solution)/shard_map/ppermute | solution.py:485
  87.2 8.2 %collective-permute-start.3 = (bf16[256,512]{1,0:T(8,128)(2,1)S(1)}, bf16[256,512]{1,0:T(8,128)(2,1)S(1)}, u32[]{:S(2)}, u32[]{:S(2)}) collective-permute-start(bf16[256,512]{1,0:T(8,128)(2,1)S(1)} %get-tuple-element.48), channel_id=1, source_target_pairs={{0,4},{2,6},{4,0},{6,2},{8,12},{10,14},{12,8},{14,10},{16,20},{18,... | collective-permute-start | bytes 786440 | tf_op jit(solution)/shard_map/ppermute | solution.py:485
  95.2 1.9 %copy-start.1 = (bf16[512,1024]{1,0:T(8,128)(2,1)S(1)}, bf16[512,1024]{1,0:T(8,128)(2,1)}, u32[]{:S(2)}) copy-start(bf16[512,1024]{1,0:T(8,128)(2,1)} %wg_ref.1) | copy-start | bytes 3145732
  95.2 1.9 %copy-start.2 = (bf16[512,1024]{1,0:T(8,128)(2,1)S(1)}, bf16[512,1024]{1,0:T(8,128)(2,1)}, u32[]{:S(2)}) copy-start(bf16[512,1024]{1,0:T(8,128)(2,1)} %wu_ref.1) | copy-start | bytes 3145732
  95.3 1.9 %copy-start.3 = (bf16[1024,512]{1,0:T(8,128)(2,1)S(1)}, bf16[1024,512]{1,0:T(8,128)(2,1)}, u32[]{:S(2)}) copy-start(bf16[1024,512]{1,0:T(8,128)(2,1)} %wd_ref.1) | copy-start | bytes 3145732
  95.3 2.0 %copy-start.6 = (bf16[512,512]{1,0:T(8,128)(2,1)S(1)}, bf16[512,512]{1,0:T(8,128)(2,1)}, u32[]{:S(2)}) copy-start(bf16[512,512]{1,0:T(8,128)(2,1)} %wpv_ref.1) | copy-start | bytes 1572868
  95.3 2.1 %copy-start.7 = (bf16[512,512]{1,0:T(8,128)(2,1)S(1)}, bf16[512,512]{1,0:T(8,128)(2,1)}, u32[]{:S(2)}) copy-start(bf16[512,512]{1,0:T(8,128)(2,1)} %wo_ref.1) | copy-start | bytes 1572868
  95.3 2.1 %copy-start.8 = (f32[512]{0:T(512)S(1)}, f32[512]{0:T(512)}, u32[]{:S(2)}) copy-start(f32[512]{0:T(512)} %param.26) | copy-start | bytes 6148
  95.4 1.7 collective-permute-start.5
  119.2 52.1 %copy-start.9 = (f32[16,128]{1,0:T(8,128)S(1)}, f32[16,128]{1,0:T(8,128)}, u32[]{:S(2)}) copy-start(f32[16,128]{1,0:T(8,128)} %get-tuple-element.26.ids_ref) | copy-start | bytes 24580

commit v5 on v4

--- a/solution.py
+++ b/solution.py
@@ -17,6 +17,9 @@
 DEPTH = 512
 BALLS_STEP = 2
 LOW = 64
+SEND_PITCH = 8
+SEND_STEPS = 2
+TAKE_STEPS = 2
 LOG2E = math.log2(math.e)
 F32 = jnp.float32
 BF16 = jnp.bfloat16
@@ -44,10 +47,6 @@
 
 def row_blocks(rows, width):
     return pl.BlockSpec((rows, width), lambda i, *_: (i, 0))
-
-
-def column_of(row):
-    return jnp.broadcast_to(row, (LANES, LANES)).T
 
 
 def picked_rows(pick_tile, rows, source_ref):
@@ -67,28 +66,49 @@
     return lambda t: jnp.where(ids_ref[t : t + 1, :] == targets, 1.0, 0.0).astype(BF16)
 
 
-def by_row_ids(ids_ref, first, rows):
-    wanted = jnp.concatenate(
-        [column_of(ids_ref[pl.ds(first + u, 1), :]) for u in range(rows // LANES)], axis=0
-    )
-    lane = lax.broadcasted_iota(jnp.int32, (rows, LANES), 1).astype(F32)
-    return lambda t: jnp.where(wanted - float(t * LANES) == lane, 1.0, 0.0).astype(BF16)
-
-
-def send_kernel(send_each, me_ref, index_ref, points_ref, out_ref, slot_ref, held, aux, arrivals):
+def chunk_rows(ref, first, rows, chunk, pitch):
+    return ref.at[pl.ds(first * pitch + chunk, rows, stride=pitch), :]
+
+
+def gather_rows(places_ref, first_tile, tiles, source, target, pitch):
+    def move(t, carry):
+        places = [places_ref[first_tile + t, l] for l in range(LANES)]
+        rows = [source[pl.ds(pl.multiple_of(p, pitch), pitch), :] for p in places]
+        for l in range(LANES):
+            target[pl.ds(pl.multiple_of((t * LANES + l) * pitch, pitch), pitch), :] = rows[l]
+        return carry
+
+    lax.fori_loop(0, tiles, move, 0)
+
+
+def scatter_rows(places_ref, tiles, source, target, pitch):
+    def move(t, carry):
+        places = [places_ref[t, l] for l in range(LANES)]
+        rows = [
+            source[pl.ds(pl.multiple_of((t * LANES + l) * pitch, pitch), pitch), :] for l in range(LANES)
+        ]
+        for l in range(LANES):
+            target[pl.ds(pl.multiple_of(places[l], pitch), pitch), :] = rows[l]
+        return carry
+
+    lax.fori_loop(0, tiles, move, 0)
+
+
+def send_kernel(send_each, me_ref, index_ref, points_ref, out_ref, slot_ref, held, rows, sent, places, places_smem, arrivals, moved):
     rows_dev, width = held.shape
     tiles = rows_dev // LANES
     chunks = width // LANES
     per_tile = LANES // send_each
     peers = rows_dev // send_each
+    step_peers = out_ref.shape[0]
     step = pl.program_id(0)
-    pieces = [
-        pltpu.make_async_copy(points_ref.at[pl.ds(k, DEPTH)], held.at[pl.ds(k, DEPTH)], arrivals.at[k // DEPTH])
-        for k in range(0, rows_dev, DEPTH)
-    ]
 
     @pl.when(step == 0)
     def _():
+        pieces = [
+            pltpu.make_async_copy(points_ref.at[pl.ds(k, DEPTH)], held.at[pl.ds(k, DEPTH)], arrivals.at[k // DEPTH])
+            for k in range(0, rows_dev, DEPTH)
+        ]
         for piece in pieces:
             piece.start()
         index = index_ref[...].astype(F32)
@@ -97,40 +117,45 @@
         high = jnp.floor(local * (1.0 / LOW))
         low = local - high * LOW
         row = lax.broadcasted_iota(jnp.int32, (LANES, LANES), 0)
-        for t in range(tiles):
-            pair = jnp.where(row == 0, high[t : t + 1, :], jnp.where(row == 1, low[t : t + 1, :], 0.0))
-            aux[t * LANES : (t + 1) * LANES, :] = pair.T.astype(BF16)
+        lane = lax.broadcasted_iota(jnp.int32, (LANES, LANES), 1)
         peer = lax.broadcasted_iota(jnp.int32, (peers, LANES), 0).astype(F32)
         member = [jnp.where(dest[t : t + 1, :] == peer, 1.0, 0.0) for t in range(tiles)]
-        lane = lax.broadcasted_iota(jnp.int32, (LANES, LANES), 1)
         up_to = jnp.where(row <= lane, 1.0, 0.0).astype(BF16)
         counts = dot(jnp.concatenate(member, axis=0).astype(BF16), up_to)
         before = peer[:, 0:1] * send_each - 1.0
         for t in range(tiles):
             count = counts[t * peers : (t + 1) * peers, :]
-            slot_ref[t : t + 1, :] = jnp.sum(member[t] * (count + before), axis=0, keepdims=True)
+            slot = jnp.sum(member[t] * (count + before), axis=0, keepdims=True)
+            places[t : t + 1, :] = (slot * SEND_PITCH).astype(jnp.int32)
+            slot_ref[t : t + 1, :] = (slot * chunks).astype(jnp.int32)
             before = before + count[:, LANES - 1 :]
-        for piece in pieces:
+        move = pltpu.make_async_copy(places, places_smem, moved.at[0])
+        move.start()
+        for t in range(tiles):
+            pair = jnp.where(row == 0, high[t : t + 1, :], jnp.where(row == 1, low[t : t + 1, :], 0.0))
+            chunk_rows(rows, t * LANES, LANES, chunks, SEND_PITCH)[...] = pair.T
+        for k, piece in enumerate(pieces):
             piece.wait()
-
-    tile = by_lane_ids(slot_ref, step * TILE, TILE)
-    rows = picked_rows(tile, TILE, held).astype(BF16)
-    ids = picked_rows(tile, TILE, aux)
-    for u in range(TILE // LANES):
-        both = ids[u * LANES : (u + 1) * LANES, :].T[0:16, :]
+            for c in range(chunks):
+                part = held[k * DEPTH : (k + 1) * DEPTH, c * LANES : (c + 1) * LANES]
+                chunk_rows(rows, k * DEPTH, DEPTH, c, SEND_PITCH)[...] = part.astype(F32)
+        move.wait()
+        scatter_rows(places_smem, tiles, rows, sent, SEND_PITCH)
+
+    base = step * (step_peers * send_each)
+    for peer in range(step_peers):
+        for c in range(chunks):
+            part = chunk_rows(sent, base + peer * send_each, send_each, c, SEND_PITCH)[...]
+            out_ref[peer, c * send_each : (c + 1) * send_each, :] = part.astype(BF16)
+    for t in range(step_peers // per_tile):
+        both = chunk_rows(sent, base + t * LANES, LANES, chunks, SEND_PITCH)[...].T[0:16, :]
         for v in range(per_tile):
-            peer = u * per_tile + v
             mine = both
             if per_tile > 1:
                 lane = lax.broadcasted_iota(jnp.int32, both.shape, 1)
                 mine = jnp.where(lane // send_each == v, both, 0.0)
                 mine = pltpu.roll(mine, (me_ref[0] - v + per_tile) % per_tile * send_each, 1)
-            out_ref[peer, chunks * send_each :, :] = mine.astype(BF16)
-            first = peer * send_each
-            for c in range(chunks):
-                out_ref[peer, c * send_each : (c + 1) * send_each, :] = rows[
-                    first : first + send_each, c * LANES : (c + 1) * LANES
-                ]
+            out_ref[t * per_tile + v, chunks * send_each :, :] = mine.astype(BF16)
 
 
 def send_order(points, index_tiles, me, peers):
@@ -142,25 +167,29 @@
         functools.partial(send_kernel, send_each),
         grid_spec=pltpu.PrefetchScalarGridSpec(
             num_scalar_prefetch=1,
-            grid=(rows_dev // TILE,),
+            grid=(SEND_STEPS,),
             in_specs=[whole((tiles, LANES)), pl.BlockSpec(memory_space=pl.ANY)],
             out_specs=[
-                pl.BlockSpec((TILE // send_each, payload, LANES), lambda i, *_: (i, 0, 0)),
+                pl.BlockSpec((peers // SEND_STEPS, payload, LANES), lambda i, *_: (i, 0, 0)),
                 kept((tiles, LANES)),
             ],
             scratch_shapes=[
                 pltpu.VMEM((rows_dev, width), BF16),
-                pltpu.VMEM((rows_dev, LANES), BF16),
+                pltpu.VMEM((rows_dev * SEND_PITCH, LANES), F32),
+                pltpu.VMEM((rows_dev * SEND_PITCH, LANES), F32),
+                pltpu.VMEM((tiles, LANES), jnp.int32),
+                pltpu.SMEM((tiles, LANES), jnp.int32),
                 pltpu.SemaphoreType.DMA((rows_dev // DEPTH,)),
+                pltpu.SemaphoreType.DMA((1,)),
             ],
         ),
         out_shape=[
             jax.ShapeDtypeStruct((peers, payload, LANES), BF16),
-            jax.ShapeDtypeStruct((tiles, LANES), F32),
+            jax.ShapeDtypeStruct((tiles, LANES), jnp.int32),
         ],
         compiler_params=params(60),
         cost_estimate=pl.CostEstimate(
-            flops=2 * rows_dev * rows_dev * (width + LANES), bytes_accessed=4 * rows_dev * width, transcendentals=0
+            flops=2 * rows_dev * rows_dev * width, bytes_accessed=4 * rows_dev * width, transcendentals=0
         ),
         name="send_order",
     )(me.reshape(1), index_tiles, points)
@@ -171,7 +200,7 @@
     return (rows32 * lax.rsqrt(mean_square + 1e-05) * gain).astype(BF16)
 
 
-def pool_kernel(arrived_ref, gain_ref, source_ref, ids_ref, pooled_ref, ids, total):
+def pool_kernel(arrived_ref, gain_ref, source_ref, ids_ref, places_ref, pooled_ref, ids, total):
     peers = arrived_ref.shape[0]
     rows, width = source_ref.shape
     chunks = width // LANES
@@ -190,6 +219,7 @@
             row = row + both[0:1, :] * LOW + both[1:2, :]
         ids[t : t + 1, :] = row
         ids_ref[pl.ds(step * (rows // LANES) + t, 1), :] = row
+        places_ref[pl.ds(step * (rows // LANES) + t, 1), :] = (row * chunks).astype(jnp.int32)
     for p in range(peers):
         for c in range(chunks):
             source_ref[p * send_each : (p + 1) * send_each, c * LANES : (c + 1) * LANES] = arrived_ref[
@@ -225,10 +255,11 @@
             pl.BlockSpec((peers // steps, payload, LANES), lambda i: (i, 0, 0)),
             whole((1, width)),
         ],
-        out_specs=[row_blocks(TILE, width), kept((tiles, LANES)), kept(pooled)],
+        out_specs=[row_blocks(TILE, width), kept((tiles, LANES)), kept((tiles, LANES)), kept(pooled)],
         out_shape=[
             jax.ShapeDtypeStruct((rows_dev, width), BF16),
             jax.ShapeDtypeStruct((tiles, LANES), F32),
+            jax.ShapeDtypeStruct((tiles, LANES), jnp.int32),
             jax.ShapeDtypeStruct(pooled, BF16),
         ],
         scratch_shapes=[pltpu.VMEM((TILE // LANES, LANES), F32), pltpu.VMEM(pooled, F32)],
@@ -367,6 +398,7 @@
 def finish_kernel(
     head_size,
     chosen_ref,
+    places_ref,
     candidates_ref,
     query_ref,
     num_ref,
@@ -384,8 +416,58 @@
     values,
     weights,
     attended,
+    rows,
+    taken,
 ):
     step = pl.program_id(0)
+    steps = pl.num_programs(0) - TAKE_STEPS
+    step_rows, width = attended.shape
+    chunks = width // LANES
+
+    @pl.when(step < steps)
+    def _():
+        result = balls_step(
+            head_size, step, chosen_ref, candidates_ref, query_ref, num_ref, den_ref, grouped_ref, wpk_ref,
+            wpv_ref, wo_ref, gain_ref, wg_ref, wu_ref, wd_ref, keys, values, weights, attended,
+        )
+        for c in range(chunks):
+            part = result[:, c * LANES : (c + 1) * LANES].astype(BF16).astype(F32)
+            chunk_rows(rows, step * step_rows, step_rows, c, chunks)[...] = part
+
+    @pl.when(step >= steps)
+    def _():
+        take_block(places_ref, step - steps, rows, taken, out_ref)
+
+
+def take_block(places_ref, block, rows, taken, out_ref):
+    count, width = out_ref.shape
+    chunks = width // LANES
+    gather_rows(places_ref, block * (count // LANES), count // LANES, rows, taken, chunks)
+    for c in range(chunks):
+        out_ref[:, c * LANES : (c + 1) * LANES] = chunk_rows(taken, 0, count, c, chunks)[...].astype(BF16)
+
+
+def balls_step(
+    head_size,
+    step,
+    chosen_ref,
+    candidates_ref,
+    query_ref,
+    num_ref,
+    den_ref,
+    grouped_ref,
+    wpk_ref,
+    wpv_ref,
+    wo_ref,
+    gain_ref,
+    wg_ref,
+    wu_ref,
+    wd_ref,
+    keys,
+    values,
+    weights,
+    attended,
+):
     groups = wo_ref.shape[0] // LANES
     far = OWNERS * BALL // POOL
 
@@ -423,29 +505,33 @@
     gate = dot(ffn, wg_ref[...])
     up = dot(ffn, wu_ref[...])
     hidden = (0.5 * gate * (1.0 + jnp.tanh(0.5 * gate)) * up).astype(BF16)
-    out_ref[...] = (rows32 + dot(hidden, wd_ref[...])).astype(BF16)
-
-
-def finish(chosen, candidates, query, num, den, grouped, wpk, wpv, wo, gain, wg, wu, wd, head_size):
+    return rows32 + dot(hidden, wd_ref[...])
+
+
+def finish(chosen, places, candidates, query, num, den, grouped, wpk, wpv, wo, gain, wg, wu, wd, head_size):
     rows_dev, width = grouped.shape
     hidden = wg.shape[1]
     groups = width // LANES
     step_rows = BALLS_STEP * BALL
     spread = LANES // head_size * OWNERS * BALL // POOL
-    rows = row_blocks(step_rows, width)
+    steps = rows_dev // step_rows
+    rows = pl.BlockSpec((step_rows, width), lambda i, *_: (jnp.minimum(i, steps - 1), 0))
+    take_rows = rows_dev // TAKE_STEPS
     fixed = [wpk, wpv, wo, gain, wg, wu, wd]
     return pl.pallas_call(
         functools.partial(finish_kernel, head_size),
         grid_spec=pltpu.PrefetchScalarGridSpec(
-            num_scalar_prefetch=1,
-            grid=(rows_dev // step_rows,),
+            num_scalar_prefetch=2,
+            grid=(steps + TAKE_STEPS,),
             in_specs=[whole(candidates.shape), rows, rows, rows, rows] + [whole(a.shape) for a in fixed],
-            out_specs=rows,
+            out_specs=pl.BlockSpec((take_rows, width), lambda i, *_: (jnp.maximum(i - steps, 0), 0)),
             scratch_shapes=[
                 pltpu.VMEM((BALLS_STEP, groups, LANES, spread), BF16),
                 pltpu.VMEM((BALLS_STEP, groups, spread, 2 * LANES), BF16),
                 pltpu.VMEM((BALLS_STEP, groups, BALL, spread), BF16),
                 pltpu.VMEM((step_rows, width), BF16),
+                pltpu.VMEM((rows_dev * (width // LANES), LANES), F32),
+                pltpu.VMEM((take_rows * (width // LANES), LANES), F32),
             ],
         ),
         out_shape=jax.ShapeDtypeStruct((rows_dev, width), BF16),
@@ -456,28 +542,45 @@
             transcendentals=0,
         ),
         name="finish_balls",
-    )(chosen, candidates, query, num, den, grouped, *fixed)
-
-
-def rows_kernel(ids_ref, source_ref, out_ref):
-    tile = by_row_ids(ids_ref, pl.program_id(0) * (TILE // LANES), TILE)
-    out_ref[...] = picked_rows(tile, TILE, source_ref).astype(BF16)
-
-
-def take_rows(ids, source):
+    )(chosen, places, candidates, query, num, den, grouped, *fixed)
+
+
+def take_kernel(places_ref, source_ref, out_ref, rows, taken):
+    count, width = source_ref.shape
+    chunks = width // LANES
+
+    @pl.when(pl.program_id(0) == 0)
+    def _():
+        for first in range(0, count, DEPTH):
+            for c in range(chunks):
+                part = source_ref[first : first + DEPTH, c * LANES : (c + 1) * LANES]
+                chunk_rows(rows, first, DEPTH, c, chunks)[...] = part.astype(F32)
+
+    take_block(places_ref, pl.program_id(0), rows, taken, out_ref)
+
+
+def take_rows(places, source):
     rows_dev, width = source.shape
+    chunks = width // LANES
     return pl.pallas_call(
-        rows_kernel,
-        grid=(rows_dev // TILE,),
-        in_specs=[whole(ids.shape), whole(source.shape)],
-        out_specs=row_blocks(TILE, width),
+        take_kernel,
+        grid_spec=pltpu.PrefetchScalarGridSpec(
+            num_scalar_prefetch=1,
+            grid=(rows_dev // TILE,),
+            in_specs=[whole(source.shape)],
+            out_specs=row_blocks(TILE, width),
+            scratch_shapes=[
+                pltpu.VMEM((rows_dev * chunks, LANES), F32),
+                pltpu.VMEM((TILE * chunks, LANES), F32),
+            ],
+        ),
         out_shape=jax.ShapeDtypeStruct((rows_dev, width), BF16),
         compiler_params=params(),
         cost_estimate=pl.CostEstimate(
             flops=2 * rows_dev * rows_dev * width, bytes_accessed=4 * rows_dev * width, transcendentals=0
         ),
         name="take_rows",
-    )(ids, source)
+    )(places, source)
 
 
 def route(block, target):
@@ -534,7 +637,7 @@
         return lax.all_to_all(array, "pts", split_axis=0, concat_axis=0, tiled=True)
 
     outgoing, slot = send_order(points, point_row_index.reshape(rows_dev // LANES, LANES), me, peers)
-    source, ids, pooled = pool(swap(outgoing), attention_norm_gain[None], rows_dev)
+    source, ids, places, pooled = pool(swap(outgoing), attention_norm_gain[None], rows_dev)
     below = route(pooled, lambda i: i + GROUP)
     above = route(pooled, lambda i: i - GROUP)
     beside = to_mate(pooled, 2)
@@ -561,8 +664,9 @@
     candidates = candidates.reshape(candidates.shape[0] * blocks_dev, comp, width)
     slots = block_slots(neighbour_ball_list // blocks_dev, me, peers)
     chosen = (slots * blocks_dev + neighbour_ball_list % blocks_dev).reshape(-1)
-    ball_out = finish(
+    returning = finish(
         chosen,
+        places,
         candidates,
         query,
         num,
@@ -577,8 +681,7 @@
         down_weight,
         head_size,
     )
-    returning = take_rows(ids, ball_out).reshape(peers, send_each, width)
-    came_back = swap(returning).reshape(rows_dev, width)
+    came_back = swap(returning.reshape(peers, send_each, width)).reshape(rows_dev, width)
     return take_rows(slot, came_back)
 
 

time: 178 us -> 169 us (0.949)
  Pallas kernels: 61.9 us -> 53.6 us
    pallas_call x2 -> x1, Pallas kernels: 11.2 us -> 4.46 us  [take_rows(): pl.pallas_call(take_kernel, grid_spec=pltpu.PrefetchScalarGridSpec(num_sc...]
    pallas_call x1, Pallas kernels: 10.4 us -> 6.45 us  [send_order(): pl.pallas_call(functools.partial(send_kernel, send_each), grid_spec=pltpu...]
    pallas_call x1, Pallas kernels: 16.6 us -> 19 us  [finish(): pl.pallas_call(functools.partial(finish_kernel, head_size), grid_spec=plt...]
  transfers between devices with their start and end apart: 7 -> 7, of which waited for: 2 -> 2; matrix products, arithmetic and copies ran while one was open for 1% -> 1% of each run, Pallas kernels for 12% -> 13%
where the time goes in v5:
time: 169 us
  Pallas kernels  53.6 us (32%)
  blocking collectives  52.1 us (31%)
  waiting for transfers between devices  41.8 us (25%)
  starting transfers between devices  18.8 us (11%)
  local copies, waits for them, and re-layouts  2.26 us (1%)
    all_to_all x1, blocking collectives, swap(): return lax.all_to_all(array, 'pts', split_axis=0, concat_axis=0, tiled=True)  52.1 us
    all_to_all x1, waiting for transfers between devices, swap(): return lax.all_to_all(array, 'pts', split_axis=0, concat_axis=0, tiled=True)  40.7 us
    pallas_call x1, Pallas kernels, finish(): pl.pallas_call(functools.partial(finish_kernel, head_size), grid_spec=plt...  19 us
    pallas_call x2, Pallas kernels, local_attention(): pl.pallas_call(functools.partial(local_kernel, head_size), grid=(steps,),...  16.1 us
    ppermute x6, starting transfers between devices, route(): lax.ppermute(block, 'pts', [(i, target(i) % len(devices)) for i in devices])  11.3 us
    all_to_all x1, starting transfers between devices, swap(): return lax.all_to_all(array, 'pts', split_axis=0, concat_axis=0, tiled=True)  7.47 us
    pallas_call x1, Pallas kernels, send_order(): pl.pallas_call(functools.partial(send_kernel, send_each), grid_spec=pltpu...  6.45 us
    pallas_call x1, Pallas kernels, group(): pl.pallas_call(group_kernel, grid=(rows_dev // TILE,), in_specs=[whole(id...  5.48 us
  transfers between devices with their start and end apart: 7, of which 2 were waited for; matrix products, arithmetic and copies ran while one was open for 1% of the time, Pallas kernels for 13%

profile of v5, /device:TPU:1, one launch (start us, length us, event | category | flops | bytes accessed | tf_op | source)
XLA Modules:
  0.0 169.0 jit_solution(5094963781199228086)
XLA Ops:
  0.0 6.4 %send_order.1 = (bf16[16,528,128]{2,1,0:T(8,128)(2,1)}, s32[16,128]{1,0:T(8,128)}) custom-call(s32[1]{0:T(128)} %bitcast.me_ref, s32[16,128]{1,0:T(8,128)} %bitcast.34, bf16[2048,512]{1,0:T(8,128)(2,1)} %points_ref.1), custom_call_target="tpu_custom_call" | custom-call | flops 4294967296 | bytes 4194304 | tf_op jit(solution)/shard_map/send_order/pallas_call | solution.py:166
  6.5 0.0 copy-start.10
  6.5 0.0 copy-start.12
  6.5 0.0 copy-start.11
  6.5 0.0 copy-start
  6.5 7.5 %all-to-all-start = ((bf16[16,528,128]{2,1,0:T(8,128)(2,1)}), bf16[16,528,128]{2,1,0:T(8,128)(2,1)S(1)}, u32[]{:S(2)}, u32[]{:S(2)}) async-start(bf16[16,528,128]{2,1,0:T(8,128)(2,1)} %get-tuple-element.28), calls=%async_computation | async-start | bytes 4325376 | tf_op jit(solution)/shard_map/all_to_all | solution.py:637
  14.0 0.0 copy-done.10
  14.0 0.2 copy.23
  14.2 0.0 copy-done.12
  14.2 0.1 broadcast_in_dim.40
  14.3 0.1 broadcast_in_dim_reshape.3.scale_ref
  14.4 0.0 copy-done.11
  14.4 0.1 copy.22
  14.5 0.1 reshape.20.chosen_ref
  14.6 1.3 copy.24
  15.8 40.7 %all-to-all-done.arrived_ref = bf16[16,528,128]{2,1,0:T(8,128)(2,1)S(1)} async-done(((bf16[16,528,128]{2,1,0:T(8,128)(2,1)}), bf16[16,528,128]{2,1,0:T(8,128)(2,1)S(1)}, u32[]{:S(2)}, u32[]{:S(2)}) %all-to-all-start) | async-done | bytes 2162720 | tf_op jit(solution)/shard_map/all_to_all | solution.py:637
  56.6 0.0 copy-done
  56.6 2.1 %pool_arrived.1 = (bf16[2048,512]{1,0:T(8,128)(2,1)S(1)}, f32[16,128]{1,0:T(8,128)S(1)}, s32[16,128]{1,0:T(8,128)S(1)}, bf16[256,512]{1,0:T(8,128)(2,1)S(1)}) custom-call(bf16[16,528,128]{2,1,0:T(8,128)(2,1)S(1)} %all-to-all-done.arrived_ref, f32[1,512]{1,0:T(1,128)S(1)} %bitcast.30), custom_call_target="tpu_custom_call" | custom-call | flops 536870912 | bytes 4194304 | tf_op jit(solution)/shard_map/pool_arrived/pallas_call | solution.py:251
  58.7 6.1 %collective-permute-start = (bf16[256,512]{1,0:T(8,128)(2,1)S(1)}, bf16[256,512]{1,0:T(8,128)(2,1)S(1)}, u32[]{:S(2)}, u32[]{:S(2)}) collective-permute-start(bf16[256,512]{1,0:T(8,128)(2,1)S(1)} %get-tuple-element.30), channel_id=1, source_target_pairs={{0,8},{2,10},{4,12},{6,14},{8,16},{10,18},{12,20},{14,22},{16,24},... | collective-permute-start | bytes 786440 | tf_op jit(solution)/shard_map/ppermute | solution.py:588
  64.8 0.2 collective-permute-start.1
  65.0 3.6 %collective-permute-start.2 = (bf16[256,512]{1,0:T(8,128)(2,1)S(1)}, bf16[256,512]{1,0:T(8,128)(2,1)S(1)}, u32[]{:S(2)}, u32[]{:S(2)}) collective-permute-start(bf16[256,512]{1,0:T(8,128)(2,1)S(1)} %get-tuple-element.30), channel_id=1, source_target_pairs={{0,4},{2,6},{4,0},{6,2},{8,12},{10,14},{12,8},{14,10},{16,20},{18,... | collective-permute-start | bytes 786440 | tf_op jit(solution)/shard_map/ppermute | solution.py:588
  68.6 0.0 copy-start.4
  68.6 0.0 copy-start.5
  68.7 5.5 %group_balls.1 = (bf16[2048,512]{1,0:T(8,128)(2,1)S(1)}, bf16[2048,512]{1,0:T(8,128)(2,1)S(1)}) custom-call(f32[16,128]{1,0:T(8,128)S(1)} %get-tuple-element.31.ids_ref, bf16[2048,512]{1,0:T(8,128)(2,1)S(1)} %get-tuple-element.32.source_ref, f32[1,512]{1,0:T(1,128)S(1)} %bitcast.31), custom_call_target="tpu_custom_call" | custom-call | flops 4294967296 | bytes 6291456 | tf_op jit(solution)/shard_map/group_balls/pallas_call | solution.py:284
  74.1 0.0 copy-done.4
  74.1 0.0 copy-done.5
  74.2 8.0 %local_attention.2 = (bf16[2048,512]{1,0:T(8,128)(2,1)S(1)}, bf16[2048,512]{1,0:T(8,128)(2,1)S(1)}, bf16[2048,512]{1,0:T(8,128)(2,1)S(1)}) custom-call(f32[1,512]{1,0:T(1,128)S(1)} %broadcast_in_dim_reshape.3.scale_ref, bf16[2048,512]{1,0:T(8,128)(2,1)S(1)} %get-tuple-element.33.normed_ref, bf16[512,512]{1,0:T(8,128)(2,1)S(1)} %copy-done.4, ...), custom_call_target="tpu_custom_call" | custom-call | flops 5368709120 | bytes 6291456 | tf_op jit(solution)/shard_map/local_attention/pallas_call | solution.py:372
  82.2 0.0 collective-permute-done
  82.2 0.0 collective-permute-done.1
  82.3 0.0 collective-permute-done.2
  82.3 0.1 pad_maximum_fusion
  82.4 0.8 collective-permute-start.4
  83.2 0.0 collective-permute-start.3
  83.2 8.0 %local_attention.3 = (bf16[2048,512]{1,0:T(8,128)(2,1)S(1)}, bf16[2048,512]{1,0:T(8,128)(2,1)S(1)}, bf16[2048,512]{1,0:T(8,128)(2,1)S(1)}) custom-call(f32[1,512]{1,0:T(1,128)S(1)} %broadcast_in_dim_reshape.3.scale_ref, bf16[2048,512]{1,0:T(8,128)(2,1)S(1)} %get-tuple-element.33.normed_ref, ...), custom_call_target="tpu_custom_call", output_to_operand_aliasing={{0}: (5, {}), {1}: (6, {}), {2}: (7, {})} | custom-call | flops 5368709120 | bytes 6291456 | tf_op jit(solution)/shard_map/local_attention/pallas_call | solution.py:372
  91.3 0.0 copy-start.1
  91.3 0.0 copy-start.2
  91.3 0.0 copy-start.3
  91.3 0.0 copy-start.6
  91.3 0.0 copy-start.7
  91.3 0.0 copy-start.8
  91.4 0.0 collective-permute-done.3
  91.4 0.5 collective-permute-start.5
  92.0 0.0 collective-permute-done.4
  92.0 0.1 constant_dynamic-update-slice_fusion
  92.1 1.1 collective-permute-done.5
  93.2 0.0 copy-done.1
  93.2 0.0 copy-done.2
  93.2 0.0 copy-done.3
  93.2 0.1 copy-done.6
  93.3 0.2 copy-done.7
  93.4 0.0 copy-done.8
  93.4 19.0 %finish_balls.1 = bf16[2048,512]{1,0:T(8,128)(2,1)S(1)} custom-call(s32[32]{0:T(128)S(1)} %reshape.20.chosen_ref, s32[16,128]{1,0:T(8,128)S(1)} %get-tuple-element.29.places_ref, bf16[72,32,512]{2,1,0:T(8,128)(2,1)S(1)} %bitcast.29, bf16[2048,512]{1,0:T(8,128)(2,1)S(1)} %get-tuple-element.45.query_ref, bf16[2048,512]{1,0:T(8,128)(2,1)S(1)} %get-tuple-element.46.num_ref, ...), custom_call_target="tpu_custom_call" | custom-call | flops 12884901888 | bytes 12582912 | tf_op jit(solution)/shard_map/finish_balls/pallas_call | solution.py:521
  112.5 0.0 copy-start.9
  112.5 52.1 %all_to_all.10 = bf16[16,128,512]{2,1,0:T(8,128)(2,1)S(1)} all-to-all(bf16[16,128,512]{2,1,0:T(8,128)(2,1)S(1)} %bitcast.23), channel_id=1, replica_groups=mesh['pts'=16,'rep'=2] {'pts'}, dimensions={0} | all-to-all | bytes 4194304 | tf_op jit(solution)/shard_map/all_to_all | solution.py:637
  164.6 0.0 copy-done.9
  164.6 4.5 %take_rows.1 = bf16[2048,512]{1,0:T(8,128)(2,1)} custom-call(s32[16,128]{1,0:T(8,128)S(1)} %copy-done.9, bf16[2048,512]{1,0:T(8,128)(2,1)S(1)} %bitcast.24), custom_call_target="tpu_custom_call" | custom-call | flops 4294967296 | bytes 4194304 | tf_op jit(solution)/shard_map/take_rows/pallas_call | solution.py:565
  (9 shorter events, 0.2 us)
Async XLA Ops:
  6.5 7.5 %copy-start.10 = (bf16[512,512]{1,0:T(8,128)(2,1)S(1)}, bf16[512,512]{1,0:T(8,128)(2,1)}, u32[]{:S(2)}) copy-start(bf16[512,512]{1,0:T(8,128)(2,1)} %param.20) | copy-start | bytes 1572868
  6.5 7.7 %copy-start.12 = (f32[16]{0:T(128)S(1)}, f32[16]{0:T(128)}, u32[]{:S(2)}) copy-start(f32[16]{0:T(128)} %param.24) | copy-start | bytes 196
  6.5 7.9 %copy-start.11 = (s32[8,4]{0,1:T(4,128)S(1)}, s32[8,4]{0,1:T(4,128)}, u32[]{:S(2)}) copy-start(s32[8,4]{0,1:T(4,128)} %param.17) | copy-start | bytes 388
  6.5 50.1 %copy-start = (f32[512]{0:T(512)S(1)}, f32[512]{0:T(512)}, u32[]{:S(2)}) copy-start(f32[512]{0:T(512)} %param.18) | copy-start | bytes 6148
  6.5 50.1 %all-to-all-start = ((bf16[16,528,128]{2,1,0:T(8,128)(2,1)}), bf16[16,528,128]{2,1,0:T(8,128)(2,1)S(1)}, u32[]{:S(2)}, u32[]{:S(2)}) async-start(bf16[16,528,128]{2,1,0:T(8,128)(2,1)} %get-tuple-element.28), calls=%async_computation | async-start | bytes 4325376 | tf_op jit(solution)/shard_map/all_to_all | solution.py:637
  58.7 23.5 %collective-permute-start = (bf16[256,512]{1,0:T(8,128)(2,1)S(1)}, bf16[256,512]{1,0:T(8,128)(2,1)S(1)}, u32[]{:S(2)}, u32[]{:S(2)}) collective-permute-start(bf16[256,512]{1,0:T(8,128)(2,1)S(1)} %get-tuple-element.30), channel_id=1, source_target_pairs={{0,8},{2,10},{4,12},{6,14},{8,16},{10,18},{12,20},{14,22},{16,24},... | collective-permute-start | bytes 786440 | tf_op jit(solution)/shard_map/ppermute | solution.py:588
  64.8 17.4 %collective-permute-start.1 = (bf16[256,512]{1,0:T(8,128)(2,1)S(1)}, bf16[256,512]{1,0:T(8,128)(2,1)S(1)}, u32[]{:S(2)}, u32[]{:S(2)}) collective-permute-start(bf16[256,512]{1,0:T(8,128)(2,1)S(1)} %get-tuple-element.30), channel_id=1, source_target_pairs={{0,24},{2,26},{4,28},{6,30},{8,0},{10,2},{12,4},{14,6},{16,8},{18,... | collective-permute-start | bytes 786440 | tf_op jit(solution)/shard_map/ppermute | solution.py:588
  65.0 17.2 %collective-permute-start.2 = (bf16[256,512]{1,0:T(8,128)(2,1)S(1)}, bf16[256,512]{1,0:T(8,128)(2,1)S(1)}, u32[]{:S(2)}, u32[]{:S(2)}) collective-permute-start(bf16[256,512]{1,0:T(8,128)(2,1)S(1)} %get-tuple-element.30), channel_id=1, source_target_pairs={{0,4},{2,6},{4,0},{6,2},{8,12},{10,14},{12,8},{14,10},{16,20},{18,... | collective-permute-start | bytes 786440 | tf_op jit(solution)/shard_map/ppermute | solution.py:588
  68.6 5.5 %copy-start.4 = (bf16[512,512]{1,0:T(8,128)(2,1)S(1)}, bf16[512,512]{1,0:T(8,128)(2,1)}, u32[]{:S(2)}) copy-start(bf16[512,512]{1,0:T(8,128)(2,1)} %wq_ref.3) | copy-start | bytes 1572868
  68.6 5.5 %copy-start.5 = (bf16[512,512]{1,0:T(8,128)(2,1)S(1)}, bf16[512,512]{1,0:T(8,128)(2,1)}, u32[]{:S(2)}) copy-start(bf16[512,512]{1,0:T(8,128)(2,1)} %wv_ref.3) | copy-start | bytes 1572868
  82.4 9.6 %collective-permute-start.4 = (bf16[3,256,512]{2,1,0:T(8,128)(2,1)S(1)}, bf16[3,256,512]{2,1,0:T(8,128)(2,1)S(1)}, u32[]{:S(2)}, u32[]{:S(2)}) collective-permute-start(bf16[3,256,512]{2,1,0:T(8,128)(2,1)S(1)} %pad_maximum_fusion), channel_id=1, source_target_pairs={{0,2},{2,0},{4,6},{6,4},{8,10},{10,8},{12,14},{14,12},{16,18},{18,... | collective-permute-start | bytes 2359304 | tf_op jit(solution)/shard_map/ppermute | solution.py:588
  83.2 8.2 %collective-permute-start.3 = (bf16[256,512]{1,0:T(8,128)(2,1)S(1)}, bf16[256,512]{1,0:T(8,128)(2,1)S(1)}, u32[]{:S(2)}, u32[]{:S(2)}) collective-permute-start(bf16[256,512]{1,0:T(8,128)(2,1)S(1)} %get-tuple-element.50), channel_id=1, source_target_pairs={{0,4},{2,6},{4,0},{6,2},{8,12},{10,14},{12,8},{14,10},{16,20},{18,... | collective-permute-start | bytes 786440 | tf_op jit(solution)/shard_map/ppermute | solution.py:588
  91.3 1.9 %copy-start.1 = (bf16[512,1024]{1,0:T(8,128)(2,1)S(1)}, bf16[512,1024]{1,0:T(8,128)(2,1)}, u32[]{:S(2)}) copy-start(bf16[512,1024]{1,0:T(8,128)(2,1)} %wg_ref.1) | copy-start | bytes 3145732
  91.3 1.9 %copy-start.2 = (bf16[512,1024]{1,0:T(8,128)(2,1)S(1)}, bf16[512,1024]{1,0:T(8,128)(2,1)}, u32[]{:S(2)}) copy-start(bf16[512,1024]{1,0:T(8,128)(2,1)} %wu_ref.1) | copy-start | bytes 3145732
  91.3 1.9 %copy-start.3 = (bf16[1024,512]{1,0:T(8,128)(2,1)S(1)}, bf16[1024,512]{1,0:T(8,128)(2,1)}, u32[]{:S(2)}) copy-start(bf16[1024,512]{1,0:T(8,128)(2,1)} %wd_ref.1) | copy-start | bytes 3145732
  91.3 2.0 %copy-start.6 = (bf16[512,512]{1,0:T(8,128)(2,1)S(1)}, bf16[512,512]{1,0:T(8,128)(2,1)}, u32[]{:S(2)}) copy-start(bf16[512,512]{1,0:T(8,128)(2,1)} %wpv_ref.1) | copy-start | bytes 1572868
  91.3 2.1 %copy-start.7 = (bf16[512,512]{1,0:T(8,128)(2,1)S(1)}, bf16[512,512]{1,0:T(8,128)(2,1)}, u32[]{:S(2)}) copy-start(bf16[512,512]{1,0:T(8,128)(2,1)} %wo_ref.1) | copy-start | bytes 1572868
  91.3 2.1 %copy-start.8 = (f32[512]{0:T(512)S(1)}, f32[512]{0:T(512)}, u32[]{:S(2)}) copy-start(f32[512]{0:T(512)} %param.26) | copy-start | bytes 6148
  91.4 1.7 %collective-permute-start.5 = (bf16[256,512]{1,0:T(8,128)(2,1)S(1)}, bf16[256,512]{1,0:T(8,128)(2,1)S(1)}, u32[]{:S(2)}, u32[]{:S(2)}) collective-permute-start(bf16[256,512]{1,0:T(8,128)(2,1)S(1)} %collective-permute-done.3), channel_id=1, source_target_pairs={{0,2},{2,0},{4,6},{6,4},{8,10},{10,8},{12,14},{14,12},{16,18},{18,... | collective-permute-start | bytes 786440 | tf_op jit(solution)/shard_map/ppermute | solution.py:588
  112.5 52.1 %copy-start.9 = (s32[16,128]{1,0:T(8,128)S(1)}, s32[16,128]{1,0:T(8,128)}, u32[]{:S(2)}) copy-start(s32[16,128]{1,0:T(8,128)} %get-tuple-element.27.places_ref) | copy-start | bytes 24580

commit v6 on v5

--- a/solution.py
+++ b/solution.py
@@ -47,23 +47,6 @@
 
 def row_blocks(rows, width):
     return pl.BlockSpec((rows, width), lambda i, *_: (i, 0))
-
-
-def picked_rows(pick_tile, rows, source_ref):
-    count = source_ref.shape[0]
-    total = None
-    for start in range(0, count, DEPTH):
-        pick = jnp.concatenate(
-            [pick_tile(t) for t in range(start // LANES, (start + DEPTH) // LANES)], axis=1
-        )
-        part = dot(pick, source_ref[start : start + DEPTH, :])
-        total = part if total is None else total + part
-    return total
-
-
-def by_lane_ids(ids_ref, first, rows):
-    targets = (lax.broadcasted_iota(jnp.int32, (rows, LANES), 0) + first).astype(F32)
-    return lambda t: jnp.where(ids_ref[t : t + 1, :] == targets, 1.0, 0.0).astype(BF16)
 
 
 def chunk_rows(ref, first, rows, chunk, pitch):
@@ -200,42 +183,35 @@
     return (rows32 * lax.rsqrt(mean_square + 1e-05) * gain).astype(BF16)
 
 
-def pool_kernel(arrived_ref, gain_ref, source_ref, ids_ref, places_ref, pooled_ref, ids, total):
-    peers = arrived_ref.shape[0]
-    rows, width = source_ref.shape
+def pool_kernel(arrived_ref, gain_ref, rows_ref, places_ref, pooled_ref, total):
+    peers, payload, _ = arrived_ref.shape
+    width = gain_ref.shape[1]
     chunks = width // LANES
-    send_each = rows // peers
+    send_each = (payload - 16) // chunks
     per_tile = LANES // send_each
+    tiles = peers // per_tile
     step = pl.program_id(0)
 
     @pl.when(step == 0)
     def _():
         total[...] = jnp.zeros_like(total)
 
-    for t in range(rows // LANES):
+    pool = lax.broadcasted_iota(jnp.int32, (total.shape[0], LANES), 0).astype(F32)
+    picks = []
+    normed = []
+    for t in range(tiles):
         row = jnp.zeros((1, LANES), F32)
         for p in range(t * per_tile, (t + 1) * per_tile):
             both = arrived_ref[p, chunks * send_each :, :].astype(F32)
             row = row + both[0:1, :] * LOW + both[1:2, :]
-        ids[t : t + 1, :] = row
-        ids_ref[pl.ds(step * (rows // LANES) + t, 1), :] = row
-        places_ref[pl.ds(step * (rows // LANES) + t, 1), :] = (row * chunks).astype(jnp.int32)
+        places_ref[pl.ds(step * tiles + t, 1), :] = (row * chunks).astype(jnp.int32)
+        picks.append(jnp.where(jnp.floor(row * (1.0 / POOL)) == pool, 1.0 / POOL, 0.0).astype(BF16))
     for p in range(peers):
+        parts = [arrived_ref[p, c * send_each : (c + 1) * send_each, :].astype(F32) for c in range(chunks)]
         for c in range(chunks):
-            source_ref[p * send_each : (p + 1) * send_each, c * LANES : (c + 1) * LANES] = arrived_ref[
-                p, c * send_each : (c + 1) * send_each, :
-            ]
-    normed = normed_rows(source_ref[...].astype(F32), gain_ref[...])
-    pools = total.shape[0]
-    pool = lax.broadcasted_iota(jnp.int32, (pools, LANES), 0).astype(F32)
-    pick = jnp.concatenate(
-        [
-            jnp.where(jnp.floor(ids[t : t + 1, :] * (1.0 / POOL)) == pool, 1.0 / POOL, 0.0).astype(BF16)
-            for t in range(rows // LANES)
-        ],
-        axis=1,
-    )
-    total[...] += dot(pick, normed)
+            chunk_rows(rows_ref, p * send_each, send_each, c, chunks)[...] = parts[c]
+        normed.append(normed_rows(jnp.concatenate(parts, axis=1), gain_ref[...]))
+    total[...] += dot(jnp.concatenate(picks, axis=1), jnp.concatenate(normed, axis=0))
 
     @pl.when(step == pl.num_programs(0) - 1)
     def _():
@@ -244,6 +220,7 @@
 
 def pool(arrived, gain, rows_dev):
     width = gain.shape[1]
+    chunks = width // LANES
     tiles = rows_dev // LANES
     peers, payload, _ = arrived.shape
     steps = rows_dev // TILE
@@ -255,14 +232,13 @@
             pl.BlockSpec((peers // steps, payload, LANES), lambda i: (i, 0, 0)),
             whole((1, width)),
         ],
-        out_specs=[row_blocks(TILE, width), kept((tiles, LANES)), kept((tiles, LANES)), kept(pooled)],
+        out_specs=[row_blocks(TILE * chunks, LANES), kept((tiles, LANES)), kept(pooled)],
         out_shape=[
-            jax.ShapeDtypeStruct((rows_dev, width), BF16),
-            jax.ShapeDtypeStruct((tiles, LANES), F32),
+            jax.ShapeDtypeStruct((rows_dev * chunks, LANES), F32),
             jax.ShapeDtypeStruct((tiles, LANES), jnp.int32),
             jax.ShapeDtypeStruct(pooled, BF16),
         ],
-        scratch_shapes=[pltpu.VMEM((TILE // LANES, LANES), F32), pltpu.VMEM(pooled, F32)],
+        scratch_shapes=[pltpu.VMEM(pooled, F32)],
         compiler_params=params(),
         cost_estimate=pl.CostEstimate(
             flops=rows_dev * rows_dev * width // 4, bytes_accessed=4 * rows_dev * width, transcendentals=0
@@ -271,28 +247,42 @@
     )(arrived, gain)
 
 
-def group_kernel(ids_ref, source_ref, gain_ref, grouped_ref, normed_ref):
-    tile = by_lane_ids(ids_ref, pl.program_id(0) * TILE, TILE)
-    grouped = picked_rows(tile, TILE, source_ref)
+def group_kernel(places_ref, rows_ref, gain_ref, grouped_ref, normed_ref, placed):
+    count, width = grouped_ref.shape
+    chunks = width // LANES
+    step = pl.program_id(0)
+
+    @pl.when(step == 0)
+    def _():
+        scatter_rows(places_ref, places_ref.shape[0], rows_ref, placed, chunks)
+
+    grouped = jnp.concatenate(
+        [chunk_rows(placed, step * count, count, c, chunks)[...] for c in range(chunks)], axis=1
+    )
     grouped_ref[...] = grouped.astype(BF16)
     normed_ref[...] = normed_rows(grouped, gain_ref[...])
 
 
-def group(ids, source, gain):
-    rows_dev, width = source.shape
-    rows = row_blocks(TILE, width)
+def group(places, rows, gain):
+    width = gain.shape[1]
+    rows_dev = rows.shape[0] * LANES // width
+    blocks = row_blocks(TILE, width)
     return pl.pallas_call(
         group_kernel,
-        grid=(rows_dev // TILE,),
-        in_specs=[whole(ids.shape), whole(source.shape), whole((1, width))],
-        out_specs=[rows, rows],
+        grid_spec=pltpu.PrefetchScalarGridSpec(
+            num_scalar_prefetch=1,
+            grid=(rows_dev // TILE,),
+            in_specs=[whole(rows.shape), whole((1, width))],
+            out_specs=[blocks, blocks],
+            scratch_shapes=[pltpu.VMEM(rows.shape, F32)],
+        ),
         out_shape=[jax.ShapeDtypeStruct((rows_dev, width), BF16)] * 2,
         compiler_params=params(),
         cost_estimate=pl.CostEstimate(
             flops=2 * rows_dev * rows_dev * width, bytes_accessed=6 * rows_dev * width, transcendentals=0
         ),
         name="group_balls",
-    )(ids, source, gain)
+    )(places, rows, gain)
 
 
 def block_matrix(rows, row_step, cols, col_step, value):
@@ -301,95 +291,118 @@
     return jnp.where(row == col, value, 0.0).astype(BF16)
 
 
-def clear_spread(head_size, keys_ref, values_ref):
-    keys_ref[...] = jnp.zeros_like(keys_ref)
-    ones = block_matrix(values_ref.shape[1], values_ref.shape[1] * head_size // LANES, LANES, head_size, 1.0)
-    for g in range(values_ref.shape[0]):
-        values_ref[g, :, LANES:] = ones
-
-
-def spread_keys(head_size, columns, ref):
+def prepare(head_size, mean_of, queries, values):
+    half = mean_of.shape[0]
+    mean_of[...] = block_matrix(half, head_size, half, head_size, 1.0 / head_size)
+    queries[...] = jnp.zeros_like(queries)
+    values[...] = jnp.ones_like(values)
+
+
+def normed_keys(keys, mean_of):
+    half = mean_of.shape[0]
+    square = (keys * keys).astype(BF16)
+    mean_square = jnp.concatenate(
+        [dot(square[:, c : c + half], mean_of[...]) for c in range(0, keys.shape[1], half)], axis=1
+    )
+    return (keys * lax.rsqrt(mean_square + 1e-06)).astype(BF16)
+
+
+def spread_head(h, head_size, columns, queries):
     count = columns.shape[1]
     per_group = LANES // head_size
-    for h in range(columns.shape[0] // head_size):
-        g, j = h // per_group, h % per_group
-        part = columns[h * head_size : (h + 1) * head_size, :]
+    g, j = h // per_group, h % per_group
+    queries[g, j * head_size : (j + 1) * head_size, j * count : (j + 1) * count] = columns
+
+
+def weigh(key_rows, queries, weights):
+    for g in range(queries.shape[0]):
+        score = dot(key_rows[:, g * LANES : (g + 1) * LANES], queries[g])
+        weights[g] = jnp.exp2(score).astype(BF16)
+
+
+def head_sums(g, head_size, values, weights):
+    per_group = LANES // head_size
+    both = dot(values[g], weights[g])
+    count = both.shape[1] // per_group
+    for j in range(per_group):
+        cols = slice(j * count, (j + 1) * count)
+        yield g * per_group + j, both[j * head_size : (j + 1) * head_size, cols], both[LANES : LANES + 1, cols]
+
+
+def local_kernel(head_size, scale_ref, normed_ref, wq_ref, wk_ref, wv_ref, *rest):
+    query_ref, num_ref, den_ref, mean_of, queries, values, weights = rest[-7:]
+    width = normed_ref.shape[1]
+    groups = width // LANES
+    balls = queries.shape[0]
+
+    @pl.when(pl.program_id(0) == 0)
+    def _():
+        prepare(head_size, mean_of, queries, values)
+
+    normed = normed_ref[...]
+    query = dot_nt(wq_ref[...], normed)
+    key_rows = normed_keys(dot(normed, wk_ref[...]), mean_of)
+    value = dot_nt(wv_ref[...], normed).astype(BF16)
+    for h in range(width // head_size):
+        rows = slice(h * head_size, (h + 1) * head_size)
+        part = query[rows, :]
         root = lax.rsqrt(jnp.mean(part * part, axis=0, keepdims=True) + 1e-06)
-        ref[g, j * head_size : (j + 1) * head_size, j * count : (j + 1) * count] = (part * root).astype(BF16)
-
-
-def spread_values(head_size, values, ref):
-    count, width = values.shape
-    head = lax.broadcasted_iota(jnp.int32, (count, LANES), 1) // head_size
-    for g in range(width // LANES):
-        lanes = values[:, g * LANES : (g + 1) * LANES]
-        for j in range(LANES // head_size):
-            ref[g, j * count : (j + 1) * count, :LANES] = jnp.where(head == j, lanes, jnp.zeros((), BF16))
-
-
-def local_kernel(head_size, scale_ref, normed_ref, wq_ref, wk_ref, wv_ref, *rest):
-    query_ref, num_ref, den_ref, mean_of, keys, values, weights = rest[-7:]
-    width = normed_ref.shape[1]
-    half = mean_of.shape[0]
-
-    @pl.when(pl.program_id(0) == 0)
-    def _():
-        mean_of[...] = block_matrix(half, head_size, half, head_size, 1.0 / head_size)
-        clear_spread(head_size, keys, values)
-
-    normed = normed_ref[...]
-    query = dot(normed, wq_ref[...])
-    square = query * query
-    high = square.astype(BF16)
-    low = (square - high.astype(F32)).astype(BF16)
-    mean_square = jnp.concatenate(
-        [
-            dot(high[:, c : c + half], mean_of[...]) + dot(low[:, c : c + half], mean_of[...])
-            for c in range(0, width, half)
-        ],
-        axis=1,
-    )
-    query = (query * lax.rsqrt(mean_square + 1e-06) * scale_ref[...]).astype(BF16)
-    query_ref[...] = query
-    spread_keys(head_size, dot_nt(wk_ref[...], normed), keys)
-    spread_values(head_size, dot(normed, wv_ref[...]).astype(BF16), values)
-    groups = width // LANES
-    for g in range(groups):
-        weights[g] = jnp.exp2(dot(query[:, g * LANES : (g + 1) * LANES], keys[g])).astype(BF16)
-    for g in range(groups):
-        both = dot(weights[g], values[g])
-        num_ref[:, g * LANES : (g + 1) * LANES] = both[:, :LANES].astype(BF16)
-        den_ref[:, g * LANES : (g + 1) * LANES] = both[:, LANES:].astype(BF16)
-
-
-def local_attention(part, parts, normed, wq, wk, wv, scale, head_size, earlier=()):
+        part = (part * (root * scale_ref[h])).astype(BF16)
+        query_ref[rows, :] = part
+        for b in range(balls):
+            spread_head(h, head_size, part[:, b * BALL : (b + 1) * BALL], queries.at[b])
+    for b in range(balls):
+        cols = slice(b * BALL, (b + 1) * BALL)
+        for g in range(groups):
+            values[b, g, :LANES, :] = value[g * LANES : (g + 1) * LANES, cols]
+        weigh(key_rows[cols, :], queries.at[b], weights.at[b])
+    for b in range(balls):
+        cols = slice(b * BALL, (b + 1) * BALL)
+        for g in range(groups):
+            for h, num, den in head_sums(g, head_size, values.at[b], weights.at[b]):
+                num_ref[h * head_size : (h + 1) * head_size, cols] = num.astype(BF16)
+                den_ref[h : h + 1, cols] = den
+
+
+def local_attention(first, last, normed, wq, wk, wv, scale, head_size, earlier=()):
     rows_dev, width = normed.shape
     square = whole((width, width))
     groups = width // LANES
+    heads = width // head_size
     spread = LANES // head_size * BALL
-    steps = rows_dev // BALL // parts
-    rows = pl.BlockSpec((BALL, width), lambda i: (part * steps + i, 0))
+    balls = math.gcd(math.gcd(first, last), BALLS_STEP)
+    steps = (last - first) // balls
+    at = lambda i: first // balls + i
+    columns = lambda count: pl.BlockSpec((count, balls * BALL), lambda i: (0, at(i)))
     return pl.pallas_call(
         functools.partial(local_kernel, head_size),
         grid=(steps,),
-        in_specs=[whole((1, width)), rows, square, square, square]
+        in_specs=[
+            pl.BlockSpec(memory_space=pltpu.SMEM),
+            pl.BlockSpec((balls * BALL, width), lambda i: (at(i), 0)),
+            square,
+            square,
+            square,
+        ]
         + [pl.BlockSpec(memory_space=pl.ANY)] * len(earlier),
-        out_specs=[rows] * 3,
+        out_specs=[columns(width), columns(width), columns(heads)],
         out_shape=[
-            jax.ShapeDtypeStruct((rows_dev, width), BF16),
-            jax.ShapeDtypeStruct((rows_dev, width), BF16),
-            jax.ShapeDtypeStruct((rows_dev, width), BF16),
+            jax.ShapeDtypeStruct((width, rows_dev), BF16),
+            jax.ShapeDtypeStruct((width, rows_dev), BF16),
+            jax.ShapeDtypeStruct((heads, rows_dev), F32),
         ],
         scratch_shapes=[
             pltpu.VMEM((2 * LANES, 2 * LANES), BF16),
-            pltpu.VMEM((groups, LANES, spread), BF16),
-            pltpu.VMEM((groups, spread, 2 * LANES), BF16),
-            pltpu.VMEM((groups, BALL, spread), BF16),
+            pltpu.VMEM((balls, groups, LANES, spread), BF16),
+            pltpu.VMEM((balls, groups, LANES + 16, BALL), BF16),
+            pltpu.VMEM((balls, groups, BALL, spread), BF16),
         ],
         input_output_aliases={5 + k: k for k in range(len(earlier))},
         compiler_params=params(),
         cost_estimate=pl.CostEstimate(
-            flops=20 * rows_dev * width * width // parts, bytes_accessed=12 * rows_dev * width // parts, transcendentals=0
+            flops=20 * (last - first) * BALL * width * width,
+            bytes_accessed=12 * (last - first) * BALL * width,
+            transcendentals=0,
         ),
         name="local_attention",
     )(scale, normed, wq, wk, wv, *earlier)
@@ -412,7 +425,8 @@
     wu_ref,
     wd_ref,
     out_ref,
-    keys,
+    mean_of,
+    queries,
     values,
     weights,
     attended,
@@ -421,14 +435,14 @@
 ):
     step = pl.program_id(0)
     steps = pl.num_programs(0) - TAKE_STEPS
-    step_rows, width = attended.shape
+    width, step_rows = attended.shape
     chunks = width // LANES
 
     @pl.when(step < steps)
     def _():
         result = balls_step(
             head_size, step, chosen_ref, candidates_ref, query_ref, num_ref, den_ref, grouped_ref, wpk_ref,
-            wpv_ref, wo_ref, gain_ref, wg_ref, wu_ref, wd_ref, keys, values, weights, attended,
+            wpv_ref, wo_ref, gain_ref, wg_ref, wu_ref, wd_ref, mean_of, queries, values, weights, attended,
         )
         for c in range(chunks):
             part = result[:, c * LANES : (c + 1) * LANES].astype(BF16).astype(F32)
@@ -463,7 +477,8 @@
     wg_ref,
     wu_ref,
     wd_ref,
-    keys,
+    mean_of,
+    queries,
     values,
     weights,
     attended,
@@ -473,32 +488,29 @@
 
     @pl.when(step == 0)
     def _():
-        for b in range(BALLS_STEP):
-            clear_spread(head_size, keys.at[b], values.at[b])
+        prepare(head_size, mean_of, queries, values)
 
     first = step * BALLS_STEP * OWNERS
     coarse = jnp.concatenate(
         [candidates_ref[chosen_ref[first + o]] for o in range(BALLS_STEP * OWNERS)], axis=0
     )
-    key_columns = dot_nt(wpk_ref[...], coarse)
-    value_rows = dot(coarse, wpv_ref[...]).astype(BF16)
+    key_rows = normed_keys(dot(coarse, wpk_ref[...]), mean_of)
+    value = dot_nt(wpv_ref[...], coarse).astype(BF16)
     for b in range(BALLS_STEP):
-        spread_keys(head_size, key_columns[:, b * far : (b + 1) * far], keys.at[b])
-        spread_values(head_size, value_rows[b * far : (b + 1) * far, :], values.at[b])
+        cols = slice(b * BALL, (b + 1) * BALL)
+        for h in range(groups * LANES // head_size):
+            spread_head(h, head_size, query_ref[h * head_size : (h + 1) * head_size, cols], queries.at[b])
+        for g in range(groups):
+            values[b, g, :LANES, :] = value[g * LANES : (g + 1) * LANES, b * far : (b + 1) * far]
+        weigh(key_rows[b * far : (b + 1) * far, :], queries.at[b], weights.at[b])
     for b in range(BALLS_STEP):
-        rows = slice(b * BALL, (b + 1) * BALL)
+        cols = slice(b * BALL, (b + 1) * BALL)
         for g in range(groups):
-            score = dot(query_ref[rows, g * LANES : (g + 1) * LANES], keys[b, g])
-            weights[b, g] = jnp.exp2(score).astype(BF16)
-    for b in range(BALLS_STEP):
-        rows = slice(b * BALL, (b + 1) * BALL)
-        for g in range(groups):
-            lanes = slice(g * LANES, (g + 1) * LANES)
-            both = dot(weights[b, g], values[b, g])
-            num = both[:, :LANES] + num_ref[rows, lanes].astype(F32)
-            den = both[:, LANES:] + den_ref[rows, lanes].astype(F32)
-            attended[rows, lanes] = (num / den).astype(BF16)
-    projected = dot(attended[...], wo_ref[...])
+            for h, num, den in head_sums(g, head_size, values.at[b], weights.at[b]):
+                rows = slice(h * head_size, (h + 1) * head_size)
+                num = num + num_ref[rows, cols].astype(F32)
+                attended[rows, cols] = (num * (1.0 / (den + den_ref[h : h + 1, cols]))).astype(BF16)
+    projected = dot(attended[...].T, wo_ref[...])
     residual = (grouped_ref[...].astype(F32) + projected).astype(BF16)
     rows32 = residual.astype(F32)
     ffn = normed_rows(rows32, gain_ref[...])
@@ -513,9 +525,11 @@
     hidden = wg.shape[1]
     groups = width // LANES
     step_rows = BALLS_STEP * BALL
-    spread = LANES // head_size * OWNERS * BALL // POOL
+    spread = LANES // head_size * BALL
+    far = OWNERS * BALL // POOL
     steps = rows_dev // step_rows
     rows = pl.BlockSpec((step_rows, width), lambda i, *_: (jnp.minimum(i, steps - 1), 0))
+    columns = lambda count: pl.BlockSpec((count, step_rows), lambda i, *_: (0, jnp.minimum(i, steps - 1)))
     take_rows = rows_dev // TAKE_STEPS
     fixed = [wpk, wpv, wo, gain, wg, wu, wd]
     return pl.pallas_call(
@@ -523,13 +537,21 @@
         grid_spec=pltpu.PrefetchScalarGridSpec(
             num_scalar_prefetch=2,
             grid=(steps + TAKE_STEPS,),
-            in_specs=[whole(candidates.shape), rows, rows, rows, rows] + [whole(a.shape) for a in fixed],
+            in_specs=[
+                whole(candidates.shape),
+                columns(width),
+                columns(width),
+                columns(width // head_size),
+                rows,
+            ]
+            + [whole(a.shape) for a in fixed],
             out_specs=pl.BlockSpec((take_rows, width), lambda i, *_: (jnp.maximum(i - steps, 0), 0)),
             scratch_shapes=[
+                pltpu.VMEM((2 * LANES, 2 * LANES), BF16),
                 pltpu.VMEM((BALLS_STEP, groups, LANES, spread), BF16),
-                pltpu.VMEM((BALLS_STEP, groups, spread, 2 * LANES), BF16),
-                pltpu.VMEM((BALLS_STEP, groups, BALL, spread), BF16),
-                pltpu.VMEM((step_rows, width), BF16),
+                pltpu.VMEM((BALLS_STEP, groups, LANES + 16, far), BF16),
+                pltpu.VMEM((BALLS_STEP, groups, far, spread), BF16),
+                pltpu.VMEM((width, step_rows), BF16),
                 pltpu.VMEM((rows_dev * (width // LANES), LANES), F32),
                 pltpu.VMEM((take_rows * (width // LANES), LANES), F32),
             ],
@@ -592,20 +614,16 @@
     return route(block, lambda i: i ^ mate)
 
 
-def wanted(below, above, place, mate):
-    return jnp.where(place > (place ^ mate), below, above)
-
-
 SLOT_INSIDE = (0, 5, 1, 6)
-SLOT_BELOW = (2, 7, 4, 8)
+SLOT_OUTSIDE = (2, 7, 4, 8)
 
 
 def block_slots(owner, me, peers):
     mate = (owner % GROUP) ^ (me % GROUP)
     ahead = jnp.mod(owner // GROUP - me // GROUP, peers // GROUP)
     pick = lambda table: sum(jnp.where(mate == m, table[m], 0) for m in range(GROUP))
-    outside = pick(SLOT_BELOW) + jnp.where((mate == 0) & (ahead == 1), 1, 0)
-    return jnp.where(ahead == 0, pick(SLOT_INSIDE), outside)
+    second = (mate == 0) & ((ahead == 1) != (me % GROUP < 2))
+    return jnp.where(ahead == 0, pick(SLOT_INSIDE), pick(SLOT_OUTSIDE) + jnp.where(second, 1, 0))
 
 
 def on_device(
@@ -637,30 +655,32 @@
         return lax.all_to_all(array, "pts", split_axis=0, concat_axis=0, tiled=True)
 
     outgoing, slot = send_order(points, point_row_index.reshape(rows_dev // LANES, LANES), me, peers)
-    source, ids, places, pooled = pool(swap(outgoing), attention_norm_gain[None], rows_dev)
-    below = route(pooled, lambda i: i + GROUP)
-    above = route(pooled, lambda i: i - GROUP)
+    rows, places, pooled = pool(swap(outgoing), attention_norm_gain[None], rows_dev)
+    up = lambda i: i % GROUP >= 2
+    first = route(pooled, lambda i: i + GROUP if up(i) else i - GROUP)
+    other = route(pooled, lambda i: i - GROUP if up(i) else i + GROUP)
     beside = to_mate(pooled, 2)
-    grouped, normed = group(ids, source, attention_norm_gain[None])
-    scale = jnp.repeat(head_score_scale * (LOG2E / head_size), head_size)[None]
+    grouped, normed = group(places, rows, attention_norm_gain[None])
+    first, normed = lax.optimization_barrier((first, normed))
+    handed = to_mate(first, 2)
+    scale = head_score_scale * (LOG2E / head_size)
     attend = functools.partial(
         local_attention,
         normed=normed,
-        wq=query_weight,
-        wk=key_weight.T,
-        wv=value_weight,
+        wq=query_weight.T,
+        wk=key_weight,
+        wv=value_weight.T,
         scale=scale,
         head_size=head_size,
     )
-    part = attend(0, 2)
-    below, above, beside, part = lax.optimization_barrier((below, above, beside, part))
+    early = blocks_dev * 3 // 4
+    part = attend(0, early)
+    first, other, beside, handed, part = lax.optimization_barrier((first, other, beside, handed, part))
     place = me % GROUP
-    second = to_mate(wanted(below, above, place, 2), 2)
-    near = to_mate(jnp.stack([pooled, beside, wanted(below, above, place, 1)]), 1)
-    query, num, den = attend(1, 2, earlier=part)
-    second, query = lax.optimization_barrier((second, query))
-    last = to_mate(second, 1)
-    candidates = jnp.concatenate([jnp.stack([pooled, beside, below, above, second]), near, last[None]])
+    held = jnp.stack([pooled, beside, jnp.where(place // 2 == place % 2, first, other), handed])
+    near = to_mate(held, 1)
+    query, num, den = attend(early, blocks_dev, earlier=part)
+    candidates = jnp.concatenate([jnp.stack([pooled, beside, first, other, handed]), near])
     candidates = candidates.reshape(candidates.shape[0] * blocks_dev, comp, width)
     slots = block_slots(neighbour_ball_list // blocks_dev, me, peers)
     chosen = (slots * blocks_dev + neighbour_ball_list % blocks_dev).reshape(-1)
@@ -672,8 +692,8 @@
         num,
         den,
         grouped,
-        pooled_key_weight.T,
-        pooled_value_weight,
+        pooled_key_weight,
+        pooled_value_weight.T,
         output_weight,
         feedforward_norm_gain[None],
         gate_weight,

time: 169 us -> 166 us (0.982)
  Pallas kernels: 53.6 us -> 49.3 us
  starting transfers between devices: 18.8 us -> 21.8 us
  waiting for transfers between devices: 41.8 us -> 38.8 us
    ppermute x6 -> x5, starting transfers between devices: 11.3 us -> 14.3 us  [route(): lax.ppermute(block, 'pts', [(i, target(i) % len(devices)) for i in devices])]
    pallas_call x2, Pallas kernels: 16.1 us -> 13.3 us  [local_attention(): pl.pallas_call(functools.partial(local_kernel, head_size), grid=(steps,),...]
    pallas_call x1, Pallas kernels: 5.48 us -> 3.24 us  [group(): pl.pallas_call(group_kernel, grid_spec=pltpu.PrefetchScalarGridSpec(num_s...]
    all_to_all x1, waiting for transfers between devices: 40.7 us -> 38.8 us  [swap(): return lax.all_to_all(array, 'pts', split_axis=0, concat_axis=0, tiled=True)]
    unnamed x34, local copies, waits for them, and re-layouts: 1.92 us -> 3.69 us
  transfers between devices with their start and end apart: 7 -> 6, of which waited for: 2 -> 1; matrix products, arithmetic and copies ran while one was open for 1% -> 2% of each run, Pallas kernels for 13% -> 10%
where the time goes in v6:
time: 166 us
  blocking collectives  51.4 us (31%)
  Pallas kernels  49.3 us (30%)
  waiting for transfers between devices  38.8 us (23%)
  starting transfers between devices  21.8 us (13%)
  local copies, waits for them, and re-layouts  3.92 us (2%)
    all_to_all x1, blocking collectives, swap(): return lax.all_to_all(array, 'pts', split_axis=0, concat_axis=0, tiled=True)  51.4 us
    all_to_all x1, waiting for transfers between devices, swap(): return lax.all_to_all(array, 'pts', split_axis=0, concat_axis=0, tiled=True)  38.8 us
    pallas_call x1, Pallas kernels, finish(): pl.pallas_call(functools.partial(finish_kernel, head_size), grid_spec=plt...  19.8 us
    ppermute x5, starting transfers between devices, route(): lax.ppermute(block, 'pts', [(i, target(i) % len(devices)) for i in devices])  14.3 us
    pallas_call x2, Pallas kernels, local_attention(): pl.pallas_call(functools.partial(local_kernel, head_size), grid=(steps,),...  13.3 us
    all_to_all x1, starting transfers between devices, swap(): return lax.all_to_all(array, 'pts', split_axis=0, concat_axis=0, tiled=True)  7.47 us
    pallas_call x1, Pallas kernels, send_order(): pl.pallas_call(functools.partial(send_kernel, send_each), grid_spec=pltpu...  6.45 us
    pallas_call x1, Pallas kernels, take_rows(): pl.pallas_call(take_kernel, grid_spec=pltpu.PrefetchScalarGridSpec(num_sc...  4.46 us
  transfers between devices with their start and end apart: 6, of which 1 were waited for; matrix products, arithmetic and copies ran while one was open for 2% of the time, Pallas kernels for 10%

profile of v6, /device:TPU:1, one launch (start us, length us, event | category | flops | bytes accessed | tf_op | source)
XLA Modules:
  0.0 165.8 jit_solution(2679708075944852596)
XLA Ops:
  0.0 6.5 %send_order.1 = (bf16[16,528,128]{2,1,0:T(8,128)(2,1)}, s32[16,128]{1,0:T(8,128)}) custom-call(s32[1]{0:T(128)} %bitcast.me_ref, s32[16,128]{1,0:T(8,128)} %bitcast.36, bf16[2048,512]{1,0:T(8,128)(2,1)} %points_ref.1), custom_call_target="tpu_custom_call" | custom-call | flops 4294967296 | bytes 4194304 | tf_op jit(solution)/shard_map/send_order/pallas_call | solution.py:149
  6.5 0.0 copy-start.10
  6.5 0.0 copy-start.11
  6.5 7.5 %all-to-all-start = ((bf16[16,528,128]{2,1,0:T(8,128)(2,1)}), bf16[16,528,128]{2,1,0:T(8,128)(2,1)S(1)}, u32[]{:S(2)}, u32[]{:S(2)}) async-start(bf16[16,528,128]{2,1,0:T(8,128)(2,1)} %get-tuple-element.28), calls=%async_computation | async-start | bytes 4325376 | tf_op jit(solution)/shard_map/all_to_all | solution.py:655
  14.0 0.0 copy-start.12
  14.0 0.0 copy-start.1
  14.0 0.0 copy-done.10
  14.0 0.2 copy.24
  14.2 1.3 copy.25
  15.5 0.0 copy-done.11
  15.6 0.1 copy.23
  15.7 0.1 reshape.20.chosen_ref
  15.7 2.0 %copy.26 = bf16[512,512]{0,1:T(8,128)(2,1)} copy(bf16[512,512]{1,0:T(8,128)(2,1)} %param.23) | data formatting | bytes 1048576 | tf_op args[8]
  17.8 0.0 copy-done.12
  17.8 38.8 %all-to-all-done.arrived_ref = bf16[16,528,128]{2,1,0:T(8,128)(2,1)S(1)} async-done(((bf16[16,528,128]{2,1,0:T(8,128)(2,1)}), bf16[16,528,128]{2,1,0:T(8,128)(2,1)S(1)}, u32[]{:S(2)}, u32[]{:S(2)}) %all-to-all-start) | async-done | bytes 2162720 | tf_op jit(solution)/shard_map/all_to_all | solution.py:655
  56.6 0.0 copy-done.1
  56.6 2.0 %pool_arrived.1 = (f32[8192,128]{1,0:T(8,128)S(1)}, s32[16,128]{1,0:T(8,128)S(1)}, bf16[256,512]{1,0:T(8,128)(2,1)S(1)}) custom-call(bf16[16,528,128]{2,1,0:T(8,128)(2,1)S(1)} %all-to-all-done.arrived_ref, f32[1,512]{1,0:T(1,128)S(1)} %bitcast.31), custom_call_target="tpu_custom_call" | custom-call | flops 536870912 | bytes 4194304 | tf_op jit(solution)/shard_map/pool_arrived/pallas_call | solution.py:228
  58.6 6.1 %collective-permute-start = (bf16[256,512]{1,0:T(8,128)(2,1)S(1)}, bf16[256,512]{1,0:T(8,128)(2,1)S(1)}, u32[]{:S(2)}, u32[]{:S(2)}) collective-permute-start(bf16[256,512]{1,0:T(8,128)(2,1)S(1)} %get-tuple-element.30), channel_id=1, source_target_pairs={{0,24},{2,26},{4,12},{6,14},{8,0},{10,2},{12,20},{14,22},{16,8},{1... | collective-permute-start | bytes 786440 | tf_op jit(solution)/shard_map/ppermute | solution.py:610
  64.7 0.3 collective-permute-start.1
  65.0 3.6 %collective-permute-start.2 = (bf16[256,512]{1,0:T(8,128)(2,1)S(1)}, bf16[256,512]{1,0:T(8,128)(2,1)S(1)}, u32[]{:S(2)}, u32[]{:S(2)}) collective-permute-start(bf16[256,512]{1,0:T(8,128)(2,1)S(1)} %get-tuple-element.30), channel_id=1, source_target_pairs={{0,4},{2,6},{4,0},{6,2},{8,12},{10,14},{12,8},{14,10},{16,20},{18,... | collective-permute-start | bytes 786440 | tf_op jit(solution)/shard_map/ppermute | solution.py:610
  68.5 0.0 copy-start.5
  68.5 3.2 %group_balls.1 = (bf16[2048,512]{1,0:T(8,128)(2,1)S(1)}, bf16[2048,512]{1,0:T(8,128)(2,1)S(1)}) custom-call(s32[16,128]{1,0:T(8,128)S(1)} %get-tuple-element.29.places_ref, f32[8192,128]{1,0:T(8,128)S(1)} %get-tuple-element.31.rows_ref, f32[1,512]{1,0:T(1,128)S(1)} %bitcast.32), custom_call_target="tpu_custom_call" | custom-call | flops 4294967296 | bytes 6291456 | tf_op jit(solution)/shard_map/group_balls/pallas_call | solution.py:270
  71.8 0.0 collective-permute-done
  71.8 3.1 %collective-permute-start.3 = (bf16[256,512]{1,0:T(8,128)(2,1)S(1)}, bf16[256,512]{1,0:T(8,128)(2,1)S(1)}, u32[]{:S(2)}, u32[]{:S(2)}) collective-permute-start(bf16[256,512]{1,0:T(8,128)(2,1)S(1)} %collective-permute-done), channel_id=1, source_target_pairs={{0,4},{2,6},{4,0},{6,2},{8,12},{10,14},{12,8},{14,10},{16,20},{18,... | collective-permute-start | bytes 786440 | tf_op jit(solution)/shard_map/ppermute | solution.py:610
  74.9 0.0 copy-done.5
  74.9 9.8 %local_attention.2 = (bf16[512,2048]{1,0:T(8,128)(2,1)S(1)}, bf16[512,2048]{1,0:T(8,128)(2,1)S(1)}, f32[16,2048]{1,0:T(8,128)S(1)}) custom-call(f32[16]{0:T(128)S(1)} %broadcast_multiply_fusion.scale_ref, bf16[2048,512]{1,0:T(8,128)(2,1)S(1)} %get-tuple-element.34.normed_ref, bf16[512,512]{1,0:T(8,128)(2,1)S(1)} %bitcast.25, bf16[512,512]{1,0:T(8,128)(2,1)S(1)} %copy-done.5, ...), custom_call_target="tpu_custom_call" | custom-call | flops 8053063680 | bytes 9437184 | tf_op jit(solution)/shard_map/local_attention/pallas_call | solution.py:377
  84.7 0.0 collective-permute-done.1
  84.7 0.0 collective-permute-done.2
  84.7 0.0 collective-permute-done.3
  84.8 0.1 pad_maximum_fusion
  84.9 1.3 collective-permute-start.4
  86.4 0.0 copy-start
  86.4 0.0 copy-start.2
  86.4 0.0 copy-start.3
  86.4 0.0 copy-start.4
  86.4 0.0 copy-start.6
  86.4 0.0 copy-start.7
  86.4 0.0 copy-start.8
  86.4 3.5 %local_attention.3 = (bf16[512,2048]{1,0:T(8,128)(2,1)S(1)}, bf16[512,2048]{1,0:T(8,128)(2,1)S(1)}, f32[16,2048]{1,0:T(8,128)S(1)}) custom-call(f32[16]{0:T(128)S(1)} %broadcast_multiply_fusion.scale_ref, bf16[2048,512]{1,0:T(8,128)(2,1)S(1)} %get-tuple-element.34.normed_ref, ...), custom_call_target="tpu_custom_call", output_to_operand_aliasing={{0}: (5, {}), {1}: (6, {}), {2}: (7, {})} | custom-call | flops 2684354560 | bytes 3145728 | tf_op jit(solution)/shard_map/local_attention/pallas_call | solution.py:377
  89.9 0.0 collective-permute-done.4
  90.0 0.1 constant_dynamic-update-slice_fusion
  90.0 0.0 copy-done
  90.0 0.0 copy-done.2
  90.1 0.0 copy-done.3
  90.1 0.0 copy-done.4
  90.1 0.0 copy-done.6
  90.1 0.0 copy-done.7
  90.1 0.0 copy-done.8
  90.1 19.8 %finish_balls.1 = bf16[2048,512]{1,0:T(8,128)(2,1)S(1)} custom-call(s32[32]{0:T(128)S(1)} %reshape.20.chosen_ref, s32[16,128]{1,0:T(8,128)S(1)} %get-tuple-element.29.places_ref, bf16[72,32,512]{2,1,0:T(8,128)(2,1)S(1)} %bitcast.30, bf16[512,2048]{1,0:T(8,128)(2,1)S(1)} %get-tuple-element.45.query_ref, bf16[512,2048]{1,0:T(8,128)(2,1)S(1)} %get-tuple-element.46.num_ref, ...), custom_call_target="tpu_custom_call" | custom-call | flops 12884901888 | bytes 12582912 | tf_op jit(solution)/shard_map/finish_balls/pallas_call | solution.py:535
  109.9 0.0 copy-start.9
  109.9 51.4 %all_to_all.10 = bf16[16,128,512]{2,1,0:T(8,128)(2,1)S(1)} all-to-all(bf16[16,128,512]{2,1,0:T(8,128)(2,1)S(1)} %bitcast.22), channel_id=1, replica_groups=mesh['pts'=16,'rep'=2] {'pts'}, dimensions={0} | all-to-all | bytes 4194304 | tf_op jit(solution)/shard_map/all_to_all | solution.py:655
  161.4 0.0 copy-done.9
  161.4 4.5 %take_rows.1 = bf16[2048,512]{1,0:T(8,128)(2,1)} custom-call(s32[16,128]{1,0:T(8,128)S(1)} %copy-done.9, bf16[2048,512]{1,0:T(8,128)(2,1)S(1)} %bitcast.23), custom_call_target="tpu_custom_call" | custom-call | flops 4294967296 | bytes 4194304 | tf_op jit(solution)/shard_map/take_rows/pallas_call | solution.py:587
  (8 shorter events, 0.2 us)
Async XLA Ops:
  6.5 7.5 %copy-start.10 = (bf16[512,512]{1,0:T(8,128)(2,1)S(1)}, bf16[512,512]{1,0:T(8,128)(2,1)}, u32[]{:S(2)}) copy-start(bf16[512,512]{1,0:T(8,128)(2,1)} %param.19) | copy-start | bytes 1572868
  6.5 9.1 %copy-start.11 = (s32[8,4]{0,1:T(4,128)S(1)}, s32[8,4]{0,1:T(4,128)}, u32[]{:S(2)}) copy-start(s32[8,4]{0,1:T(4,128)} %param.17) | copy-start | bytes 388
  6.5 50.1 %all-to-all-start = ((bf16[16,528,128]{2,1,0:T(8,128)(2,1)}), bf16[16,528,128]{2,1,0:T(8,128)(2,1)S(1)}, u32[]{:S(2)}, u32[]{:S(2)}) async-start(bf16[16,528,128]{2,1,0:T(8,128)(2,1)} %get-tuple-element.28), calls=%async_computation | async-start | bytes 4325376 | tf_op jit(solution)/shard_map/all_to_all | solution.py:655
  14.0 3.8 %copy-start.12 = (f32[16]{0:T(128)S(1)}, f32[16]{0:T(128)}, u32[]{:S(2)}) copy-start(f32[16]{0:T(128)} %param.24) | copy-start | bytes 196
  14.0 42.6 %copy-start.1 = (f32[512]{0:T(512)S(1)}, f32[512]{0:T(512)}, u32[]{:S(2)}) copy-start(f32[512]{0:T(512)} %param.18) | copy-start | bytes 6148
  58.6 13.2 %collective-permute-start = (bf16[256,512]{1,0:T(8,128)(2,1)S(1)}, bf16[256,512]{1,0:T(8,128)(2,1)S(1)}, u32[]{:S(2)}, u32[]{:S(2)}) collective-permute-start(bf16[256,512]{1,0:T(8,128)(2,1)S(1)} %get-tuple-element.30), channel_id=1, source_target_pairs={{0,24},{2,26},{4,12},{6,14},{8,0},{10,2},{12,20},{14,22},{16,8},{1... | collective-permute-start | bytes 786440 | tf_op jit(solution)/shard_map/ppermute | solution.py:610
  64.7 20.1 %collective-permute-start.1 = (bf16[256,512]{1,0:T(8,128)(2,1)S(1)}, bf16[256,512]{1,0:T(8,128)(2,1)S(1)}, u32[]{:S(2)}, u32[]{:S(2)}) collective-permute-start(bf16[256,512]{1,0:T(8,128)(2,1)S(1)} %get-tuple-element.30), channel_id=1, source_target_pairs={{0,8},{2,10},{4,28},{6,30},{8,16},{10,18},{12,4},{14,6},{16,24},{1... | collective-permute-start | bytes 786440 | tf_op jit(solution)/shard_map/ppermute | solution.py:610
  65.0 19.8 %collective-permute-start.2 = (bf16[256,512]{1,0:T(8,128)(2,1)S(1)}, bf16[256,512]{1,0:T(8,128)(2,1)S(1)}, u32[]{:S(2)}, u32[]{:S(2)}) collective-permute-start(bf16[256,512]{1,0:T(8,128)(2,1)S(1)} %get-tuple-element.30), channel_id=1, source_target_pairs={{0,4},{2,6},{4,0},{6,2},{8,12},{10,14},{12,8},{14,10},{16,20},{18,... | collective-permute-start | bytes 786440 | tf_op jit(solution)/shard_map/ppermute | solution.py:610
  68.5 6.4 %copy-start.5 = (bf16[512,512]{1,0:T(8,128)(2,1)S(1)}, bf16[512,512]{1,0:T(8,128)(2,1)}, u32[]{:S(2)}) copy-start(bf16[512,512]{1,0:T(8,128)(2,1)} %wk_ref.3) | copy-start | bytes 1572868
  71.8 12.9 %collective-permute-start.3 = (bf16[256,512]{1,0:T(8,128)(2,1)S(1)}, bf16[256,512]{1,0:T(8,128)(2,1)S(1)}, u32[]{:S(2)}, u32[]{:S(2)}) collective-permute-start(bf16[256,512]{1,0:T(8,128)(2,1)S(1)} %collective-permute-done), channel_id=1, source_target_pairs={{0,4},{2,6},{4,0},{6,2},{8,12},{10,14},{12,8},{14,10},{16,20},{18,... | collective-permute-start | bytes 786440 | tf_op jit(solution)/shard_map/ppermute | solution.py:610
  84.9 5.0 %collective-permute-start.4 = (bf16[4,256,512]{2,1,0:T(8,128)(2,1)S(1)}, bf16[4,256,512]{2,1,0:T(8,128)(2,1)S(1)}, u32[]{:S(2)}, u32[]{:S(2)}) collective-permute-start(bf16[4,256,512]{2,1,0:T(8,128)(2,1)S(1)} %pad_maximum_fusion), channel_id=1, source_target_pairs={{0,2},{2,0},{4,6},{6,4},{8,10},{10,8},{12,14},{14,12},{16,18},{18,... | collective-permute-start | bytes 3145736 | tf_op jit(solution)/shard_map/ppermute | solution.py:610
  86.4 3.7 %copy-start = (bf16[512,512]{0,1:T(8,128)(2,1)S(1)}, bf16[512,512]{0,1:T(8,128)(2,1)}, u32[]{:S(2)}) copy-start(bf16[512,512]{0,1:T(8,128)(2,1)} %copy.26) | copy-start | bytes 1572868
  86.4 3.7 %copy-start.2 = (bf16[512,1024]{1,0:T(8,128)(2,1)S(1)}, bf16[512,1024]{1,0:T(8,128)(2,1)}, u32[]{:S(2)}) copy-start(bf16[512,1024]{1,0:T(8,128)(2,1)} %wg_ref.1) | copy-start | bytes 3145732
  86.4 3.7 %copy-start.3 = (bf16[512,1024]{1,0:T(8,128)(2,1)S(1)}, bf16[512,1024]{1,0:T(8,128)(2,1)}, u32[]{:S(2)}) copy-start(bf16[512,1024]{1,0:T(8,128)(2,1)} %wu_ref.1) | copy-start | bytes 3145732
  86.4 3.7 %copy-start.4 = (bf16[1024,512]{1,0:T(8,128)(2,1)S(1)}, bf16[1024,512]{1,0:T(8,128)(2,1)}, u32[]{:S(2)}) copy-start(bf16[1024,512]{1,0:T(8,128)(2,1)} %wd_ref.1) | copy-start | bytes 3145732
  86.4 3.7 %copy-start.6 = (bf16[512,512]{1,0:T(8,128)(2,1)S(1)}, bf16[512,512]{1,0:T(8,128)(2,1)}, u32[]{:S(2)}) copy-start(bf16[512,512]{1,0:T(8,128)(2,1)} %wpk_ref.1) | copy-start | bytes 1572868
  86.4 3.7 %copy-start.7 = (bf16[512,512]{1,0:T(8,128)(2,1)S(1)}, bf16[512,512]{1,0:T(8,128)(2,1)}, u32[]{:S(2)}) copy-start(bf16[512,512]{1,0:T(8,128)(2,1)} %wo_ref.1) | copy-start | bytes 1572868
  86.4 3.7 %copy-start.8 = (f32[512]{0:T(512)S(1)}, f32[512]{0:T(512)}, u32[]{:S(2)}) copy-start(f32[512]{0:T(512)} %param.26) | copy-start | bytes 6148
  109.9 51.4 %copy-start.9 = (s32[16,128]{1,0:T(8,128)S(1)}, s32[16,128]{1,0:T(8,128)}, u32[]{:S(2)}) copy-start(s32[16,128]{1,0:T(8,128)} %get-tuple-element.27.places_ref) | copy-start | bytes 24580

commit v7 on v6

--- a/solution.py
+++ b/solution.py
@@ -15,7 +15,7 @@
 LANES = 128
 TILE = 512
 DEPTH = 512
-BALLS_STEP = 2
+BALLS_STEP = 4
 LOW = 64
 SEND_PITCH = 8
 SEND_STEPS = 2
@@ -370,7 +370,7 @@
     groups = width // LANES
     heads = width // head_size
     spread = LANES // head_size * BALL
-    balls = math.gcd(math.gcd(first, last), BALLS_STEP)
+    balls = math.gcd(math.gcd(first, last), 2)
     steps = (last - first) // balls
     at = lambda i: first // balls + i
     columns = lambda count: pl.BlockSpec((count, balls * BALL), lambda i: (0, at(i)))
@@ -661,8 +661,6 @@
     other = route(pooled, lambda i: i - GROUP if up(i) else i + GROUP)
     beside = to_mate(pooled, 2)
     grouped, normed = group(places, rows, attention_norm_gain[None])
-    first, normed = lax.optimization_barrier((first, normed))
-    handed = to_mate(first, 2)
     scale = head_score_scale * (LOG2E / head_size)
     attend = functools.partial(
         local_attention,
@@ -673,8 +671,11 @@
         scale=scale,
         head_size=head_size,
     )
-    early = blocks_dev * 3 // 4
-    part = attend(0, early)
+    soon, early = blocks_dev // 4, blocks_dev * 3 // 4
+    part = attend(0, soon)
+    first, part = lax.optimization_barrier((first, part))
+    handed = to_mate(first, 2)
+    part = attend(soon, early, earlier=part)
     first, other, beside, handed, part = lax.optimization_barrier((first, other, beside, handed, part))
     place = me % GROUP
     held = jnp.stack([pooled, beside, jnp.where(place // 2 == place % 2, first, other), handed])

time: 166 us -> 163 us (0.982)
  starting transfers between devices: 21.8 us -> 19.2 us
    ppermute x5, starting transfers between devices: 14.3 us -> 11.7 us  [route(): lax.ppermute(block, 'pts', [(i, target(i) % len(devices)) for i in devices])]
    pallas_call x2 -> x3, Pallas kernels: 13.3 us -> 13.7 us  [local_attention(): pl.pallas_call(functools.partial(local_kernel, head_size), grid=(steps,),...]
  transfers between devices with their start and end apart: 6 -> 6, of which waited for: 1 -> 2; matrix products, arithmetic and copies ran while one was open for 2% -> 2% of each run, Pallas kernels for 10% -> 10%
where the time goes in v7:
time: 163 us; the launch traced here: 162 us
  blocking collectives  51 us (31%)
  Pallas kernels  48.7 us (30%)
  waiting for transfers between devices  39 us (24%)
  starting transfers between devices  19.2 us (12%)
  local copies, waits for them, and re-layouts  3.92 us (2%)
    all_to_all x1, blocking collectives, swap(): return lax.all_to_all(array, 'pts', split_axis=0, concat_axis=0, tiled=True)  51 us
    all_to_all x1, waiting for transfers between devices, swap(): return lax.all_to_all(array, 'pts', split_axis=0, concat_axis=0, tiled=True)  38.8 us
    pallas_call x1, Pallas kernels, finish(): pl.pallas_call(functools.partial(finish_kernel, head_size), grid_spec=plt...  18.8 us
    pallas_call x3, Pallas kernels, local_attention(): pl.pallas_call(functools.partial(local_kernel, head_size), grid=(steps,),...  13.7 us
    ppermute x5, starting transfers between devices, route(): lax.ppermute(block, 'pts', [(i, target(i) % len(devices)) for i in devices])  11.7 us
    all_to_all x1, starting transfers between devices, swap(): return lax.all_to_all(array, 'pts', split_axis=0, concat_axis=0, tiled=True)  7.47 us
    pallas_call x1, Pallas kernels, send_order(): pl.pallas_call(functools.partial(send_kernel, send_each), grid_spec=pltpu...  6.45 us
    pallas_call x1, Pallas kernels, take_rows(): pl.pallas_call(take_kernel, grid_spec=pltpu.PrefetchScalarGridSpec(num_sc...  4.46 us
  transfers between devices with their start and end apart: 6, of which 2 were waited for; matrix products, arithmetic and copies ran while one was open for 2% of the time, Pallas kernels for 10%

profile of v7, /device:TPU:1, one launch (start us, length us, event | category | flops | bytes accessed | tf_op | source)
XLA Modules:
  0.0 162.4 jit_solution(9307841055974730879)
XLA Ops:
  0.0 6.4 %send_order.1 = (bf16[16,528,128]{2,1,0:T(8,128)(2,1)}, s32[16,128]{1,0:T(8,128)}) custom-call(s32[1]{0:T(128)} %bitcast.me_ref, s32[16,128]{1,0:T(8,128)} %bitcast.38, bf16[2048,512]{1,0:T(8,128)(2,1)} %points_ref.1), custom_call_target="tpu_custom_call" | custom-call | flops 4294967296 | bytes 4194304 | tf_op jit(solution)/shard_map/send_order/pallas_call | solution.py:149
  6.5 0.0 copy-start.10
  6.5 0.0 copy-start.11
  6.5 7.5 %all-to-all-start = ((bf16[16,528,128]{2,1,0:T(8,128)(2,1)}), bf16[16,528,128]{2,1,0:T(8,128)(2,1)S(1)}, u32[]{:S(2)}, u32[]{:S(2)}) async-start(bf16[16,528,128]{2,1,0:T(8,128)(2,1)} %get-tuple-element.33), calls=%async_computation | async-start | bytes 4325376 | tf_op jit(solution)/shard_map/all_to_all | solution.py:655
  13.9 0.0 copy-start.12
  14.0 0.0 copy-start.1
  14.0 0.0 copy-done.10
  14.0 0.2 copy.27
  14.2 1.3 copy.28
  15.5 0.0 copy-done.11
  15.6 0.1 copy.26
  15.7 0.1 reshape.20.chosen_ref
  15.7 2.0 %copy.29 = bf16[512,512]{0,1:T(8,128)(2,1)} copy(bf16[512,512]{1,0:T(8,128)(2,1)} %param.23) | data formatting | bytes 1048576 | tf_op args[8]
  17.8 0.0 copy-done.12
  17.8 38.8 %all-to-all-done.arrived_ref = bf16[16,528,128]{2,1,0:T(8,128)(2,1)S(1)} async-done(((bf16[16,528,128]{2,1,0:T(8,128)(2,1)}), bf16[16,528,128]{2,1,0:T(8,128)(2,1)S(1)}, u32[]{:S(2)}, u32[]{:S(2)}) %all-to-all-start) | async-done | bytes 2162720 | tf_op jit(solution)/shard_map/all_to_all | solution.py:655
  56.6 0.0 copy-done.1
  56.6 2.0 %pool_arrived.1 = (f32[8192,128]{1,0:T(8,128)S(1)}, s32[16,128]{1,0:T(8,128)S(1)}, bf16[256,512]{1,0:T(8,128)(2,1)S(1)}) custom-call(bf16[16,528,128]{2,1,0:T(8,128)(2,1)S(1)} %all-to-all-done.arrived_ref, f32[1,512]{1,0:T(1,128)S(1)} %bitcast.33), custom_call_target="tpu_custom_call" | custom-call | flops 536870912 | bytes 4194304 | tf_op jit(solution)/shard_map/pool_arrived/pallas_call | solution.py:228
  58.6 6.1 %collective-permute-start = (bf16[256,512]{1,0:T(8,128)(2,1)S(1)}, bf16[256,512]{1,0:T(8,128)(2,1)S(1)}, u32[]{:S(2)}, u32[]{:S(2)}) collective-permute-start(bf16[256,512]{1,0:T(8,128)(2,1)S(1)} %get-tuple-element.35), channel_id=1, source_target_pairs={{0,24},{2,26},{4,12},{6,14},{8,0},{10,2},{12,20},{14,22},{16,8},{1... | collective-permute-start | bytes 786440 | tf_op jit(solution)/shard_map/ppermute | solution.py:610
  64.6 0.3 collective-permute-start.1
  65.0 3.6 %collective-permute-start.2 = (bf16[256,512]{1,0:T(8,128)(2,1)S(1)}, bf16[256,512]{1,0:T(8,128)(2,1)S(1)}, u32[]{:S(2)}, u32[]{:S(2)}) collective-permute-start(bf16[256,512]{1,0:T(8,128)(2,1)S(1)} %get-tuple-element.35), channel_id=1, source_target_pairs={{0,4},{2,6},{4,0},{6,2},{8,12},{10,14},{12,8},{14,10},{16,20},{18,... | collective-permute-start | bytes 786440 | tf_op jit(solution)/shard_map/ppermute | solution.py:610
  68.5 0.0 copy-start.5
  68.5 3.2 %group_balls.1 = (bf16[2048,512]{1,0:T(8,128)(2,1)S(1)}, bf16[2048,512]{1,0:T(8,128)(2,1)S(1)}) custom-call(s32[16,128]{1,0:T(8,128)S(1)} %get-tuple-element.34.places_ref, f32[8192,128]{1,0:T(8,128)S(1)} %get-tuple-element.36.rows_ref, f32[1,512]{1,0:T(1,128)S(1)} %bitcast.34), custom_call_target="tpu_custom_call" | custom-call | flops 4294967296 | bytes 6291456 | tf_op jit(solution)/shard_map/group_balls/pallas_call | solution.py:270
  71.8 0.0 copy-done.5
  71.8 3.5 %local_attention.3 = (bf16[512,2048]{1,0:T(8,128)(2,1)S(1)}, bf16[512,2048]{1,0:T(8,128)(2,1)S(1)}, f32[16,2048]{1,0:T(8,128)S(1)}) custom-call(f32[16]{0:T(128)S(1)} %broadcast_multiply_fusion.scale_ref, bf16[2048,512]{1,0:T(8,128)(2,1)S(1)} %get-tuple-element.37.normed_ref, bf16[512,512]{1,0:T(8,128)(2,1)S(1)} %bitcast.25, bf16[512,512]{1,0:T(8,128)(2,1)S(1)} %copy-done.5, ...), custom_call_target="tpu_custom_call" | custom-call | flops 2684354560 | bytes 3145728 | tf_op jit(solution)/shard_map/local_attention/pallas_call | solution.py:377
  75.3 0.0 collective-permute-done
  75.3 0.1 collective-permute-start.3
  75.4 6.8 %local_attention.4 = (bf16[512,2048]{1,0:T(8,128)(2,1)S(1)}, bf16[512,2048]{1,0:T(8,128)(2,1)S(1)}, f32[16,2048]{1,0:T(8,128)S(1)}) custom-call(f32[16]{0:T(128)S(1)} %broadcast_multiply_fusion.scale_ref, bf16[2048,512]{1,0:T(8,128)(2,1)S(1)} %get-tuple-element.37.normed_ref, ...), custom_call_target="tpu_custom_call", output_to_operand_aliasing={{0}: (5, {}), {1}: (6, {}), {2}: (7, {})} | custom-call | flops 5368709120 | bytes 6291456 | tf_op jit(solution)/shard_map/local_attention/pallas_call | solution.py:377
  82.1 0.0 collective-permute-done.1
  82.2 0.0 collective-permute-done.2
  82.2 0.2 collective-permute-done.3
  82.5 0.1 pad_maximum_fusion
  82.6 1.7 %collective-permute-start.4 = (bf16[4,256,512]{2,1,0:T(8,128)(2,1)S(1)}, bf16[4,256,512]{2,1,0:T(8,128)(2,1)S(1)}, u32[]{:S(2)}, u32[]{:S(2)}) collective-permute-start(bf16[4,256,512]{2,1,0:T(8,128)(2,1)S(1)} %pad_maximum_fusion), channel_id=1, source_target_pairs={{0,2},{2,0},{4,6},{6,4},{8,10},{10,8},{12,14},{14,12},{16,18},{18,... | collective-permute-start | bytes 3145736 | tf_op jit(solution)/shard_map/ppermute | solution.py:610
  84.4 0.0 copy-start
  84.4 0.0 copy-start.2
  84.4 0.0 copy-start.3
  84.4 0.0 copy-start.4
  84.5 0.0 copy-start.6
  84.5 0.0 copy-start.7
  84.5 0.0 copy-start.8
  84.5 3.5 %local_attention.5 = (bf16[512,2048]{1,0:T(8,128)(2,1)S(1)}, bf16[512,2048]{1,0:T(8,128)(2,1)S(1)}, f32[16,2048]{1,0:T(8,128)S(1)}) custom-call(f32[16]{0:T(128)S(1)} %broadcast_multiply_fusion.scale_ref, bf16[2048,512]{1,0:T(8,128)(2,1)S(1)} %get-tuple-element.37.normed_ref, ...), custom_call_target="tpu_custom_call", output_to_operand_aliasing={{0}: (5, {}), {1}: (6, {}), {2}: (7, {})} | custom-call | flops 2684354560 | bytes 3145728 | tf_op jit(solution)/shard_map/local_attention/pallas_call | solution.py:377
  88.0 0.0 collective-permute-done.4
  88.0 0.1 constant_dynamic-update-slice_fusion
  88.1 0.0 copy-done
  88.1 0.0 copy-done.2
  88.1 0.0 copy-done.3
  88.1 0.0 copy-done.4
  88.1 0.0 copy-done.6
  88.1 0.0 copy-done.7
  88.1 0.0 copy-done.8
  88.1 18.8 %finish_balls.1 = bf16[2048,512]{1,0:T(8,128)(2,1)S(1)} custom-call(s32[32]{0:T(128)S(1)} %reshape.20.chosen_ref, s32[16,128]{1,0:T(8,128)S(1)} %get-tuple-element.34.places_ref, bf16[72,32,512]{2,1,0:T(8,128)(2,1)S(1)} %bitcast.32, bf16[512,2048]{1,0:T(8,128)(2,1)S(1)} %get-tuple-element.55.query_ref, bf16[512,2048]{1,0:T(8,128)(2,1)S(1)} %get-tuple-element.56.num_ref, ...), custom_call_target="tpu_custom_call" | custom-call | flops 12884901888 | bytes 12582912 | tf_op jit(solution)/shard_map/finish_balls/pallas_call | solution.py:535
  106.9 0.0 copy-start.9
  106.9 51.0 %all_to_all.10 = bf16[16,128,512]{2,1,0:T(8,128)(2,1)S(1)} all-to-all(bf16[16,128,512]{2,1,0:T(8,128)(2,1)S(1)} %bitcast.22), channel_id=1, replica_groups=mesh['pts'=16,'rep'=2] {'pts'}, dimensions={0} | all-to-all | bytes 4194304 | tf_op jit(solution)/shard_map/all_to_all | solution.py:655
  157.9 0.0 copy-done.9
  157.9 4.5 %take_rows.1 = bf16[2048,512]{1,0:T(8,128)(2,1)} custom-call(s32[16,128]{1,0:T(8,128)S(1)} %copy-done.9, bf16[2048,512]{1,0:T(8,128)(2,1)S(1)} %bitcast.23), custom_call_target="tpu_custom_call" | custom-call | flops 4294967296 | bytes 4194304 | tf_op jit(solution)/shard_map/take_rows/pallas_call | solution.py:587
  (8 shorter events, 0.2 us)
Async XLA Ops:
  6.5 7.5 %copy-start.10 = (bf16[512,512]{1,0:T(8,128)(2,1)S(1)}, bf16[512,512]{1,0:T(8,128)(2,1)}, u32[]{:S(2)}) copy-start(bf16[512,512]{1,0:T(8,128)(2,1)} %param.19) | copy-start | bytes 1572868
  6.5 9.1 %copy-start.11 = (s32[8,4]{0,1:T(4,128)S(1)}, s32[8,4]{0,1:T(4,128)}, u32[]{:S(2)}) copy-start(s32[8,4]{0,1:T(4,128)} %param.17) | copy-start | bytes 388
  6.5 50.1 %all-to-all-start = ((bf16[16,528,128]{2,1,0:T(8,128)(2,1)}), bf16[16,528,128]{2,1,0:T(8,128)(2,1)S(1)}, u32[]{:S(2)}, u32[]{:S(2)}) async-start(bf16[16,528,128]{2,1,0:T(8,128)(2,1)} %get-tuple-element.33), calls=%async_computation | async-start | bytes 4325376 | tf_op jit(solution)/shard_map/all_to_all | solution.py:655
  13.9 3.8 %copy-start.12 = (f32[16]{0:T(128)S(1)}, f32[16]{0:T(128)}, u32[]{:S(2)}) copy-start(f32[16]{0:T(128)} %param.24) | copy-start | bytes 196
  14.0 42.6 %copy-start.1 = (f32[512]{0:T(512)S(1)}, f32[512]{0:T(512)}, u32[]{:S(2)}) copy-start(f32[512]{0:T(512)} %param.18) | copy-start | bytes 6148
  58.6 16.7 %collective-permute-start = (bf16[256,512]{1,0:T(8,128)(2,1)S(1)}, bf16[256,512]{1,0:T(8,128)(2,1)S(1)}, u32[]{:S(2)}, u32[]{:S(2)}) collective-permute-start(bf16[256,512]{1,0:T(8,128)(2,1)S(1)} %get-tuple-element.35), channel_id=1, source_target_pairs={{0,24},{2,26},{4,12},{6,14},{8,0},{10,2},{12,20},{14,22},{16,8},{1... | collective-permute-start | bytes 786440 | tf_op jit(solution)/shard_map/ppermute | solution.py:610
  64.6 17.5 %collective-permute-start.1 = (bf16[256,512]{1,0:T(8,128)(2,1)S(1)}, bf16[256,512]{1,0:T(8,128)(2,1)S(1)}, u32[]{:S(2)}, u32[]{:S(2)}) collective-permute-start(bf16[256,512]{1,0:T(8,128)(2,1)S(1)} %get-tuple-element.35), channel_id=1, source_target_pairs={{0,8},{2,10},{4,28},{6,30},{8,16},{10,18},{12,4},{14,6},{16,24},{1... | collective-permute-start | bytes 786440 | tf_op jit(solution)/shard_map/ppermute | solution.py:610
  65.0 17.2 %collective-permute-start.2 = (bf16[256,512]{1,0:T(8,128)(2,1)S(1)}, bf16[256,512]{1,0:T(8,128)(2,1)S(1)}, u32[]{:S(2)}, u32[]{:S(2)}) collective-permute-start(bf16[256,512]{1,0:T(8,128)(2,1)S(1)} %get-tuple-element.35), channel_id=1, source_target_pairs={{0,4},{2,6},{4,0},{6,2},{8,12},{10,14},{12,8},{14,10},{16,20},{18,... | collective-permute-start | bytes 786440 | tf_op jit(solution)/shard_map/ppermute | solution.py:610
  68.5 3.3 %copy-start.5 = (bf16[512,512]{1,0:T(8,128)(2,1)S(1)}, bf16[512,512]{1,0:T(8,128)(2,1)}, u32[]{:S(2)}) copy-start(bf16[512,512]{1,0:T(8,128)(2,1)} %wk_ref.5) | copy-start | bytes 1572868
  75.3 7.1 %collective-permute-start.3 = (bf16[256,512]{1,0:T(8,128)(2,1)S(1)}, bf16[256,512]{1,0:T(8,128)(2,1)S(1)}, u32[]{:S(2)}, u32[]{:S(2)}) collective-permute-start(bf16[256,512]{1,0:T(8,128)(2,1)S(1)} %collective-permute-done), channel_id=1, source_target_pairs={{0,4},{2,6},{4,0},{6,2},{8,12},{10,14},{12,8},{14,10},{16,20},{18,... | collective-permute-start | bytes 786440 | tf_op jit(solution)/shard_map/ppermute | solution.py:610
  82.6 5.4 %collective-permute-start.4 = (bf16[4,256,512]{2,1,0:T(8,128)(2,1)S(1)}, bf16[4,256,512]{2,1,0:T(8,128)(2,1)S(1)}, u32[]{:S(2)}, u32[]{:S(2)}) collective-permute-start(bf16[4,256,512]{2,1,0:T(8,128)(2,1)S(1)} %pad_maximum_fusion), channel_id=1, source_target_pairs={{0,2},{2,0},{4,6},{6,4},{8,10},{10,8},{12,14},{14,12},{16,18},{18,... | collective-permute-start | bytes 3145736 | tf_op jit(solution)/shard_map/ppermute | solution.py:610
  84.4 3.7 %copy-start = (bf16[512,512]{0,1:T(8,128)(2,1)S(1)}, bf16[512,512]{0,1:T(8,128)(2,1)}, u32[]{:S(2)}) copy-start(bf16[512,512]{0,1:T(8,128)(2,1)} %copy.29) | copy-start | bytes 1572868
  84.4 3.7 %copy-start.2 = (bf16[512,1024]{1,0:T(8,128)(2,1)S(1)}, bf16[512,1024]{1,0:T(8,128)(2,1)}, u32[]{:S(2)}) copy-start(bf16[512,1024]{1,0:T(8,128)(2,1)} %wg_ref.1) | copy-start | bytes 3145732
  84.4 3.7 %copy-start.3 = (bf16[512,1024]{1,0:T(8,128)(2,1)S(1)}, bf16[512,1024]{1,0:T(8,128)(2,1)}, u32[]{:S(2)}) copy-start(bf16[512,1024]{1,0:T(8,128)(2,1)} %wu_ref.1) | copy-start | bytes 3145732
  84.4 3.7 %copy-start.4 = (bf16[1024,512]{1,0:T(8,128)(2,1)S(1)}, bf16[1024,512]{1,0:T(8,128)(2,1)}, u32[]{:S(2)}) copy-start(bf16[1024,512]{1,0:T(8,128)(2,1)} %wd_ref.1) | copy-start | bytes 3145732
  84.5 3.7 %copy-start.6 = (bf16[512,512]{1,0:T(8,128)(2,1)S(1)}, bf16[512,512]{1,0:T(8,128)(2,1)}, u32[]{:S(2)}) copy-start(bf16[512,512]{1,0:T(8,128)(2,1)} %wpk_ref.1) | copy-start | bytes 1572868
  84.5 3.7 %copy-start.7 = (bf16[512,512]{1,0:T(8,128)(2,1)S(1)}, bf16[512,512]{1,0:T(8,128)(2,1)}, u32[]{:S(2)}) copy-start(bf16[512,512]{1,0:T(8,128)(2,1)} %wo_ref.1) | copy-start | bytes 1572868
  84.5 3.7 %copy-start.8 = (f32[512]{0:T(512)S(1)}, f32[512]{0:T(512)}, u32[]{:S(2)}) copy-start(f32[512]{0:T(512)} %param.26) | copy-start | bytes 6148
  106.9 51.0 %copy-start.9 = (s32[16,128]{1,0:T(8,128)S(1)}, s32[16,128]{1,0:T(8,128)}, u32[]{:S(2)}) copy-start(s32[16,128]{1,0:T(8,128)} %get-tuple-element.32.places_ref) | copy-start | bytes 24580

commit v8 on v7

--- a/solution.py
+++ b/solution.py
@@ -13,7 +13,7 @@
 OWNERS = 4
 GROUP = 4
 LANES = 128
-TILE = 512
+TILE = 1024
 DEPTH = 512
 BALLS_STEP = 4
 LOW = 64
@@ -499,10 +499,10 @@
     for b in range(BALLS_STEP):
         cols = slice(b * BALL, (b + 1) * BALL)
         for h in range(groups * LANES // head_size):
-            spread_head(h, head_size, query_ref[h * head_size : (h + 1) * head_size, cols], queries.at[b])
+            spread_head(h, head_size, query_ref[h * head_size : (h + 1) * head_size, cols], queries.at[b % 2])
         for g in range(groups):
             values[b, g, :LANES, :] = value[g * LANES : (g + 1) * LANES, b * far : (b + 1) * far]
-        weigh(key_rows[b * far : (b + 1) * far, :], queries.at[b], weights.at[b])
+        weigh(key_rows[b * far : (b + 1) * far, :], queries.at[b % 2], weights.at[b])
     for b in range(BALLS_STEP):
         cols = slice(b * BALL, (b + 1) * BALL)
         for g in range(groups):
@@ -548,7 +548,7 @@
             out_specs=pl.BlockSpec((take_rows, width), lambda i, *_: (jnp.maximum(i - steps, 0), 0)),
             scratch_shapes=[
                 pltpu.VMEM((2 * LANES, 2 * LANES), BF16),
-                pltpu.VMEM((BALLS_STEP, groups, LANES, spread), BF16),
+                pltpu.VMEM((2, groups, LANES, spread), BF16),
                 pltpu.VMEM((BALLS_STEP, groups, LANES + 16, far), BF16),
                 pltpu.VMEM((BALLS_STEP, groups, far, spread), BF16),
                 pltpu.VMEM((width, step_rows), BF16),

time: 163 us -> 162 us (level)
  no operation moved by 1% of the time
where the time goes in v8:
time: 162 us
  blocking collectives  51 us (31%)
  Pallas kernels  48.1 us (30%)
  waiting for transfers between devices  39 us (24%)
  starting transfers between devices  19.2 us (12%)
  local copies, waits for them, and re-layouts  3.92 us (2%)
    all_to_all x1, blocking collectives, swap(): return lax.all_to_all(array, 'pts', split_axis=0, concat_axis=0, tiled=True)  51 us
    all_to_all x1, waiting for transfers between devices, swap(): return lax.all_to_all(array, 'pts', split_axis=0, concat_axis=0, tiled=True)  38.8 us
    pallas_call x1, Pallas kernels, finish(): pl.pallas_call(functools.partial(finish_kernel, head_size), grid_spec=plt...  18.7 us
    pallas_call x3, Pallas kernels, local_attention(): pl.pallas_call(functools.partial(local_kernel, head_size), grid=(steps,),...  13.7 us
    ppermute x5, starting transfers between devices, route(): lax.ppermute(block, 'pts', [(i, target(i) % len(devices)) for i in devices])  11.7 us
    all_to_all x1, starting transfers between devices, swap(): return lax.all_to_all(array, 'pts', split_axis=0, concat_axis=0, tiled=True)  7.47 us
    pallas_call x1, Pallas kernels, send_order(): pl.pallas_call(functools.partial(send_kernel, send_each), grid_spec=pltpu...  6.45 us
    pallas_call x1, Pallas kernels, take_rows(): pl.pallas_call(take_kernel, grid_spec=pltpu.PrefetchScalarGridSpec(num_sc...  4.44 us
  transfers between devices with their start and end apart: 6, of which 2 were waited for; matrix products, arithmetic and copies ran while one was open for 2% of the time, Pallas kernels for 10%

profile of v8, /device:TPU:1, one launch (start us, length us, event | category | flops | bytes accessed | tf_op | source)
XLA Modules:
  0.0 161.8 jit_solution(13365908805960411260)
XLA Ops:
  0.0 6.4 %send_order.1 = (bf16[16,528,128]{2,1,0:T(8,128)(2,1)}, s32[16,128]{1,0:T(8,128)}) custom-call(s32[1]{0:T(128)} %bitcast.me_ref, s32[16,128]{1,0:T(8,128)} %bitcast.38, bf16[2048,512]{1,0:T(8,128)(2,1)} %points_ref.1), custom_call_target="tpu_custom_call" | custom-call | flops 4294967296 | bytes 4194304 | tf_op jit(solution)/shard_map/send_order/pallas_call | solution.py:149
  6.5 0.0 copy-start.10
  6.5 0.0 copy-start.11
  6.5 7.5 %all-to-all-start = ((bf16[16,528,128]{2,1,0:T(8,128)(2,1)}), bf16[16,528,128]{2,1,0:T(8,128)(2,1)S(1)}, u32[]{:S(2)}, u32[]{:S(2)}) async-start(bf16[16,528,128]{2,1,0:T(8,128)(2,1)} %get-tuple-element.33), calls=%async_computation | async-start | bytes 4325376 | tf_op jit(solution)/shard_map/all_to_all | solution.py:655
  13.9 0.0 copy-start.12
  14.0 0.0 copy-start.1
  14.0 0.0 copy-done.10
  14.0 0.2 copy.27
  14.2 1.3 copy.28
  15.5 0.0 copy-done.11
  15.6 0.1 copy.26
  15.7 0.1 reshape.20.chosen_ref
  15.7 2.0 %copy.29 = bf16[512,512]{0,1:T(8,128)(2,1)} copy(bf16[512,512]{1,0:T(8,128)(2,1)} %param.23) | data formatting | bytes 1048576 | tf_op args[8]
  17.8 0.0 copy-done.12
  17.8 38.8 %all-to-all-done.arrived_ref = bf16[16,528,128]{2,1,0:T(8,128)(2,1)S(1)} async-done(((bf16[16,528,128]{2,1,0:T(8,128)(2,1)}), bf16[16,528,128]{2,1,0:T(8,128)(2,1)S(1)}, u32[]{:S(2)}, u32[]{:S(2)}) %all-to-all-start) | async-done | bytes 2162720 | tf_op jit(solution)/shard_map/all_to_all | solution.py:655
  56.6 0.0 copy-done.1
  56.6 1.6 pool_arrived.1
  58.2 6.1 %collective-permute-start = (bf16[256,512]{1,0:T(8,128)(2,1)S(1)}, bf16[256,512]{1,0:T(8,128)(2,1)S(1)}, u32[]{:S(2)}, u32[]{:S(2)}) collective-permute-start(bf16[256,512]{1,0:T(8,128)(2,1)S(1)} %get-tuple-element.35), channel_id=1, source_target_pairs={{0,24},{2,26},{4,12},{6,14},{8,0},{10,2},{12,20},{14,22},{16,8},{1... | collective-permute-start | bytes 786440 | tf_op jit(solution)/shard_map/ppermute | solution.py:610
  64.2 0.3 collective-permute-start.1
  64.5 3.6 %collective-permute-start.2 = (bf16[256,512]{1,0:T(8,128)(2,1)S(1)}, bf16[256,512]{1,0:T(8,128)(2,1)S(1)}, u32[]{:S(2)}, u32[]{:S(2)}) collective-permute-start(bf16[256,512]{1,0:T(8,128)(2,1)S(1)} %get-tuple-element.35), channel_id=1, source_target_pairs={{0,4},{2,6},{4,0},{6,2},{8,12},{10,14},{12,8},{14,10},{16,20},{18,... | collective-permute-start | bytes 786440 | tf_op jit(solution)/shard_map/ppermute | solution.py:610
  68.1 0.0 copy-start.5
  68.1 3.2 %group_balls.1 = (bf16[2048,512]{1,0:T(8,128)(2,1)S(1)}, bf16[2048,512]{1,0:T(8,128)(2,1)S(1)}) custom-call(s32[16,128]{1,0:T(8,128)S(1)} %get-tuple-element.34.places_ref, f32[8192,128]{1,0:T(8,128)S(1)} %get-tuple-element.36.rows_ref, f32[1,512]{1,0:T(1,128)S(1)} %bitcast.34), custom_call_target="tpu_custom_call" | custom-call | flops 4294967296 | bytes 6291456 | tf_op jit(solution)/shard_map/group_balls/pallas_call | solution.py:270
  71.3 0.0 copy-done.5
  71.3 3.5 %local_attention.3 = (bf16[512,2048]{1,0:T(8,128)(2,1)S(1)}, bf16[512,2048]{1,0:T(8,128)(2,1)S(1)}, f32[16,2048]{1,0:T(8,128)S(1)}) custom-call(f32[16]{0:T(128)S(1)} %broadcast_multiply_fusion.scale_ref, bf16[2048,512]{1,0:T(8,128)(2,1)S(1)} %get-tuple-element.37.normed_ref, bf16[512,512]{1,0:T(8,128)(2,1)S(1)} %bitcast.25, bf16[512,512]{1,0:T(8,128)(2,1)S(1)} %copy-done.5, ...), custom_call_target="tpu_custom_call" | custom-call | flops 2684354560 | bytes 3145728 | tf_op jit(solution)/shard_map/local_attention/pallas_call | solution.py:377
  74.8 0.0 collective-permute-done
  74.8 0.1 collective-permute-start.3
  74.9 6.8 %local_attention.4 = (bf16[512,2048]{1,0:T(8,128)(2,1)S(1)}, bf16[512,2048]{1,0:T(8,128)(2,1)S(1)}, f32[16,2048]{1,0:T(8,128)S(1)}) custom-call(f32[16]{0:T(128)S(1)} %broadcast_multiply_fusion.scale_ref, bf16[2048,512]{1,0:T(8,128)(2,1)S(1)} %get-tuple-element.37.normed_ref, ...), custom_call_target="tpu_custom_call", output_to_operand_aliasing={{0}: (5, {}), {1}: (6, {}), {2}: (7, {})} | custom-call | flops 5368709120 | bytes 6291456 | tf_op jit(solution)/shard_map/local_attention/pallas_call | solution.py:377
  81.7 0.0 collective-permute-done.1
  81.7 0.0 collective-permute-done.2
  81.7 0.2 collective-permute-done.3
  82.0 0.1 pad_maximum_fusion
  82.1 1.7 %collective-permute-start.4 = (bf16[4,256,512]{2,1,0:T(8,128)(2,1)S(1)}, bf16[4,256,512]{2,1,0:T(8,128)(2,1)S(1)}, u32[]{:S(2)}, u32[]{:S(2)}) collective-permute-start(bf16[4,256,512]{2,1,0:T(8,128)(2,1)S(1)} %pad_maximum_fusion), channel_id=1, source_target_pairs={{0,2},{2,0},{4,6},{6,4},{8,10},{10,8},{12,14},{14,12},{16,18},{18,... | collective-permute-start | bytes 3145736 | tf_op jit(solution)/shard_map/ppermute | solution.py:610
  83.9 0.0 copy-start
  83.9 0.0 copy-start.2
  83.9 0.0 copy-start.3
  84.0 0.0 copy-start.4
  84.0 0.0 copy-start.6
  84.0 0.0 copy-start.7
  84.0 0.0 copy-start.8
  84.0 3.5 %local_attention.5 = (bf16[512,2048]{1,0:T(8,128)(2,1)S(1)}, bf16[512,2048]{1,0:T(8,128)(2,1)S(1)}, f32[16,2048]{1,0:T(8,128)S(1)}) custom-call(f32[16]{0:T(128)S(1)} %broadcast_multiply_fusion.scale_ref, bf16[2048,512]{1,0:T(8,128)(2,1)S(1)} %get-tuple-element.37.normed_ref, ...), custom_call_target="tpu_custom_call", output_to_operand_aliasing={{0}: (5, {}), {1}: (6, {}), {2}: (7, {})} | custom-call | flops 2684354560 | bytes 3145728 | tf_op jit(solution)/shard_map/local_attention/pallas_call | solution.py:377
  87.5 0.0 collective-permute-done.4
  87.5 0.1 constant_dynamic-update-slice_fusion
  87.6 0.0 copy-done
  87.6 0.0 copy-done.2
  87.6 0.0 copy-done.3
  87.6 0.0 copy-done.4
  87.6 0.0 copy-done.6
  87.6 0.0 copy-done.7
  87.6 0.0 copy-done.8
  87.7 18.7 %finish_balls.1 = bf16[2048,512]{1,0:T(8,128)(2,1)S(1)} custom-call(s32[32]{0:T(128)S(1)} %reshape.20.chosen_ref, s32[16,128]{1,0:T(8,128)S(1)} %get-tuple-element.34.places_ref, bf16[72,32,512]{2,1,0:T(8,128)(2,1)S(1)} %bitcast.32, bf16[512,2048]{1,0:T(8,128)(2,1)S(1)} %get-tuple-element.55.query_ref, bf16[512,2048]{1,0:T(8,128)(2,1)S(1)} %get-tuple-element.56.num_ref, ...), custom_call_target="tpu_custom_call" | custom-call | flops 12884901888 | bytes 12582912 | tf_op jit(solution)/shard_map/finish_balls/pallas_call | solution.py:535
  106.4 0.0 copy-start.9
  106.4 51.0 %all_to_all.10 = bf16[16,128,512]{2,1,0:T(8,128)(2,1)S(1)} all-to-all(bf16[16,128,512]{2,1,0:T(8,128)(2,1)S(1)} %bitcast.22), channel_id=1, replica_groups=mesh['pts'=16,'rep'=2] {'pts'}, dimensions={0} | all-to-all | bytes 4194304 | tf_op jit(solution)/shard_map/all_to_all | solution.py:655
  157.4 0.0 copy-done.9
  157.4 4.4 %take_rows.1 = bf16[2048,512]{1,0:T(8,128)(2,1)} custom-call(s32[16,128]{1,0:T(8,128)S(1)} %copy-done.9, bf16[2048,512]{1,0:T(8,128)(2,1)S(1)} %bitcast.23), custom_call_target="tpu_custom_call" | custom-call | flops 4294967296 | bytes 4194304 | tf_op jit(solution)/shard_map/take_rows/pallas_call | solution.py:587
  (8 shorter events, 0.2 us)
Async XLA Ops:
  6.5 7.5 %copy-start.10 = (bf16[512,512]{1,0:T(8,128)(2,1)S(1)}, bf16[512,512]{1,0:T(8,128)(2,1)}, u32[]{:S(2)}) copy-start(bf16[512,512]{1,0:T(8,128)(2,1)} %param.19) | copy-start | bytes 1572868
  6.5 9.1 %copy-start.11 = (s32[8,4]{0,1:T(4,128)S(1)}, s32[8,4]{0,1:T(4,128)}, u32[]{:S(2)}) copy-start(s32[8,4]{0,1:T(4,128)} %param.17) | copy-start | bytes 388
  6.5 50.1 %all-to-all-start = ((bf16[16,528,128]{2,1,0:T(8,128)(2,1)}), bf16[16,528,128]{2,1,0:T(8,128)(2,1)S(1)}, u32[]{:S(2)}, u32[]{:S(2)}) async-start(bf16[16,528,128]{2,1,0:T(8,128)(2,1)} %get-tuple-element.33), calls=%async_computation | async-start | bytes 4325376 | tf_op jit(solution)/shard_map/all_to_all | solution.py:655
  13.9 3.8 %copy-start.12 = (f32[16]{0:T(128)S(1)}, f32[16]{0:T(128)}, u32[]{:S(2)}) copy-start(f32[16]{0:T(128)} %param.24) | copy-start | bytes 196
  14.0 42.6 %copy-start.1 = (f32[512]{0:T(512)S(1)}, f32[512]{0:T(512)}, u32[]{:S(2)}) copy-start(f32[512]{0:T(512)} %param.18) | copy-start | bytes 6148
  58.2 16.6 %collective-permute-start = (bf16[256,512]{1,0:T(8,128)(2,1)S(1)}, bf16[256,512]{1,0:T(8,128)(2,1)S(1)}, u32[]{:S(2)}, u32[]{:S(2)}) collective-permute-start(bf16[256,512]{1,0:T(8,128)(2,1)S(1)} %get-tuple-element.35), channel_id=1, source_target_pairs={{0,24},{2,26},{4,12},{6,14},{8,0},{10,2},{12,20},{14,22},{16,8},{1... | collective-permute-start | bytes 786440 | tf_op jit(solution)/shard_map/ppermute | solution.py:610
  64.2 17.4 %collective-permute-start.1 = (bf16[256,512]{1,0:T(8,128)(2,1)S(1)}, bf16[256,512]{1,0:T(8,128)(2,1)S(1)}, u32[]{:S(2)}, u32[]{:S(2)}) collective-permute-start(bf16[256,512]{1,0:T(8,128)(2,1)S(1)} %get-tuple-element.35), channel_id=1, source_target_pairs={{0,8},{2,10},{4,28},{6,30},{8,16},{10,18},{12,4},{14,6},{16,24},{1... | collective-permute-start | bytes 786440 | tf_op jit(solution)/shard_map/ppermute | solution.py:610
  64.5 17.1 %collective-permute-start.2 = (bf16[256,512]{1,0:T(8,128)(2,1)S(1)}, bf16[256,512]{1,0:T(8,128)(2,1)S(1)}, u32[]{:S(2)}, u32[]{:S(2)}) collective-permute-start(bf16[256,512]{1,0:T(8,128)(2,1)S(1)} %get-tuple-element.35), channel_id=1, source_target_pairs={{0,4},{2,6},{4,0},{6,2},{8,12},{10,14},{12,8},{14,10},{16,20},{18,... | collective-permute-start | bytes 786440 | tf_op jit(solution)/shard_map/ppermute | solution.py:610
  68.1 3.2 %copy-start.5 = (bf16[512,512]{1,0:T(8,128)(2,1)S(1)}, bf16[512,512]{1,0:T(8,128)(2,1)}, u32[]{:S(2)}) copy-start(bf16[512,512]{1,0:T(8,128)(2,1)} %wk_ref.5) | copy-start | bytes 1572868
  74.8 7.1 %collective-permute-start.3 = (bf16[256,512]{1,0:T(8,128)(2,1)S(1)}, bf16[256,512]{1,0:T(8,128)(2,1)S(1)}, u32[]{:S(2)}, u32[]{:S(2)}) collective-permute-start(bf16[256,512]{1,0:T(8,128)(2,1)S(1)} %collective-permute-done), channel_id=1, source_target_pairs={{0,4},{2,6},{4,0},{6,2},{8,12},{10,14},{12,8},{14,10},{16,20},{18,... | collective-permute-start | bytes 786440 | tf_op jit(solution)/shard_map/ppermute | solution.py:610
  82.1 5.4 %collective-permute-start.4 = (bf16[4,256,512]{2,1,0:T(8,128)(2,1)S(1)}, bf16[4,256,512]{2,1,0:T(8,128)(2,1)S(1)}, u32[]{:S(2)}, u32[]{:S(2)}) collective-permute-start(bf16[4,256,512]{2,1,0:T(8,128)(2,1)S(1)} %pad_maximum_fusion), channel_id=1, source_target_pairs={{0,2},{2,0},{4,6},{6,4},{8,10},{10,8},{12,14},{14,12},{16,18},{18,... | collective-permute-start | bytes 3145736 | tf_op jit(solution)/shard_map/ppermute | solution.py:610
  83.9 3.7 %copy-start = (bf16[512,512]{0,1:T(8,128)(2,1)S(1)}, bf16[512,512]{0,1:T(8,128)(2,1)}, u32[]{:S(2)}) copy-start(bf16[512,512]{0,1:T(8,128)(2,1)} %copy.29) | copy-start | bytes 1572868
  83.9 3.7 %copy-start.2 = (bf16[512,1024]{1,0:T(8,128)(2,1)S(1)}, bf16[512,1024]{1,0:T(8,128)(2,1)}, u32[]{:S(2)}) copy-start(bf16[512,1024]{1,0:T(8,128)(2,1)} %wg_ref.1) | copy-start | bytes 3145732
  83.9 3.7 %copy-start.3 = (bf16[512,1024]{1,0:T(8,128)(2,1)S(1)}, bf16[512,1024]{1,0:T(8,128)(2,1)}, u32[]{:S(2)}) copy-start(bf16[512,1024]{1,0:T(8,128)(2,1)} %wu_ref.1) | copy-start | bytes 3145732
  84.0 3.7 %copy-start.4 = (bf16[1024,512]{1,0:T(8,128)(2,1)S(1)}, bf16[1024,512]{1,0:T(8,128)(2,1)}, u32[]{:S(2)}) copy-start(bf16[1024,512]{1,0:T(8,128)(2,1)} %wd_ref.1) | copy-start | bytes 3145732
  84.0 3.7 %copy-start.6 = (bf16[512,512]{1,0:T(8,128)(2,1)S(1)}, bf16[512,512]{1,0:T(8,128)(2,1)}, u32[]{:S(2)}) copy-start(bf16[512,512]{1,0:T(8,128)(2,1)} %wpk_ref.1) | copy-start | bytes 1572868
  84.0 3.7 %copy-start.7 = (bf16[512,512]{1,0:T(8,128)(2,1)S(1)}, bf16[512,512]{1,0:T(8,128)(2,1)}, u32[]{:S(2)}) copy-start(bf16[512,512]{1,0:T(8,128)(2,1)} %wo_ref.1) | copy-start | bytes 1572868
  84.0 3.7 %copy-start.8 = (f32[512]{0:T(512)S(1)}, f32[512]{0:T(512)}, u32[]{:S(2)}) copy-start(f32[512]{0:T(512)} %param.26) | copy-start | bytes 6148
  106.4 51.0 %copy-start.9 = (s32[16,128]{1,0:T(8,128)S(1)}, s32[16,128]{1,0:T(8,128)}, u32[]{:S(2)}) copy-start(s32[16,128]{1,0:T(8,128)} %get-tuple-element.32.places_ref) | copy-start | bytes 24580

commit v9 on v8

--- a/solution.py
+++ b/solution.py
@@ -13,6 +13,7 @@
 OWNERS = 4
 GROUP = 4
 LANES = 128
+BATCH = 32
 TILE = 1024
 DEPTH = 512
 BALLS_STEP = 4
@@ -55,10 +56,12 @@
 
 def gather_rows(places_ref, first_tile, tiles, source, target, pitch):
     def move(t, carry):
-        places = [places_ref[first_tile + t, l] for l in range(LANES)]
-        rows = [source[pl.ds(pl.multiple_of(p, pitch), pitch), :] for p in places]
-        for l in range(LANES):
-            target[pl.ds(pl.multiple_of((t * LANES + l) * pitch, pitch), pitch), :] = rows[l]
+        for first in range(0, LANES, BATCH):
+            lanes = range(first, first + BATCH)
+            places = [places_ref[first_tile + t, l] for l in lanes]
+            rows = [source[pl.ds(pl.multiple_of(p, pitch), pitch), :] for p in places]
+            for l, row in zip(lanes, rows):
+                target[pl.ds(pl.multiple_of((t * LANES + l) * pitch, pitch), pitch), :] = row
         return carry
 
     lax.fori_loop(0, tiles, move, 0)
@@ -66,12 +69,12 @@
 
 def scatter_rows(places_ref, tiles, source, target, pitch):
     def move(t, carry):
-        places = [places_ref[t, l] for l in range(LANES)]
-        rows = [
-            source[pl.ds(pl.multiple_of((t * LANES + l) * pitch, pitch), pitch), :] for l in range(LANES)
-        ]
-        for l in range(LANES):
-            target[pl.ds(pl.multiple_of(places[l], pitch), pitch), :] = rows[l]
+        for first in range(0, LANES, BATCH):
+            lanes = range(first, first + BATCH)
+            places = [places_ref[t, l] for l in lanes]
+            rows = [source[pl.ds(pl.multiple_of((t * LANES + l) * pitch, pitch), pitch), :] for l in lanes]
+            for place, row in zip(places, rows):
+                target[pl.ds(pl.multiple_of(place, pitch), pitch), :] = row
         return carry
 
     lax.fori_loop(0, tiles, move, 0)
@@ -514,9 +517,13 @@
     residual = (grouped_ref[...].astype(F32) + projected).astype(BF16)
     rows32 = residual.astype(F32)
     ffn = normed_rows(rows32, gain_ref[...])
-    gate = dot(ffn, wg_ref[...])
-    up = dot(ffn, wu_ref[...])
-    hidden = (0.5 * gate * (1.0 + jnp.tanh(0.5 * gate)) * up).astype(BF16)
+    parts = []
+    for first_col in range(0, wg_ref.shape[1], 2 * LANES):
+        cols = slice(first_col, first_col + 2 * LANES)
+        gate = dot(ffn, wg_ref[:, cols])
+        up = dot(ffn, wu_ref[:, cols])
+        parts.append((0.5 * gate * (1.0 + jnp.tanh(0.5 * gate)) * up).astype(BF16))
+    hidden = jnp.concatenate(parts, axis=1)
     return rows32 + dot(hidden, wd_ref[...])
 
 

time: 162 us -> 162 us (level)
  no operation moved by 1% of the time
where the time goes in v9:
time: 162 us
  blocking collectives  51 us (31%)
  Pallas kernels  47.8 us (30%)
  waiting for transfers between devices  39 us (24%)
  starting transfers between devices  19.2 us (12%)
  local copies, waits for them, and re-layouts  3.92 us (2%)
    all_to_all x1, blocking collectives, swap(): return lax.all_to_all(array, 'pts', split_axis=0, concat_axis=0, tiled=True)  51 us
    all_to_all x1, waiting for transfers between devices, swap(): return lax.all_to_all(array, 'pts', split_axis=0, concat_axis=0, tiled=True)  38.8 us
    pallas_call x1, Pallas kernels, finish(): pl.pallas_call(functools.partial(finish_kernel, head_size), grid_spec=plt...  18.4 us
    pallas_call x3, Pallas kernels, local_attention(): pl.pallas_call(functools.partial(local_kernel, head_size), grid=(steps,),...  13.7 us
    ppermute x5, starting transfers between devices, route(): lax.ppermute(block, 'pts', [(i, target(i) % len(devices)) for i in devices])  11.7 us
    all_to_all x1, starting transfers between devices, swap(): return lax.all_to_all(array, 'pts', split_axis=0, concat_axis=0, tiled=True)  7.47 us
    pallas_call x1, Pallas kernels, send_order(): pl.pallas_call(functools.partial(send_kernel, send_each), grid_spec=pltpu...  6.45 us
    pallas_call x1, Pallas kernels, take_rows(): pl.pallas_call(take_kernel, grid_spec=pltpu.PrefetchScalarGridSpec(num_sc...  4.44 us
  transfers between devices with their start and end apart: 6, of which 2 were waited for; matrix products, arithmetic and copies ran while one was open for 2% of the time, Pallas kernels for 10%

profile of v9, /device:TPU:1, one launch (start us, length us, event | category | flops | bytes accessed | tf_op | source)
XLA Modules:
  0.0 161.5 jit_solution(14335597068182928109)
XLA Ops:
  0.0 6.4 %send_order.1 = (bf16[16,528,128]{2,1,0:T(8,128)(2,1)}, s32[16,128]{1,0:T(8,128)}) custom-call(s32[1]{0:T(128)} %bitcast.me_ref, s32[16,128]{1,0:T(8,128)} %bitcast.38, bf16[2048,512]{1,0:T(8,128)(2,1)} %points_ref.1), custom_call_target="tpu_custom_call" | custom-call | flops 4294967296 | bytes 4194304 | tf_op jit(solution)/shard_map/send_order/pallas_call | solution.py:152
  6.5 0.0 copy-start.10
  6.5 0.0 copy-start.11
  6.5 7.5 %all-to-all-start = ((bf16[16,528,128]{2,1,0:T(8,128)(2,1)}), bf16[16,528,128]{2,1,0:T(8,128)(2,1)S(1)}, u32[]{:S(2)}, u32[]{:S(2)}) async-start(bf16[16,528,128]{2,1,0:T(8,128)(2,1)} %get-tuple-element.33), calls=%async_computation | async-start | bytes 4325376 | tf_op jit(solution)/shard_map/all_to_all | solution.py:662
  13.9 0.0 copy-start.12
  14.0 0.0 copy-start.1
  14.0 0.0 copy-done.10
  14.0 0.2 copy.27
  14.2 1.3 copy.28
  15.5 0.0 copy-done.11
  15.6 0.1 copy.26
  15.7 0.1 reshape.20.chosen_ref
  15.7 2.0 %copy.29 = bf16[512,512]{0,1:T(8,128)(2,1)} copy(bf16[512,512]{1,0:T(8,128)(2,1)} %param.23) | data formatting | bytes 1048576 | tf_op args[8]
  17.8 0.0 copy-done.12
  17.8 38.8 %all-to-all-done.arrived_ref = bf16[16,528,128]{2,1,0:T(8,128)(2,1)S(1)} async-done(((bf16[16,528,128]{2,1,0:T(8,128)(2,1)}), bf16[16,528,128]{2,1,0:T(8,128)(2,1)S(1)}, u32[]{:S(2)}, u32[]{:S(2)}) %all-to-all-start) | async-done | bytes 2162720 | tf_op jit(solution)/shard_map/all_to_all | solution.py:662
  56.6 0.0 copy-done.1
  56.6 1.6 pool_arrived.1
  58.2 6.1 %collective-permute-start = (bf16[256,512]{1,0:T(8,128)(2,1)S(1)}, bf16[256,512]{1,0:T(8,128)(2,1)S(1)}, u32[]{:S(2)}, u32[]{:S(2)}) collective-permute-start(bf16[256,512]{1,0:T(8,128)(2,1)S(1)} %get-tuple-element.35), channel_id=1, source_target_pairs={{0,24},{2,26},{4,12},{6,14},{8,0},{10,2},{12,20},{14,22},{16,8},{1... | collective-permute-start | bytes 786440 | tf_op jit(solution)/shard_map/ppermute | solution.py:617
  64.2 0.3 collective-permute-start.1
  64.5 3.6 %collective-permute-start.2 = (bf16[256,512]{1,0:T(8,128)(2,1)S(1)}, bf16[256,512]{1,0:T(8,128)(2,1)S(1)}, u32[]{:S(2)}, u32[]{:S(2)}) collective-permute-start(bf16[256,512]{1,0:T(8,128)(2,1)S(1)} %get-tuple-element.35), channel_id=1, source_target_pairs={{0,4},{2,6},{4,0},{6,2},{8,12},{10,14},{12,8},{14,10},{16,20},{18,... | collective-permute-start | bytes 786440 | tf_op jit(solution)/shard_map/ppermute | solution.py:617
  68.1 0.0 copy-start.5
  68.1 3.2 %group_balls.1 = (bf16[2048,512]{1,0:T(8,128)(2,1)S(1)}, bf16[2048,512]{1,0:T(8,128)(2,1)S(1)}) custom-call(s32[16,128]{1,0:T(8,128)S(1)} %get-tuple-element.34.places_ref, f32[8192,128]{1,0:T(8,128)S(1)} %get-tuple-element.36.rows_ref, f32[1,512]{1,0:T(1,128)S(1)} %bitcast.34), custom_call_target="tpu_custom_call" | custom-call | flops 4294967296 | bytes 6291456 | tf_op jit(solution)/shard_map/group_balls/pallas_call | solution.py:273
  71.3 0.0 copy-done.5
  71.3 3.5 %local_attention.3 = (bf16[512,2048]{1,0:T(8,128)(2,1)S(1)}, bf16[512,2048]{1,0:T(8,128)(2,1)S(1)}, f32[16,2048]{1,0:T(8,128)S(1)}) custom-call(f32[16]{0:T(128)S(1)} %broadcast_multiply_fusion.scale_ref, bf16[2048,512]{1,0:T(8,128)(2,1)S(1)} %get-tuple-element.37.normed_ref, bf16[512,512]{1,0:T(8,128)(2,1)S(1)} %bitcast.25, bf16[512,512]{1,0:T(8,128)(2,1)S(1)} %copy-done.5, ...), custom_call_target="tpu_custom_call" | custom-call | flops 2684354560 | bytes 3145728 | tf_op jit(solution)/shard_map/local_attention/pallas_call | solution.py:380
  74.8 0.0 collective-permute-done
  74.8 0.1 collective-permute-start.3
  74.9 6.8 %local_attention.4 = (bf16[512,2048]{1,0:T(8,128)(2,1)S(1)}, bf16[512,2048]{1,0:T(8,128)(2,1)S(1)}, f32[16,2048]{1,0:T(8,128)S(1)}) custom-call(f32[16]{0:T(128)S(1)} %broadcast_multiply_fusion.scale_ref, bf16[2048,512]{1,0:T(8,128)(2,1)S(1)} %get-tuple-element.37.normed_ref, ...), custom_call_target="tpu_custom_call", output_to_operand_aliasing={{0}: (5, {}), {1}: (6, {}), {2}: (7, {})} | custom-call | flops 5368709120 | bytes 6291456 | tf_op jit(solution)/shard_map/local_attention/pallas_call | solution.py:380
  81.7 0.0 collective-permute-done.1
  81.7 0.0 collective-permute-done.2
  81.7 0.2 collective-permute-done.3
  82.0 0.1 pad_maximum_fusion
  82.1 1.7 %collective-permute-start.4 = (bf16[4,256,512]{2,1,0:T(8,128)(2,1)S(1)}, bf16[4,256,512]{2,1,0:T(8,128)(2,1)S(1)}, u32[]{:S(2)}, u32[]{:S(2)}) collective-permute-start(bf16[4,256,512]{2,1,0:T(8,128)(2,1)S(1)} %pad_maximum_fusion), channel_id=1, source_target_pairs={{0,2},{2,0},{4,6},{6,4},{8,10},{10,8},{12,14},{14,12},{16,18},{18,... | collective-permute-start | bytes 3145736 | tf_op jit(solution)/shard_map/ppermute | solution.py:617
  83.9 0.0 copy-start
  83.9 0.0 copy-start.2
  83.9 0.0 copy-start.3
  84.0 0.0 copy-start.4
  84.0 0.0 copy-start.6
  84.0 0.0 copy-start.7
  84.0 0.0 copy-start.8
  84.0 3.5 %local_attention.5 = (bf16[512,2048]{1,0:T(8,128)(2,1)S(1)}, bf16[512,2048]{1,0:T(8,128)(2,1)S(1)}, f32[16,2048]{1,0:T(8,128)S(1)}) custom-call(f32[16]{0:T(128)S(1)} %broadcast_multiply_fusion.scale_ref, bf16[2048,512]{1,0:T(8,128)(2,1)S(1)} %get-tuple-element.37.normed_ref, ...), custom_call_target="tpu_custom_call", output_to_operand_aliasing={{0}: (5, {}), {1}: (6, {}), {2}: (7, {})} | custom-call | flops 2684354560 | bytes 3145728 | tf_op jit(solution)/shard_map/local_attention/pallas_call | solution.py:380
  87.5 0.0 collective-permute-done.4
  87.5 0.1 constant_dynamic-update-slice_fusion
  87.6 0.0 copy-done
  87.6 0.0 copy-done.2
  87.6 0.0 copy-done.3
  87.6 0.0 copy-done.4
  87.6 0.0 copy-done.6
  87.6 0.0 copy-done.7
  87.6 0.0 copy-done.8
  87.7 18.4 %finish_balls.1 = bf16[2048,512]{1,0:T(8,128)(2,1)S(1)} custom-call(s32[32]{0:T(128)S(1)} %reshape.20.chosen_ref, s32[16,128]{1,0:T(8,128)S(1)} %get-tuple-element.34.places_ref, bf16[72,32,512]{2,1,0:T(8,128)(2,1)S(1)} %bitcast.32, bf16[512,2048]{1,0:T(8,128)(2,1)S(1)} %get-tuple-element.55.query_ref, bf16[512,2048]{1,0:T(8,128)(2,1)S(1)} %get-tuple-element.56.num_ref, ...), custom_call_target="tpu_custom_call" | custom-call | flops 12884901888 | bytes 12582912 | tf_op jit(solution)/shard_map/finish_balls/pallas_call | solution.py:542
  106.1 0.0 copy-start.9
  106.1 51.0 %all_to_all.10 = bf16[16,128,512]{2,1,0:T(8,128)(2,1)S(1)} all-to-all(bf16[16,128,512]{2,1,0:T(8,128)(2,1)S(1)} %bitcast.22), channel_id=1, replica_groups=mesh['pts'=16,'rep'=2] {'pts'}, dimensions={0} | all-to-all | bytes 4194304 | tf_op jit(solution)/shard_map/all_to_all | solution.py:662
  157.1 0.0 copy-done.9
  157.1 4.4 %take_rows.1 = bf16[2048,512]{1,0:T(8,128)(2,1)} custom-call(s32[16,128]{1,0:T(8,128)S(1)} %copy-done.9, bf16[2048,512]{1,0:T(8,128)(2,1)S(1)} %bitcast.23), custom_call_target="tpu_custom_call" | custom-call | flops 4294967296 | bytes 4194304 | tf_op jit(solution)/shard_map/take_rows/pallas_call | solution.py:594
  (8 shorter events, 0.2 us)
Async XLA Ops:
  6.5 7.5 %copy-start.10 = (bf16[512,512]{1,0:T(8,128)(2,1)S(1)}, bf16[512,512]{1,0:T(8,128)(2,1)}, u32[]{:S(2)}) copy-start(bf16[512,512]{1,0:T(8,128)(2,1)} %param.19) | copy-start | bytes 1572868
  6.5 9.1 %copy-start.11 = (s32[8,4]{0,1:T(4,128)S(1)}, s32[8,4]{0,1:T(4,128)}, u32[]{:S(2)}) copy-start(s32[8,4]{0,1:T(4,128)} %param.17) | copy-start | bytes 388
  6.5 50.1 %all-to-all-start = ((bf16[16,528,128]{2,1,0:T(8,128)(2,1)}), bf16[16,528,128]{2,1,0:T(8,128)(2,1)S(1)}, u32[]{:S(2)}, u32[]{:S(2)}) async-start(bf16[16,528,128]{2,1,0:T(8,128)(2,1)} %get-tuple-element.33), calls=%async_computation | async-start | bytes 4325376 | tf_op jit(solution)/shard_map/all_to_all | solution.py:662
  13.9 3.8 %copy-start.12 = (f32[16]{0:T(128)S(1)}, f32[16]{0:T(128)}, u32[]{:S(2)}) copy-start(f32[16]{0:T(128)} %param.24) | copy-start | bytes 196
  14.0 42.6 %copy-start.1 = (f32[512]{0:T(512)S(1)}, f32[512]{0:T(512)}, u32[]{:S(2)}) copy-start(f32[512]{0:T(512)} %param.18) | copy-start | bytes 6148
  58.2 16.6 %collective-permute-start = (bf16[256,512]{1,0:T(8,128)(2,1)S(1)}, bf16[256,512]{1,0:T(8,128)(2,1)S(1)}, u32[]{:S(2)}, u32[]{:S(2)}) collective-permute-start(bf16[256,512]{1,0:T(8,128)(2,1)S(1)} %get-tuple-element.35), channel_id=1, source_target_pairs={{0,24},{2,26},{4,12},{6,14},{8,0},{10,2},{12,20},{14,22},{16,8},{1... | collective-permute-start | bytes 786440 | tf_op jit(solution)/shard_map/ppermute | solution.py:617
  64.2 17.4 %collective-permute-start.1 = (bf16[256,512]{1,0:T(8,128)(2,1)S(1)}, bf16[256,512]{1,0:T(8,128)(2,1)S(1)}, u32[]{:S(2)}, u32[]{:S(2)}) collective-permute-start(bf16[256,512]{1,0:T(8,128)(2,1)S(1)} %get-tuple-element.35), channel_id=1, source_target_pairs={{0,8},{2,10},{4,28},{6,30},{8,16},{10,18},{12,4},{14,6},{16,24},{1... | collective-permute-start | bytes 786440 | tf_op jit(solution)/shard_map/ppermute | solution.py:617
  64.5 17.1 %collective-permute-start.2 = (bf16[256,512]{1,0:T(8,128)(2,1)S(1)}, bf16[256,512]{1,0:T(8,128)(2,1)S(1)}, u32[]{:S(2)}, u32[]{:S(2)}) collective-permute-start(bf16[256,512]{1,0:T(8,128)(2,1)S(1)} %get-tuple-element.35), channel_id=1, source_target_pairs={{0,4},{2,6},{4,0},{6,2},{8,12},{10,14},{12,8},{14,10},{16,20},{18,... | collective-permute-start | bytes 786440 | tf_op jit(solution)/shard_map/ppermute | solution.py:617
  68.1 3.2 %copy-start.5 = (bf16[512,512]{1,0:T(8,128)(2,1)S(1)}, bf16[512,512]{1,0:T(8,128)(2,1)}, u32[]{:S(2)}) copy-start(bf16[512,512]{1,0:T(8,128)(2,1)} %wk_ref.5) | copy-start | bytes 1572868
  74.8 7.1 %collective-permute-start.3 = (bf16[256,512]{1,0:T(8,128)(2,1)S(1)}, bf16[256,512]{1,0:T(8,128)(2,1)S(1)}, u32[]{:S(2)}, u32[]{:S(2)}) collective-permute-start(bf16[256,512]{1,0:T(8,128)(2,1)S(1)} %collective-permute-done), channel_id=1, source_target_pairs={{0,4},{2,6},{4,0},{6,2},{8,12},{10,14},{12,8},{14,10},{16,20},{18,... | collective-permute-start | bytes 786440 | tf_op jit(solution)/shard_map/ppermute | solution.py:617
  82.1 5.4 %collective-permute-start.4 = (bf16[4,256,512]{2,1,0:T(8,128)(2,1)S(1)}, bf16[4,256,512]{2,1,0:T(8,128)(2,1)S(1)}, u32[]{:S(2)}, u32[]{:S(2)}) collective-permute-start(bf16[4,256,512]{2,1,0:T(8,128)(2,1)S(1)} %pad_maximum_fusion), channel_id=1, source_target_pairs={{0,2},{2,0},{4,6},{6,4},{8,10},{10,8},{12,14},{14,12},{16,18},{18,... | collective-permute-start | bytes 3145736 | tf_op jit(solution)/shard_map/ppermute | solution.py:617
  83.9 3.7 %copy-start = (bf16[512,512]{0,1:T(8,128)(2,1)S(1)}, bf16[512,512]{0,1:T(8,128)(2,1)}, u32[]{:S(2)}) copy-start(bf16[512,512]{0,1:T(8,128)(2,1)} %copy.29) | copy-start | bytes 1572868
  83.9 3.7 %copy-start.2 = (bf16[512,1024]{1,0:T(8,128)(2,1)S(1)}, bf16[512,1024]{1,0:T(8,128)(2,1)}, u32[]{:S(2)}) copy-start(bf16[512,1024]{1,0:T(8,128)(2,1)} %wg_ref.1) | copy-start | bytes 3145732
  83.9 3.7 %copy-start.3 = (bf16[512,1024]{1,0:T(8,128)(2,1)S(1)}, bf16[512,1024]{1,0:T(8,128)(2,1)}, u32[]{:S(2)}) copy-start(bf16[512,1024]{1,0:T(8,128)(2,1)} %wu_ref.1) | copy-start | bytes 3145732
  84.0 3.7 %copy-start.4 = (bf16[1024,512]{1,0:T(8,128)(2,1)S(1)}, bf16[1024,512]{1,0:T(8,128)(2,1)}, u32[]{:S(2)}) copy-start(bf16[1024,512]{1,0:T(8,128)(2,1)} %wd_ref.1) | copy-start | bytes 3145732
  84.0 3.7 %copy-start.6 = (bf16[512,512]{1,0:T(8,128)(2,1)S(1)}, bf16[512,512]{1,0:T(8,128)(2,1)}, u32[]{:S(2)}) copy-start(bf16[512,512]{1,0:T(8,128)(2,1)} %wpk_ref.1) | copy-start | bytes 1572868
  84.0 3.7 %copy-start.7 = (bf16[512,512]{1,0:T(8,128)(2,1)S(1)}, bf16[512,512]{1,0:T(8,128)(2,1)}, u32[]{:S(2)}) copy-start(bf16[512,512]{1,0:T(8,128)(2,1)} %wo_ref.1) | copy-start | bytes 1572868
  84.0 3.7 %copy-start.8 = (f32[512]{0:T(512)S(1)}, f32[512]{0:T(512)}, u32[]{:S(2)}) copy-start(f32[512]{0:T(512)} %param.26) | copy-start | bytes 6148
  106.1 51.0 %copy-start.9 = (s32[16,128]{1,0:T(8,128)S(1)}, s32[16,128]{1,0:T(8,128)}, u32[]{:S(2)}) copy-start(s32[16,128]{1,0:T(8,128)} %get-tuple-element.32.places_ref) | copy-start | bytes 24580

commit v10 on v9

--- a/solution.py
+++ b/solution.py
@@ -15,7 +15,7 @@
 LANES = 128
 BATCH = 32
 TILE = 1024
-DEPTH = 512
+DEPTH = 256
 BALLS_STEP = 4
 LOW = 64
 SEND_PITCH = 8

time: 162 us -> 162 us (level)
  no operation moved by 1% of the time
where the time goes in v10:
time: 162 us; the launch traced here: 161 us
  blocking collectives  51 us (31%)
  Pallas kernels  47.7 us (29%)
  waiting for transfers between devices  39 us (24%)
  starting transfers between devices  19.2 us (12%)
  local copies, waits for them, and re-layouts  3.92 us (2%)
    all_to_all x1, blocking collectives, swap(): return lax.all_to_all(array, 'pts', split_axis=0, concat_axis=0, tiled=True)  51 us
    all_to_all x1, waiting for transfers between devices, swap(): return lax.all_to_all(array, 'pts', split_axis=0, concat_axis=0, tiled=True)  38.8 us
    pallas_call x1, Pallas kernels, finish(): pl.pallas_call(functools.partial(finish_kernel, head_size), grid_spec=plt...  18.4 us
    pallas_call x3, Pallas kernels, local_attention(): pl.pallas_call(functools.partial(local_kernel, head_size), grid=(steps,),...  13.7 us
    ppermute x5, starting transfers between devices, route(): lax.ppermute(block, 'pts', [(i, target(i) % len(devices)) for i in devices])  11.7 us
    all_to_all x1, starting transfers between devices, swap(): return lax.all_to_all(array, 'pts', split_axis=0, concat_axis=0, tiled=True)  7.47 us
    pallas_call x1, Pallas kernels, send_order(): pl.pallas_call(functools.partial(send_kernel, send_each), grid_spec=pltpu...  6.37 us
    pallas_call x1, Pallas kernels, take_rows(): pl.pallas_call(take_kernel, grid_spec=pltpu.PrefetchScalarGridSpec(num_sc...  4.36 us
  transfers between devices with their start and end apart: 6, of which 2 were waited for; matrix products, arithmetic and copies ran while one was open for 2% of the time, Pallas kernels for 10%

profile of v10, /device:TPU:1, one launch (start us, length us, event | category | flops | bytes accessed | tf_op | source)
XLA Modules:
  0.0 161.4 jit_solution(14583022654351864818)
XLA Ops:
  0.0 6.4 %send_order.1 = (bf16[16,528,128]{2,1,0:T(8,128)(2,1)}, s32[16,128]{1,0:T(8,128)}) custom-call(s32[1]{0:T(128)} %bitcast.me_ref, s32[16,128]{1,0:T(8,128)} %bitcast.38, bf16[2048,512]{1,0:T(8,128)(2,1)} %points_ref.1), custom_call_target="tpu_custom_call" | custom-call | flops 4294967296 | bytes 4194304 | tf_op jit(solution)/shard_map/send_order/pallas_call | solution.py:152
  6.4 0.0 copy-start.10
  6.4 0.0 copy-start.11
  6.4 7.5 %all-to-all-start = ((bf16[16,528,128]{2,1,0:T(8,128)(2,1)}), bf16[16,528,128]{2,1,0:T(8,128)(2,1)S(1)}, u32[]{:S(2)}, u32[]{:S(2)}) async-start(bf16[16,528,128]{2,1,0:T(8,128)(2,1)} %get-tuple-element.33), calls=%async_computation | async-start | bytes 4325376 | tf_op jit(solution)/shard_map/all_to_all | solution.py:662
  13.9 0.0 copy-start.12
  13.9 0.0 copy-start.1
  13.9 0.0 copy-done.10
  13.9 0.2 copy.27
  14.2 1.3 copy.28
  15.4 0.0 copy-done.11
  15.5 0.1 copy.26
  15.6 0.1 reshape.20.chosen_ref
  15.7 2.0 %copy.29 = bf16[512,512]{0,1:T(8,128)(2,1)} copy(bf16[512,512]{1,0:T(8,128)(2,1)} %param.23) | data formatting | bytes 1048576 | tf_op args[8]
  17.7 0.0 copy-done.12
  17.7 38.8 %all-to-all-done.arrived_ref = bf16[16,528,128]{2,1,0:T(8,128)(2,1)S(1)} async-done(((bf16[16,528,128]{2,1,0:T(8,128)(2,1)}), bf16[16,528,128]{2,1,0:T(8,128)(2,1)S(1)}, u32[]{:S(2)}, u32[]{:S(2)}) %all-to-all-start) | async-done | bytes 2162720 | tf_op jit(solution)/shard_map/all_to_all | solution.py:662
  56.5 0.0 copy-done.1
  56.5 1.6 pool_arrived.1
  58.1 6.1 %collective-permute-start = (bf16[256,512]{1,0:T(8,128)(2,1)S(1)}, bf16[256,512]{1,0:T(8,128)(2,1)S(1)}, u32[]{:S(2)}, u32[]{:S(2)}) collective-permute-start(bf16[256,512]{1,0:T(8,128)(2,1)S(1)} %get-tuple-element.35), channel_id=1, source_target_pairs={{0,24},{2,26},{4,12},{6,14},{8,0},{10,2},{12,20},{14,22},{16,8},{1... | collective-permute-start | bytes 786440 | tf_op jit(solution)/shard_map/ppermute | solution.py:617
  64.2 0.3 collective-permute-start.1
  64.5 3.6 %collective-permute-start.2 = (bf16[256,512]{1,0:T(8,128)(2,1)S(1)}, bf16[256,512]{1,0:T(8,128)(2,1)S(1)}, u32[]{:S(2)}, u32[]{:S(2)}) collective-permute-start(bf16[256,512]{1,0:T(8,128)(2,1)S(1)} %get-tuple-element.35), channel_id=1, source_target_pairs={{0,4},{2,6},{4,0},{6,2},{8,12},{10,14},{12,8},{14,10},{16,20},{18,... | collective-permute-start | bytes 786440 | tf_op jit(solution)/shard_map/ppermute | solution.py:617
  68.0 0.0 copy-start.5
  68.0 3.2 %group_balls.1 = (bf16[2048,512]{1,0:T(8,128)(2,1)S(1)}, bf16[2048,512]{1,0:T(8,128)(2,1)S(1)}) custom-call(s32[16,128]{1,0:T(8,128)S(1)} %get-tuple-element.34.places_ref, f32[8192,128]{1,0:T(8,128)S(1)} %get-tuple-element.36.rows_ref, f32[1,512]{1,0:T(1,128)S(1)} %bitcast.34), custom_call_target="tpu_custom_call" | custom-call | flops 4294967296 | bytes 6291456 | tf_op jit(solution)/shard_map/group_balls/pallas_call | solution.py:273
  71.2 0.0 copy-done.5
  71.2 3.5 %local_attention.3 = (bf16[512,2048]{1,0:T(8,128)(2,1)S(1)}, bf16[512,2048]{1,0:T(8,128)(2,1)S(1)}, f32[16,2048]{1,0:T(8,128)S(1)}) custom-call(f32[16]{0:T(128)S(1)} %broadcast_multiply_fusion.scale_ref, bf16[2048,512]{1,0:T(8,128)(2,1)S(1)} %get-tuple-element.37.normed_ref, bf16[512,512]{1,0:T(8,128)(2,1)S(1)} %bitcast.25, bf16[512,512]{1,0:T(8,128)(2,1)S(1)} %copy-done.5, ...), custom_call_target="tpu_custom_call" | custom-call | flops 2684354560 | bytes 3145728 | tf_op jit(solution)/shard_map/local_attention/pallas_call | solution.py:380
  74.7 0.0 collective-permute-done
  74.7 0.1 collective-permute-start.3
  74.8 6.8 %local_attention.4 = (bf16[512,2048]{1,0:T(8,128)(2,1)S(1)}, bf16[512,2048]{1,0:T(8,128)(2,1)S(1)}, f32[16,2048]{1,0:T(8,128)S(1)}) custom-call(f32[16]{0:T(128)S(1)} %broadcast_multiply_fusion.scale_ref, bf16[2048,512]{1,0:T(8,128)(2,1)S(1)} %get-tuple-element.37.normed_ref, ...), custom_call_target="tpu_custom_call", output_to_operand_aliasing={{0}: (5, {}), {1}: (6, {}), {2}: (7, {})} | custom-call | flops 5368709120 | bytes 6291456 | tf_op jit(solution)/shard_map/local_attention/pallas_call | solution.py:380
  81.6 0.0 collective-permute-done.1
  81.6 0.0 collective-permute-done.2
  81.6 0.2 collective-permute-done.3
  81.9 0.1 pad_maximum_fusion
  82.0 1.7 %collective-permute-start.4 = (bf16[4,256,512]{2,1,0:T(8,128)(2,1)S(1)}, bf16[4,256,512]{2,1,0:T(8,128)(2,1)S(1)}, u32[]{:S(2)}, u32[]{:S(2)}) collective-permute-start(bf16[4,256,512]{2,1,0:T(8,128)(2,1)S(1)} %pad_maximum_fusion), channel_id=1, source_target_pairs={{0,2},{2,0},{4,6},{6,4},{8,10},{10,8},{12,14},{14,12},{16,18},{18,... | collective-permute-start | bytes 3145736 | tf_op jit(solution)/shard_map/ppermute | solution.py:617
  83.8 0.0 copy-start
  83.9 0.0 copy-start.2
  83.9 0.0 copy-start.3
  83.9 0.0 copy-start.4
  83.9 0.0 copy-start.6
  83.9 0.0 copy-start.7
  83.9 0.0 copy-start.8
  83.9 3.5 %local_attention.5 = (bf16[512,2048]{1,0:T(8,128)(2,1)S(1)}, bf16[512,2048]{1,0:T(8,128)(2,1)S(1)}, f32[16,2048]{1,0:T(8,128)S(1)}) custom-call(f32[16]{0:T(128)S(1)} %broadcast_multiply_fusion.scale_ref, bf16[2048,512]{1,0:T(8,128)(2,1)S(1)} %get-tuple-element.37.normed_ref, ...), custom_call_target="tpu_custom_call", output_to_operand_aliasing={{0}: (5, {}), {1}: (6, {}), {2}: (7, {})} | custom-call | flops 2684354560 | bytes 3145728 | tf_op jit(solution)/shard_map/local_attention/pallas_call | solution.py:380
  87.4 0.0 collective-permute-done.4
  87.4 0.1 constant_dynamic-update-slice_fusion
  87.5 0.0 copy-done
  87.5 0.0 copy-done.2
  87.5 0.0 copy-done.3
  87.5 0.0 copy-done.4
  87.6 0.0 copy-done.6
  87.6 0.0 copy-done.7
  87.6 0.0 copy-done.8
  87.6 18.4 %finish_balls.1 = bf16[2048,512]{1,0:T(8,128)(2,1)S(1)} custom-call(s32[32]{0:T(128)S(1)} %reshape.20.chosen_ref, s32[16,128]{1,0:T(8,128)S(1)} %get-tuple-element.34.places_ref, bf16[72,32,512]{2,1,0:T(8,128)(2,1)S(1)} %bitcast.32, bf16[512,2048]{1,0:T(8,128)(2,1)S(1)} %get-tuple-element.55.query_ref, bf16[512,2048]{1,0:T(8,128)(2,1)S(1)} %get-tuple-element.56.num_ref, ...), custom_call_target="tpu_custom_call" | custom-call | flops 12884901888 | bytes 12582912 | tf_op jit(solution)/shard_map/finish_balls/pallas_call | solution.py:542
  106.0 0.0 copy-start.9
  106.0 51.0 %all_to_all.10 = bf16[16,128,512]{2,1,0:T(8,128)(2,1)S(1)} all-to-all(bf16[16,128,512]{2,1,0:T(8,128)(2,1)S(1)} %bitcast.22), channel_id=1, replica_groups=mesh['pts'=16,'rep'=2] {'pts'}, dimensions={0} | all-to-all | bytes 4194304 | tf_op jit(solution)/shard_map/all_to_all | solution.py:662
  157.0 0.0 copy-done.9
  157.0 4.4 %take_rows.1 = bf16[2048,512]{1,0:T(8,128)(2,1)} custom-call(s32[16,128]{1,0:T(8,128)S(1)} %copy-done.9, bf16[2048,512]{1,0:T(8,128)(2,1)S(1)} %bitcast.23), custom_call_target="tpu_custom_call" | custom-call | flops 4294967296 | bytes 4194304 | tf_op jit(solution)/shard_map/take_rows/pallas_call | solution.py:594
  (8 shorter events, 0.2 us)
Async XLA Ops:
  6.4 7.5 %copy-start.10 = (bf16[512,512]{1,0:T(8,128)(2,1)S(1)}, bf16[512,512]{1,0:T(8,128)(2,1)}, u32[]{:S(2)}) copy-start(bf16[512,512]{1,0:T(8,128)(2,1)} %param.19) | copy-start | bytes 1572868
  6.4 9.1 %copy-start.11 = (s32[8,4]{0,1:T(4,128)S(1)}, s32[8,4]{0,1:T(4,128)}, u32[]{:S(2)}) copy-start(s32[8,4]{0,1:T(4,128)} %param.17) | copy-start | bytes 388
  6.4 50.1 %all-to-all-start = ((bf16[16,528,128]{2,1,0:T(8,128)(2,1)}), bf16[16,528,128]{2,1,0:T(8,128)(2,1)S(1)}, u32[]{:S(2)}, u32[]{:S(2)}) async-start(bf16[16,528,128]{2,1,0:T(8,128)(2,1)} %get-tuple-element.33), calls=%async_computation | async-start | bytes 4325376 | tf_op jit(solution)/shard_map/all_to_all | solution.py:662
  13.9 3.8 %copy-start.12 = (f32[16]{0:T(128)S(1)}, f32[16]{0:T(128)}, u32[]{:S(2)}) copy-start(f32[16]{0:T(128)} %param.24) | copy-start | bytes 196
  13.9 42.6 %copy-start.1 = (f32[512]{0:T(512)S(1)}, f32[512]{0:T(512)}, u32[]{:S(2)}) copy-start(f32[512]{0:T(512)} %param.18) | copy-start | bytes 6148
  58.1 16.6 %collective-permute-start = (bf16[256,512]{1,0:T(8,128)(2,1)S(1)}, bf16[256,512]{1,0:T(8,128)(2,1)S(1)}, u32[]{:S(2)}, u32[]{:S(2)}) collective-permute-start(bf16[256,512]{1,0:T(8,128)(2,1)S(1)} %get-tuple-element.35), channel_id=1, source_target_pairs={{0,24},{2,26},{4,12},{6,14},{8,0},{10,2},{12,20},{14,22},{16,8},{1... | collective-permute-start | bytes 786440 | tf_op jit(solution)/shard_map/ppermute | solution.py:617
  64.2 17.4 %collective-permute-start.1 = (bf16[256,512]{1,0:T(8,128)(2,1)S(1)}, bf16[256,512]{1,0:T(8,128)(2,1)S(1)}, u32[]{:S(2)}, u32[]{:S(2)}) collective-permute-start(bf16[256,512]{1,0:T(8,128)(2,1)S(1)} %get-tuple-element.35), channel_id=1, source_target_pairs={{0,8},{2,10},{4,28},{6,30},{8,16},{10,18},{12,4},{14,6},{16,24},{1... | collective-permute-start | bytes 786440 | tf_op jit(solution)/shard_map/ppermute | solution.py:617
  64.5 17.1 %collective-permute-start.2 = (bf16[256,512]{1,0:T(8,128)(2,1)S(1)}, bf16[256,512]{1,0:T(8,128)(2,1)S(1)}, u32[]{:S(2)}, u32[]{:S(2)}) collective-permute-start(bf16[256,512]{1,0:T(8,128)(2,1)S(1)} %get-tuple-element.35), channel_id=1, source_target_pairs={{0,4},{2,6},{4,0},{6,2},{8,12},{10,14},{12,8},{14,10},{16,20},{18,... | collective-permute-start | bytes 786440 | tf_op jit(solution)/shard_map/ppermute | solution.py:617
  68.0 3.2 %copy-start.5 = (bf16[512,512]{1,0:T(8,128)(2,1)S(1)}, bf16[512,512]{1,0:T(8,128)(2,1)}, u32[]{:S(2)}) copy-start(bf16[512,512]{1,0:T(8,128)(2,1)} %wk_ref.5) | copy-start | bytes 1572868
  74.7 7.1 %collective-permute-start.3 = (bf16[256,512]{1,0:T(8,128)(2,1)S(1)}, bf16[256,512]{1,0:T(8,128)(2,1)S(1)}, u32[]{:S(2)}, u32[]{:S(2)}) collective-permute-start(bf16[256,512]{1,0:T(8,128)(2,1)S(1)} %collective-permute-done), channel_id=1, source_target_pairs={{0,4},{2,6},{4,0},{6,2},{8,12},{10,14},{12,8},{14,10},{16,20},{18,... | collective-permute-start | bytes 786440 | tf_op jit(solution)/shard_map/ppermute | solution.py:617
  82.0 5.4 %collective-permute-start.4 = (bf16[4,256,512]{2,1,0:T(8,128)(2,1)S(1)}, bf16[4,256,512]{2,1,0:T(8,128)(2,1)S(1)}, u32[]{:S(2)}, u32[]{:S(2)}) collective-permute-start(bf16[4,256,512]{2,1,0:T(8,128)(2,1)S(1)} %pad_maximum_fusion), channel_id=1, source_target_pairs={{0,2},{2,0},{4,6},{6,4},{8,10},{10,8},{12,14},{14,12},{16,18},{18,... | collective-permute-start | bytes 3145736 | tf_op jit(solution)/shard_map/ppermute | solution.py:617
  83.8 3.7 %copy-start = (bf16[512,512]{0,1:T(8,128)(2,1)S(1)}, bf16[512,512]{0,1:T(8,128)(2,1)}, u32[]{:S(2)}) copy-start(bf16[512,512]{0,1:T(8,128)(2,1)} %copy.29) | copy-start | bytes 1572868
  83.9 3.7 %copy-start.2 = (bf16[512,1024]{1,0:T(8,128)(2,1)S(1)}, bf16[512,1024]{1,0:T(8,128)(2,1)}, u32[]{:S(2)}) copy-start(bf16[512,1024]{1,0:T(8,128)(2,1)} %wg_ref.1) | copy-start | bytes 3145732
  83.9 3.7 %copy-start.3 = (bf16[512,1024]{1,0:T(8,128)(2,1)S(1)}, bf16[512,1024]{1,0:T(8,128)(2,1)}, u32[]{:S(2)}) copy-start(bf16[512,1024]{1,0:T(8,128)(2,1)} %wu_ref.1) | copy-start | bytes 3145732
  83.9 3.7 %copy-start.4 = (bf16[1024,512]{1,0:T(8,128)(2,1)S(1)}, bf16[1024,512]{1,0:T(8,128)(2,1)}, u32[]{:S(2)}) copy-start(bf16[1024,512]{1,0:T(8,128)(2,1)} %wd_ref.1) | copy-start | bytes 3145732
  83.9 3.7 %copy-start.6 = (bf16[512,512]{1,0:T(8,128)(2,1)S(1)}, bf16[512,512]{1,0:T(8,128)(2,1)}, u32[]{:S(2)}) copy-start(bf16[512,512]{1,0:T(8,128)(2,1)} %wpk_ref.1) | copy-start | bytes 1572868
  83.9 3.7 %copy-start.7 = (bf16[512,512]{1,0:T(8,128)(2,1)S(1)}, bf16[512,512]{1,0:T(8,128)(2,1)}, u32[]{:S(2)}) copy-start(bf16[512,512]{1,0:T(8,128)(2,1)} %wo_ref.1) | copy-start | bytes 1572868
  83.9 3.7 %copy-start.8 = (f32[512]{0:T(512)S(1)}, f32[512]{0:T(512)}, u32[]{:S(2)}) copy-start(f32[512]{0:T(512)} %param.26) | copy-start | bytes 6148
  106.0 51.0 %copy-start.9 = (s32[16,128]{1,0:T(8,128)S(1)}, s32[16,128]{1,0:T(8,128)}, u32[]{:S(2)}) copy-start(s32[16,128]{1,0:T(8,128)} %get-tuple-element.32.places_ref) | copy-start | bytes 24580
